TPU v7x, 128 devices: a whole 4x4x4 slice. The times are simulated.
128 devices in a mesh: elem: 8 (over x, core), mode: 16 (over z, y).
Axes of the slice: x: 4, y: 4, z: 4, core: 2. Of those that a mesh axis runs over, the one named last changes fastest.
Arguments:
- velocity: float32 [3, 2, 256, 64, 1024], P(None, None, 'mode', None, 'elem'), may hold values from -0.625 to 0.625
- metric: float32 [4, 64, 1024], P(None, None, 'elem'), may hold values from -2 to 2
- mass: float32 [64, 1024], P(None, 'elem'), may hold values from 0.3 to 4.5
- sponge_rate: float32 [64, 1024], P(None, 'elem'), may hold values from 0.5 to 4
- sponge_mask: int32 [1024], P('elem'), may hold values 0 or 1
- neighbours: int32 [4, 1024], P(None, 'elem'), may hold values from -1 to 1023, as said below
Outputs:
- nonlinear: float32 [3, 2, 256, 64, 1024], P(None, None, 'mode', None, 'elem')
- pressure: float32 [2, 256, 64, 1024], P(None, 'mode', None, 'elem')
Inputs may be any that keep to these rules, and one draw needn't show every extreme that they name: Rows are the west, east, south and north neighbour of each element, -1 where there is none. The elements form one grid of 16 rows; relations are mutual; north and south neighbours lie on the same index of elem, east and west ones on the same or an adjacent index; the south neighbour of the west neighbour is the west neighbour of the south neighbour, and likewise at all four corners.
All inputs are finite; a program needn't handle non-finite values. No bound on the sum of `sponge_mask` on one device may be relied on, other than what follows from the above.
Results may differ from a plain program's by a relative error of at most 0.00013.
Values sent between devices are 32-bit elements; how exact they have to be, the bound alone decides.
No kernel may reach another device: no remote copies, remote signals or barrier semaphores. Data moves between devices by JAX's collectives and lax.ppermute only.
A program may use at most 192 MiB of HBM per device.

v0:
```python
import jax
import jax.numpy as jnp
import numpy as np
from jax import lax
from jax.sharding import PartitionSpec as P

ITERS = 2


def padded(cells, sides, width):
    for axis, dim in sides:
        count = lax.axis_size(axis)
        ends = count - 1
        head = lax.slice_in_dim(cells, 0, width, axis=dim)
        tail = lax.slice_in_dim(cells, cells.shape[dim] - width, cells.shape[dim], axis=dim)
        cells = jnp.concatenate(
            [
                lax.ppermute(tail, axis, [(i, (i + 1) % count) for i in range(ends)]),
                cells,
                lax.ppermute(head, axis, [((i + 1) % count, i) for i in range(ends)]),
            ],
            axis=dim,
        )
    return cells


def cheb_matrix():
    count = 8
    places = np.arange(count)
    points = np.cos(np.pi * places / (count - 1))
    weights = np.where((places == 0) | (places == count - 1), 2.0, 1.0)
    signs = weights * (-1.0) ** places
    differ = points[:, None] - points[None, :] + np.eye(count)
    table = np.outer(signs, 1.0 / signs) / differ
    table = table - np.eye(count) * np.sum(table, axis=1)[:, None]
    return jnp.asarray(table, dtype=jnp.float32)


def node_grads(field, table):
    shape = field.shape
    grid = field.reshape(shape[:-2] + (8, 8, shape[-1]))
    along_r = jnp.einsum("bc,...ace->...abe", table, grid, precision=lax.Precision.HIGHEST)
    along_s = jnp.einsum("ac,...cbe->...abe", table, grid, precision=lax.Precision.HIGHEST)
    return (along_r.reshape(shape), along_s.reshape(shape))


def node_grads_adjoint(first, second, table):
    shape = first.shape
    grid_r = first.reshape(shape[:-2] + (8, 8, shape[-1]))
    grid_s = second.reshape(shape[:-2] + (8, 8, shape[-1]))
    back_r = jnp.einsum("cb,...ace->...abe", table, grid_r, precision=lax.Precision.HIGHEST)
    back_s = jnp.einsum("ca,...cbe->...abe", table, grid_s, precision=lax.Precision.HIGHEST)
    return (back_r + back_s).reshape(shape)


def plane_grads(field, metric, table):
    along_r, along_s = node_grads(field, table)
    return (metric[0] * along_r + metric[2] * along_s, metric[1] * along_r + metric[3] * along_s)


def stiffness(field, metric, mass, shift, table):
    grad_x, grad_y = plane_grads(field, metric, table)
    flux_x = mass * grad_x
    flux_y = mass * grad_y
    folded = node_grads_adjoint(
        metric[0] * flux_x + metric[1] * flux_y, metric[2] * flux_x + metric[3] * flux_y, table
    )
    return folded + shift * mass * field


def span_grad(field, wave):
    return jnp.stack([-wave * field[..., 1, :, :, :], wave * field[..., 0, :, :, :]], axis=-4)


def vorticity(field, metric, wave, table):
    grad_x, grad_y = plane_grads(field, metric, table)
    return jnp.stack(
        [
            grad_y[2] - span_grad(field[1], wave),
            span_grad(field[0], wave) - grad_x[2],
            grad_x[1] - grad_y[0],
        ]
    )


def forcing(speed, swirl, damping):
    return jnp.stack(
        [
            speed[1] * swirl[2] - speed[2] * swirl[1] - damping * (speed[0] - 1.0),
            speed[2] * swirl[0] - speed[0] * swirl[2] - damping * speed[1],
            speed[0] * swirl[1] - speed[1] * swirl[0] - damping * speed[2],
        ]
    )


def spectral_tables(modes):
    planes = 2 * modes
    order = jnp.arange(modes, dtype=jnp.int32)
    spots = jnp.arange(planes, dtype=jnp.int32)
    phase = spots[:, None] * order[None, :] % planes
    angle = phase.astype(jnp.float32) * (2.0 * jnp.pi / planes)
    cosine = jnp.cos(angle)
    sine = jnp.sin(angle)
    weight = jnp.where(order == 0, 1.0, 2.0).astype(jnp.float32)
    wave = order.astype(jnp.float32) * (jnp.pi / modes)
    synth = jnp.concatenate([weight * cosine, -weight * sine], axis=1)
    slope = jnp.concatenate([-weight * wave * sine, -weight * wave * cosine], axis=1)
    analyse = jnp.concatenate([cosine.T, -sine.T], axis=0) / planes
    return (synth, slope, analyse)


def pick_from(values, index, present):
    return jnp.take(values, index, axis=3) * present


def shared_sum(field, links):
    (
        west_index,
        west_here,
        east_index,
        east_here,
        south_index,
        south_here,
        north_index,
        north_here,
    ) = links
    width = field.shape[3]
    grid = field.reshape(field.shape[:2] + (8, 8, width))
    extended = padded(field, (("elem", 3),), width)
    outer = extended.reshape(field.shape[:2] + (8, 8, 3 * width))
    from_west = pick_from(outer[:, :, :, 7, :], west_index, west_here)
    from_east = pick_from(outer[:, :, :, 0, :], east_index, east_here)
    first = grid[:, :, :, 0, :] + from_west
    last = grid[:, :, :, 7, :] + from_east
    grid = jnp.concatenate(
        [first[:, :, :, None, :], grid[:, :, :, 1:7, :], last[:, :, :, None, :]], axis=3
    )
    bottom = grid[:, :, 0, :, :] + pick_from(grid[:, :, 7, :, :], south_index, south_here)
    top = grid[:, :, 7, :, :] + pick_from(grid[:, :, 0, :, :], north_index, north_here)
    grid = jnp.concatenate(
        [bottom[:, :, None, :, :], grid[:, :, 1:7, :, :], top[:, :, None, :, :]], axis=2
    )
    return grid.reshape(field.shape)


def per_device(velocity, metric, mass, sponge_rate, sponge_mask, neighbours):
    table = cheb_matrix()
    local_modes = velocity.shape[2]
    width = velocity.shape[4]
    node_count = velocity.shape[3]
    mode_size = lax.axis_size("mode")
    mode_count = local_modes * mode_size
    plane_count = 2 * mode_count
    span_block = node_count * width // mode_size
    wave = (
        (lax.axis_index("mode") * local_modes + jnp.arange(local_modes)).astype(jnp.float32)
        * (jnp.pi / mode_count)
    )[:, None, None]
    synth, slope, analyse = spectral_tables(mode_count)
    damping_all = sponge_mask.astype(jnp.float32)[None, :] * sponge_rate
    swirl_modes = vorticity(velocity, metric, wave, table)
    packed = jnp.concatenate([velocity, swirl_modes], axis=0).reshape(
        6, 2, local_modes, node_count * width
    )
    gathered = lax.all_to_all(packed, "mode", split_axis=3, concat_axis=2, tiled=True)
    flat = gathered.reshape(6, plane_count, span_block)
    both = jnp.einsum("jc,fcp->fjp", synth, flat, precision=lax.Precision.HIGHEST)
    speed = both[:3]
    swirl = both[3:]
    damping = lax.dynamic_slice_in_dim(
        damping_all.reshape(node_count * width),
        lax.axis_index("mode") * span_block,
        span_block,
        axis=0,
    )
    force = forcing(speed, swirl, damping)
    coeff = jnp.einsum("cj,fjp->fcp", analyse, force, precision=lax.Precision.HIGHEST)
    outgoing = coeff.reshape(3, 2, mode_count, span_block)
    returned = lax.all_to_all(outgoing, "mode", split_axis=2, concat_axis=3, tiled=True)
    nonlinear = returned.reshape(3, 2, local_modes, node_count, width)
    device = lax.axis_index("elem")
    west_global = neighbours[0]
    east_global = neighbours[1]
    south_global = neighbours[2]
    north_global = neighbours[3]
    west_here = (west_global >= 0).astype(jnp.float32)
    east_here = (east_global >= 0).astype(jnp.float32)
    south_here = (south_global >= 0).astype(jnp.float32)
    north_here = (north_global >= 0).astype(jnp.float32)
    outer_base = (device - 1) * width
    inner_base = device * width
    links = (
        jnp.where(west_global >= 0, west_global - outer_base, 0),
        west_here,
        jnp.where(east_global >= 0, east_global - outer_base, 0),
        east_here,
        jnp.where(south_global >= 0, south_global - inner_base, 0),
        south_here,
        jnp.where(north_global >= 0, north_global - inner_base, 0),
        north_here,
    )
    corner_index = jnp.arange(8)
    column_factor = (
        1.0
        + west_here[None, :] * (corner_index == 0)[:, None]
        + east_here[None, :] * (corner_index == 7)[:, None]
    )
    row_factor = (
        1.0
        + south_here[None, :] * (corner_index == 0)[:, None]
        + north_here[None, :] * (corner_index == 7)[:, None]
    )
    multiplicity = (row_factor[:, None, :] * column_factor[None, :, :]).reshape(node_count, width)

    def inner(first, second):
        return lax.psum(jnp.sum(first * second / multiplicity, axis=(0, 2, 3)), "elem")[
            :, None, None
        ]

    shift = wave * wave + 1.0
    grad_x0 = plane_grads(nonlinear[0], metric, table)[0]
    grad_y1 = plane_grads(nonlinear[1], metric, table)[1]
    divergence = grad_x0 + grad_y1 + span_grad(nonlinear[2], wave)
    right = shared_sum(-mass * divergence, links)
    solution = jnp.zeros_like(right)
    residual = right
    direction = right
    norm_now = inner(residual, residual)
    for sweep in range(ITERS):
        image = shared_sum(stiffness(direction, metric, mass, shift, table), links)
        alpha = norm_now / inner(direction, image)
        solution = solution + alpha * direction
        residual = residual - alpha * image
        norm_next = inner(residual, residual)
        direction = residual + norm_next / norm_now * direction
        norm_now = norm_next
    return (nonlinear, solution)


def solution(mesh):
    return jax.shard_map(
        per_device,
        mesh=mesh,
        in_specs=(
            P(None, None, "mode", None, "elem"),
            P(None, None, "elem"),
            P(None, "elem"),
            P(None, "elem"),
            P("elem"),
            P(None, "elem"),
        ),
        out_specs=(P(None, None, "mode", None, "elem"), P(None, "mode", None, "elem")),
        check_vma=False,
    )
```

profile of v0, /device:TPU:0, one launch (start us, length us, event | category | flops | bytes accessed | tf_op | source)
XLA Modules:
  0.0 763.3 jit_solution(5949175719569052121)
XLA Ops:
  2.0 4.8 concatenate.48
  6.8 2.9 fusion.10
  9.9 3.5 fusion.7
  13.5 1.8 slice_subtract_fusion.2
  15.3 2.5 concatenate.49
  17.8 2.4 concatenate.50
  20.2 2.4 concatenate.51
  22.6 4.2 pad_maximum_fusion
  26.8 54.6 %copy.264 = f32[6,2,16,8192]{2,1,0,3:T(2,128)} copy(f32[6,2,16,8192]{3,2,1,0:T(8,128)} %pad_maximum_fusion) | data formatting | bytes 12582912 | tf_op jit(solution)/shard_map/concatenate | solution.py:162
  81.4 69.9 %reshape.660 = f32[16,1,98304]{2,1,0:T(1,128)} reshape(f32[8192,6,2,16]{3,2,1,0:T(2,128)} %bitcast.418) | data formatting | bytes 12582912
  151.3 8.3 %all-to-all-start = ((f32[16,1,98304]{2,1,0:T(1,128)}), f32[16,1,98304]{2,1,0:T(1,128)}, u32[]{:S(2)}, u32[]{:S(2)}) async-start(f32[16,1,98304]{2,1,0:T(1,128)} %reshape.660), calls=%async_computation | async-start | bytes 12582912 | tf_op jit(solution)/shard_map/all_to_all | solution.py:165
  159.7 2.1 sine_negate_fusion
  161.8 2.1 sine_multiply_fusion
  163.9 88.9 %all-to-all-done = f32[16,1,98304]{2,1,0:T(1,128)} async-done(((f32[16,1,98304]{2,1,0:T(1,128)}), f32[16,1,98304]{2,1,0:T(1,128)}, u32[]{:S(2)}, u32[]{:S(2)}) %all-to-all-start) | async-done | bytes 6291488 | tf_op jit(solution)/shard_map/all_to_all | solution.py:165
  253.3 19.4 %reduce.4 = f32[16,98304]{1,0:T(8,128)} reduce(f32[16,1,98304]{2,1,0:T(1,128)} %all-to-all-done, f32[]{:T(128)} %broadcast.524), dimensions={1}, to_apply=%all_to_all.22.reduce_sub_computation | reduce | bytes 12582916 | tf_op jit(solution)/shard_map/all_to_all | solution.py:165
  272.7 96.7 %reshape.661 = f32[8192,6,2,16]{3,2,1,0:T(2,128)} reshape(f32[16,98304]{1,0:T(8,128)} %reduce.4) | data formatting | bytes 12582912
  369.3 62.4 %copy.344 = f32[6,2,16,16,512]{4,2,3,1,0:T(8,128)} copy(f32[6,2,16,16,512]{2,1,0,4,3:T(2,128)} %bitcast.419) | data formatting | bytes 12582912 | tf_op jit(solution)/shard_map/all_to_all | solution.py:165
  431.8 22.9 %convolution_bitcast_fusion = f32[6,512,512]{1,2,0:T(8,128)S(1)} fusion(f32[6,512,512]{2,1,0:T(8,128)} %bitcast.424, f32[512,256]{1,0:T(8,128)S(1)} %get-tuple-element.83, f32[512,256]{1,0:T(8,128)S(1)} %get-tuple-element.84), kind=kOutput, calls=%fused_computation.31 | convolution fusion | flops 9663938560 | bytes 13631488 | tf_op jit(solution)/shard_map/jc,fcp->fjp/dot_general | solution.py:167
  455.3 5.4 fusion
  460.7 4.1 copy.269
  464.8 6.0 all-to-all-start.1
  472.1 42.8 %all-to-all-done.1 = f32[3,2,256,512]{3,1,0,2:T(2,128)S(1)} async-done(((f32[3,2,256,512]{3,1,0,2:T(2,128)}), f32[3,2,256,512]{3,1,0,2:T(2,128)S(1)}, u32[]{:S(2)}, u32[]{:S(2)}) %all-to-all-start.1) | async-done | bytes 3145760 | tf_op jit(solution)/shard_map/all_to_all | solution.py:179
  516.5 3.7 copy.455
  520.2 1.8 fusion.131
  522.0 2.3 reshape_squeeze.6
  524.3 3.2 fusion.135
  527.5 3.3 fusion.56
  531.9 2.0 squeeze.45
  535.0 1.9 squeeze.44
  546.5 3.2 collective-permute-done.1
  550.5 2.3 copy.352
  552.7 3.7 gather_fusion
  558.0 2.6 copy.354
  560.7 2.7 gather_fusion.1
  565.8 3.0 gather_fusion.2
  572.4 1.8 gather_fusion.3
  577.8 2.9 multiply_add_fusion.4
  585.3 14.0 %collective-permute-start.2 = (f32[2,16,64,128]{3,2,1,0:T(8,128)S(1)}, f32[2,16,64,128]{3,2,1,0:T(8,128)S(1)}, u32[]{:S(2)}, u32[]{:S(2)}) collective-permute-start(f32[2,16,64,128]{3,2,1,0:T(8,128)S(1)} %fusion.38), channel_id=1, source_target_pairs={{0,16},{16,32},{32,48},{48,64},{64,80},{80,96},{96,112},{1,17},{17... | collective-permute-start | bytes 3145736 | tf_op jit(solution)/shard_map/ppermute | solution.py:18
  601.5 2.3 collective-permute-done.3
  605.5 3.2 copy.356
  608.7 3.7 gather_fusion.4
  614.1 3.1 copy.357
  617.3 3.7 gather_fusion.5
  626.3 2.0 gather_fusion.6
  632.4 1.8 gather_fusion.7
  636.7 2.7 fusion.67
  639.3 24.0 %all-reduce = (f32[16]{0:T(128)S(1)}, f32[16]{0:T(128)S(1)}) all-reduce(f32[16]{0:T(128)} %get-tuple-element.5, f32[16]{0:T(128)} %get-tuple-element.4), channel_id=1, replica_groups=mesh['elem'=8,'mode'=16] {'elem'}, use_global_device_ids=true, to_apply=%region_1.4 | all-reduce | flops 32 | bytes 256 | tf_op jit(solution)/shard_map/psum | solution.py:216
  664.0 1.9 fusion.68
  665.8 13.1 %psum.30 = f32[16]{0:T(128)} all-reduce(f32[16]{0:T(128)} %fusion.68), channel_id=1, replica_groups=mesh['elem'=8,'mode'=16] {'elem'}, use_global_device_ids=true, to_apply=%region_5.8 | all-reduce | flops 16 | bytes 128 | tf_op jit(solution)/shard_map/psum | solution.py:216
  681.8 2.1 multiply_add_fusion.1
  685.4 2.4 multiply_add_fusion
  687.9 3.1 bitcast_add_fusion
  691.0 2.8 collective-permute-start.4
  695.0 4.6 reshape.504
  701.8 2.4 maximum_bitcast_fusion.2
  705.4 3.1 copy.361
  708.5 3.7 gather_fusion.8
  714.6 2.3 copy.362
  716.9 3.7 gather_fusion.9
  724.7 3.0 gather_fusion.10
  727.7 2.3 copy.330
  732.9 3.0 gather_fusion.11
  739.8 19.5 %psum.31 = f32[16]{0:T(128)S(1)} all-reduce(f32[16]{0:T(128)S(1)} %fusion.70), channel_id=1, replica_groups=mesh['elem'=8,'mode'=16] {'elem'}, use_global_device_ids=true, to_apply=%region_7.10 | all-reduce | flops 16 | bytes 128 | tf_op jit(solution)/shard_map/psum | solution.py:216
  760.0 3.0 fusion.39
  (224 shorter events, 74.5 us)
Async XLA Ops:
  2.0 537.6 %copy-start.24 = (f32[8,8,128]{2,1,0:T(8,128)}, f32[8,8,128]{2,1,0:T(8,128)S(1)}, u32[]{:S(2)}) copy-start(f32[8,8,128]{2,1,0:T(8,128)S(1)} %get-tuple-element.49) | copy-start | bytes 98308
  2.0 537.6 %copy-start.27 = (f32[8,8,128]{2,1,0:T(8,128)}, f32[8,8,128]{2,1,0:T(8,128)S(1)}, u32[]{:S(2)}) copy-start(f32[8,8,128]{2,1,0:T(8,128)S(1)} %get-tuple-element.50) | copy-start | bytes 98308
  2.0 537.6 %copy-start.30 = (f32[8,8,128]{2,1,0:T(8,128)}, f32[8,8,128]{2,1,0:T(8,128)S(1)}, u32[]{:S(2)}) copy-start(f32[8,8,128]{2,1,0:T(8,128)S(1)} %get-tuple-element.51) | copy-start | bytes 98308
  2.0 537.6 %copy-start.33 = (f32[8,8,128]{2,1,0:T(8,128)}, f32[8,8,128]{2,1,0:T(8,128)S(1)}, u32[]{:S(2)}) copy-start(f32[8,8,128]{2,1,0:T(8,128)S(1)} %get-tuple-element.52) | copy-start | bytes 98308
  2.0 4.8 copy-start
  2.0 4.8 copy-start.39
  15.3 7.3 copy-start.5
  151.3 8.3 %copy-start.59 = (s32[128]{0:T(128)S(1)}, s32[128]{0:T(128)}, u32[]{:S(2)}) copy-start(s32[128]{0:T(128)} %param.15) | copy-start | bytes 1540
  151.3 8.3 %copy-start.37 = (f32[64,128]{1,0:T(8,128)S(1)}, f32[64,128]{1,0:T(8,128)}, u32[]{:S(2)}) copy-start(f32[64,128]{1,0:T(8,128)} %param.14) | copy-start | bytes 98308
  151.3 101.5 %all-to-all-start = ((f32[16,1,98304]{2,1,0:T(1,128)}), f32[16,1,98304]{2,1,0:T(1,128)}, u32[]{:S(2)}, u32[]{:S(2)}) async-start(f32[16,1,98304]{2,1,0:T(1,128)} %reshape.660), calls=%async_computation | async-start | bytes 12582912 | tf_op jit(solution)/shard_map/all_to_all | solution.py:165
  464.8 6.0 copy-start.21
  464.8 6.0 copy-start.54
  464.8 50.0 %all-to-all-start.1 = ((f32[3,2,256,512]{3,1,0,2:T(2,128)}), f32[3,2,256,512]{3,1,0,2:T(2,128)S(1)}, u32[]{:S(2)}, u32[]{:S(2)}) async-start(f32[3,2,256,512]{3,1,0,2:T(2,128)} %copy.269), calls=%async_computation.1 | async-start | bytes 6291456 | tf_op jit(solution)/shard_map/all_to_all | solution.py:179
  520.2 10.6 %copy-start.1 = (f32[3,2,16,16,512]{4,2,3,1,0:T(8,128)}, f32[3,2,16,16,512]{4,2,3,1,0:T(8,128)S(1)}, u32[]{:S(2)}) copy-start(f32[3,2,16,16,512]{4,2,3,1,0:T(8,128)S(1)} %copy.455) | copy-start | bytes 9437188
  520.2 4.1 copy-start.36
  531.9 5.0 copy-start.14
  531.9 5.0 copy-start.16
  537.0 2.6 copy-start.6
  537.0 2.6 copy-start.7
  541.3 3.6 copy-start.58
  541.3 4.2 copy-start.55
  541.3 4.2 copy-start.57
  542.2 4.3 collective-permute-start
  543.6 6.2 collective-permute-start.1
  545.5 18.3 %copy-start.40 = (f32[128]{0:T(128)}, f32[128]{0:T(128)S(1)}, u32[]{:S(2)}) copy-start(f32[128]{0:T(128)S(1)} %get-tuple-element.61) | copy-start | bytes 1540
  545.5 18.4 %copy-start.43 = (f32[128]{0:T(128)}, f32[128]{0:T(128)S(1)}, u32[]{:S(2)}) copy-start(f32[128]{0:T(128)S(1)} %get-tuple-element.60) | copy-start | bytes 1540
  545.6 38.1 %copy-start.10 = (f32[16,64,128]{2,1,0:T(8,128)}, f32[16,64,128]{2,1,0:T(8,128)S(1)}, u32[]{:S(2)}) copy-start(f32[16,64,128]{2,1,0:T(8,128)S(1)} %broadcast_multiply_fusion) | copy-start | bytes 1572868
  545.8 36.4 %copy-start.12 = (f32[16,8,8,128]{3,1,0,2:T(8,128)}, f32[16,8,8,128]{3,1,0,2:T(8,128)S(1)}, u32[]{:S(2)}) copy-start(f32[16,8,8,128]{3,1,0,2:T(8,128)S(1)} %broadcast_multiply_fusion.1) | copy-start | bytes 1572868
  556.4 7.4 copy-start.51
  556.4 7.5 copy-start.52
  564.0 6.4 copy-start.46
  576.7 3.9 copy-start.22
  576.7 3.9 copy-start.25
  576.8 3.9 copy-start.28
  576.8 3.9 copy-start.31
  576.8 3.9 copy-start.34
  577.8 4.4 copy-start.38
  583.7 17.8 %copy-start.15 = (f32[2,16,8,8,128]{4,2,1,0,3:T(8,128)}, f32[2,16,8,8,128]{4,2,1,0,3:T(8,128)S(1)}, u32[]{:S(2)}) copy-start(f32[2,16,8,8,128]{4,2,1,0,3:T(8,128)S(1)} %get-tuple-element.75) | copy-start | bytes 3145732
  583.7 16.9 %copy-start.41 = (f32[128]{0:T(128)S(1)}, f32[128]{0:T(128)}, u32[]{:S(2)}) copy-start(f32[128]{0:T(128)} %copy-done.40) | copy-start | bytes 1540
  583.7 16.9 %copy-start.44 = (f32[128]{0:T(128)S(1)}, f32[128]{0:T(128)}, u32[]{:S(2)}) copy-start(f32[128]{0:T(128)} %copy-done.43) | copy-start | bytes 1540
  585.3 16.2 %collective-permute-start.2 = (f32[2,16,64,128]{3,2,1,0:T(8,128)S(1)}, f32[2,16,64,128]{3,2,1,0:T(8,128)S(1)}, u32[]{:S(2)}, u32[]{:S(2)}) collective-permute-start(f32[2,16,64,128]{3,2,1,0:T(8,128)S(1)} %fusion.38), channel_id=1, source_target_pairs={{0,16},{16,32},{32,48},{48,64},{64,80},{80,96},{96,112},{1,17},{17... | collective-permute-start | bytes 3145736 | tf_op jit(solution)/shard_map/ppermute | solution.py:18
  599.3 4.6 collective-permute-start.3
  601.4 22.1 %copy-start.9 = (f32[2,16,8,6,128]{4,2,1,0,3:T(8,128)}, f32[2,16,8,6,128]{4,2,1,0,3:T(8,128)S(1)}, u32[]{:S(2)}) copy-start(f32[2,16,8,6,128]{4,2,1,0,3:T(8,128)S(1)} %slice.306) | copy-start | bytes 2359300
  604.1 9.9 %copy-start.53 = (pred[128]{0:T(512)(128)(4,1)S(1)}, pred[128]{0:T(512)(128)(4,1)}, u32[]{:S(2)}) copy-start(pred[128]{0:T(512)(128)(4,1)} %get-tuple-element.65) | copy-start | bytes 388
  614.1 10.2 %copy-start.19 = (f32[2,16,8,1,128]{4,2,1,0,3:T(8,128)}, f32[2,16,8,1,128]{4,2,1,0,3:T(8,128)S(1)}, u32[]{:S(2)}) copy-start(f32[2,16,8,1,128]{4,2,1,0,3:T(8,128)S(1)} %copy.303) | copy-start | bytes 393220
  665.8 16.0 %copy-start.23 = (f32[64,128]{1,0:T(8,128)S(1)}, f32[64,128]{1,0:T(8,128)}, u32[]{:S(2)}) copy-start(f32[64,128]{1,0:T(8,128)} %param.13) | copy-start | bytes 98308
  665.8 16.0 %copy-start.26 = (f32[8,8,128]{2,1,0:T(8,128)S(1)}, f32[8,8,128]{2,1,0:T(8,128)}, u32[]{:S(2)}) copy-start(f32[8,8,128]{2,1,0:T(8,128)} %copy-done.24) | copy-start | bytes 98308
  665.8 16.0 %copy-start.29 = (f32[8,8,128]{2,1,0:T(8,128)S(1)}, f32[8,8,128]{2,1,0:T(8,128)}, u32[]{:S(2)}) copy-start(f32[8,8,128]{2,1,0:T(8,128)} %copy-done.27) | copy-start | bytes 98308
  665.8 16.0 %copy-start.32 = (f32[8,8,128]{2,1,0:T(8,128)S(1)}, f32[8,8,128]{2,1,0:T(8,128)}, u32[]{:S(2)}) copy-start(f32[8,8,128]{2,1,0:T(8,128)} %copy-done.30) | copy-start | bytes 98308
  679.0 2.9 copy-start.35
  679.6 8.2 %copy-start.56 = (f32[16]{0:T(128)}, f32[16]{0:T(128)S(1)}, u32[]{:S(2)}) copy-start(f32[16]{0:T(128)S(1)} %div.55) | copy-start | bytes 196
  680.8 4.6 copy-start.2
  681.8 3.6 copy-start.13
  685.4 2.5 copy-start.11
  685.4 2.5 copy-start.49
  691.0 10.8 %collective-permute-start.4 = (f32[2,16,64,128]{3,2,1,0:T(8,128)}, f32[2,16,64,128]{3,2,1,0:T(8,128)}, u32[]{:S(2)}, u32[]{:S(2)}) collective-permute-start(f32[2,16,64,128]{3,2,1,0:T(8,128)} %bitcast_add_fusion), channel_id=1, source_target_pairs={{0,16},{16,32},{32,48},{48,64},{64,80},{80,96},{96,112},{1,17},{17... | collective-permute-start | bytes 3145736 | tf_op jit(solution)/shard_map/ppermute | solution.py:18
  693.7 8.0 %collective-permute-start.5 = (f32[2,16,64,128]{3,2,1,0:T(8,128)}, f32[2,16,64,128]{3,2,1,0:T(8,128)}, u32[]{:S(2)}, u32[]{:S(2)}) collective-permute-start(f32[2,16,64,128]{3,2,1,0:T(8,128)} %bitcast_add_fusion), channel_id=1, source_target_pairs={{16,0},{32,16},{48,32},{64,48},{80,64},{96,80},{112,96},{17,1},{33... | collective-permute-start | bytes 3145736 | tf_op jit(solution)/shard_map/ppermute | solution.py:20
  701.7 21.4 %copy-start.8 = (f32[2,16,8,6,128]{4,2,1,0,3:T(8,128)}, f32[2,16,8,6,128]{4,2,1,0,3:T(8,128)S(1)}, u32[]{:S(2)}) copy-start(f32[2,16,8,6,128]{4,2,1,0,3:T(8,128)S(1)} %slice.311) | copy-start | bytes 2359300
  704.2 9.6 %copy-start.45 = (f32[128]{0:T(128)S(1)}, f32[128]{0:T(128)}, u32[]{:S(2)}) copy-start(f32[128]{0:T(128)} %copy-done.43) | copy-start | bytes 1540
  712.2 10.0 %copy-start.42 = (f32[128]{0:T(128)S(1)}, f32[128]{0:T(128)}, u32[]{:S(2)}) copy-start(f32[128]{0:T(128)} %copy-done.40) | copy-start | bytes 1540
  714.6 8.6 %copy-start.20 = (f32[2,16,8,1,128]{4,2,1,0,3:T(8,128)}, f32[2,16,8,1,128]{4,2,1,0,3:T(8,128)S(1)}, u32[]{:S(2)}) copy-start(f32[2,16,8,1,128]{4,2,1,0,3:T(8,128)S(1)} %copy.326) | copy-start | bytes 393220
  720.6 10.7 %copy-start.47 = (pred[128]{0:T(512)(128)(4,1)S(1)}, pred[128]{0:T(512)(128)(4,1)}, u32[]{:S(2)}) copy-start(pred[128]{0:T(512)(128)(4,1)} %get-tuple-element.67) | copy-start | bytes 388
  723.4 14.7 %copy-start.3 = (f32[2,16,8,8,128]{4,2,1,0,3:T(8,128)S(1)}, f32[2,16,8,8,128]{4,2,1,0,3:T(8,128)}, u32[]{:S(2)}) copy-start(f32[2,16,8,8,128]{4,2,1,0,3:T(8,128)} %copy-done.2) | copy-start | bytes 3145732
  730.0 30.1 %copy-start.50 = (f32[16]{0:T(128)S(1)}, f32[16]{0:T(128)}, u32[]{:S(2)}) copy-start(f32[16]{0:T(128)} %copy-done.48) | copy-start | bytes 196
  (5 other events, 5.7 us)
where the time goes:
time: 777 us; the launch traced here: 763 us
  local copies, waits for them, and re-layouts  408 us (53%)
  waiting for transfers between devices  137 us (18%)
  other arithmetic  65.5 us (8%)
  matrix products  57.7 us (7%)
  blocking collectives  56.7 us (7%)
  starting transfers between devices  36.3 us (5%)
    unnamed x131, local copies, waits for them, and re-layouts  187 us
    all_to_all x1, waiting for transfers between devices, per_device(): lax.all_to_all(packed, 'mode', split_axis=3, concat_axis=2, tiled=True)  88.9 us
    concatenate x5, local copies, waits for them, and re-layouts, per_device(): jnp.concatenate([velocity, swirl_modes], axis=0)  66.6 us
    all_to_all x2, local copies, waits for them, and re-layouts, per_device(): lax.all_to_all(packed, 'mode', split_axis=3, concat_axis=2, tiled=True)  63 us
    psum x3, blocking collectives, inner(): lax.psum(jnp.sum(first * second / multiplicity, axis=(0, 2, 3)), 'elem')  56.7 us
    gather x24, local copies, waits for them, and re-layouts, pick_from(): return jnp.take(values, index, axis=3) * present  53.9 us
    all_to_all x1, waiting for transfers between devices, per_device(): lax.all_to_all(outgoing, 'mode', split_axis=2, concat_axis=3, tiled=True)  42.8 us
    dot_general x1, matrix products, per_device(): jnp.einsum('jc,fcp->fjp', synth, flat, precision=lax.Precision.HIGHEST)  22.9 us
  transfers between devices with their start and end apart: 8, of which 5 were waited for; matrix products, arithmetic and copies ran while one was open for 2% of the time, Pallas kernels for 0%

commit v1 on v0

v1 whole, which is shorter than its diff:
```python
import jax
import jax.numpy as jnp
import ml_dtypes
import numpy as np
from jax import lax
from jax.experimental import pallas as pl
from jax.experimental.pallas import tpu as pltpu
from jax.sharding import PartitionSpec as P

F32 = jnp.float32
BF16 = jnp.bfloat16
LIMIT = 50 * 1024 * 1024


def cheb_matrix():
    count = 8
    places = np.arange(count)
    points = np.cos(np.pi * places / (count - 1))
    weights = np.where((places == 0) | (places == count - 1), 2.0, 1.0)
    signs = weights * (-1.0) ** places
    differ = points[:, None] - points[None, :] + np.eye(count)
    table = np.outer(signs, 1.0 / signs) / differ
    table = table - np.eye(count) * np.sum(table, axis=1)[:, None]
    return table.astype(np.float32).astype(np.float64)


def two_parts(table):
    high = table.astype(np.float32).astype(ml_dtypes.bfloat16)
    low = (table - high.astype(np.float64)).astype(np.float32).astype(ml_dtypes.bfloat16)
    return high, low


def tables(modes):
    planes = 2 * modes
    order = np.arange(modes)
    spots = np.arange(modes)
    phase = (spots[:, None] * order[None, :]) % planes
    angle = phase * (2.0 * np.pi / planes)
    weight = np.where(order == 0, 1.0, 2.0)
    cosine = np.cos(angle)
    sine = np.sin(angle)
    last = np.zeros((16, modes))
    last[0] = weight * (-1.0) ** order
    synth_cos = np.concatenate([weight * cosine, last], axis=0)
    synth_sin = weight * sine
    back_cos = cosine.T / planes
    back_sin = -sine.T / planes
    wave = np.broadcast_to((order * np.pi / modes)[:, None], (modes, 128)).astype(np.float32)
    sign = np.broadcast_to(((-1.0) ** order / planes)[:, None], (modes, 128)).astype(np.float32)
    return synth_cos, synth_sin, back_cos, back_sin, wave, sign


def right_tables():
    table = cheb_matrix()
    two = np.eye(2)
    eight = np.eye(8)
    along_r = np.kron(two, np.kron(eight, table.T))
    along_s = np.kron(two, np.kron(table.T, eight))
    both = np.concatenate([along_r, along_s], axis=1)
    high, low = two_parts(both)
    return np.concatenate([high, high], axis=0), low


def left_tables():
    table = cheb_matrix()
    eight = np.eye(8)
    along_r = np.kron(eight, table)
    along_s = np.kron(table, eight)
    high, low = two_parts(np.concatenate([along_r, along_s], axis=0))
    forward = np.concatenate([high, high, low], axis=1)
    high, low = two_parts(np.concatenate([along_r.T, along_s.T], axis=1))
    return forward, np.concatenate([high, high], axis=1), low


def split(value):
    high = value.astype(BF16)
    low = (value - high.astype(F32)).astype(BF16)
    return high, low


def dot(first, second):
    return jnp.dot(first, second, preferred_element_type=F32)


def low_half(shape):
    return lax.broadcasted_iota(jnp.int32, shape, len(shape) - 1) < 64


def swap(value):
    return pltpu.roll(value, 64, 1)


def pre_kernel(v_ref, y_ref, tmp):
    for kl in range(16):
        block = v_ref[0, :, kl].reshape(128, 128)
        tmp[pl.ds(kl, 128, stride=16), :] = block.T
    half = low_half((16, 128))
    for pair in range(64):
        first = tmp[32 * pair : 32 * pair + 16, :]
        second = tmp[32 * pair + 16 : 32 * pair + 32, :]
        g, i = divmod(pair, 4)
        cols = slice(128 * i, 128 * i + 128)
        y_ref[g, 0, 0, :, cols] = jnp.where(half, first, swap(second))
        y_ref[g, 0, 1, :, cols] = jnp.where(half, swap(first), second)


def to_blocks(velocity):
    return pl.pallas_call(
        pre_kernel,
        grid=(3,),
        in_specs=[pl.BlockSpec((1, 2, 16, 64, 128), lambda c: (c, 0, 0, 0, 0))],
        out_specs=pl.BlockSpec((16, 1, 2, 16, 512), lambda c: (0, c, 0, 0, 0)),
        out_shape=jax.ShapeDtypeStruct((16, 3, 2, 16, 512), F32),
        scratch_shapes=[pltpu.VMEM((2048, 128), F32)],
        compiler_params=pltpu.CompilerParams(vmem_limit_bytes=LIMIT),
        name="to_blocks",
    )(velocity)


ROWS = 32


def plane_kernel(
    z_ref, rows_ref, wave_ref, sign_ref, wst_ref, wlo_ref, ch_ref, cl_ref, sh_ref, sl_ref,
    bch_ref, bcl_ref, bsh_ref, bsl_ref, out_ref, high, low, planes, eh, el, tail,
):
    rx = rows_ref[0:1, :]
    ry = rows_ref[1:2, :]
    sx = rows_ref[2:3, :]
    sy = rows_ref[3:4, :]
    damping = rows_ref[4:5, :]
    count = ROWS // 16

    def curls(step, carry):
        rows = pl.ds(pl.multiple_of(step * ROWS, ROWS), ROWS)
        wave = jnp.concatenate([wave_ref[rows, :]] * 2, axis=1)
        fields = {}
        slopes = {}
        for c in range(3):
            for part in range(2):
                value = z_ref[pl.ds(step * count, count), c, part].reshape(ROWS, 256)
                up, down = split(value)
                high[c, part, rows, :] = up
                low[c, part, rows, :] = down
                fields[c, part] = value
                pieces = []
                for q in range(2):
                    cols = slice(128 * q, 128 * q + 128)
                    both = jnp.concatenate([up[:, cols], down[:, cols]], axis=1)
                    pieces.append(dot(both, wst_ref[...]) + dot(up[:, cols], wlo_ref[...]))
                slopes[c, part] = (
                    jnp.concatenate([pieces[0][:, :128], pieces[1][:, :128]], axis=1),
                    jnp.concatenate([pieces[0][:, 128:], pieces[1][:, 128:]], axis=1),
                )
        for part in range(2):
            u_r, u_s = slopes[0, part]
            v_r, v_s = slopes[1, part]
            w_r, w_s = slopes[2, part]
            if part == 0:
                dz_u = -wave * fields[0, 1]
                dz_v = -wave * fields[1, 1]
            else:
                dz_u = wave * fields[0, 0]
                dz_v = wave * fields[1, 0]
            swirl = (
                ry * w_r + sy * w_s - dz_v,
                dz_u - (rx * w_r + sx * w_s),
                rx * v_r + sx * v_s - (ry * u_r + sy * u_s),
            )
            for c in range(3):
                up, down = split(swirl[c])
                high[3 + c, part, rows, :] = up
                low[3 + c, part, rows, :] = down
        return carry

    lax.fori_loop(0, 256 // ROWS, curls, 0)

    def synth(c, carry):
        re_h = high[c, 0]
        re_l = low[c, 0]
        im_h = high[c, 1]
        im_l = low[c, 1]
        even = dot(ch_ref[...], re_h) + dot(ch_ref[...], re_l) + dot(cl_ref[...], re_h)
        odd = dot(sh_ref[...], im_h) + dot(sh_ref[...], im_l) + dot(sl_ref[...], im_h)
        planes[c, 0] = even[:256] - odd
        planes[c, 1] = even[:256] + odd
        planes[c, 1, 0:1, :] = even[256:257, :]
        return carry

    lax.fori_loop(0, 6, synth, 0)

    def force(u, w):
        return (
            u[1] * w[2] - u[2] * w[1] - damping * (u[0] - 1.0),
            u[2] * w[0] - u[0] * w[2] - damping * u[1],
            u[0] * w[1] - u[1] * w[0] - damping * u[2],
        )

    def forces(step, carry):
        rows = pl.ds(pl.multiple_of(step * ROWS, ROWS), ROWS)
        front = [planes[c, 0, rows, :] for c in range(6)]
        back = [planes[c, 1, rows, :] for c in range(6)]
        front = force(front[:3], front[3:])
        back = force(back[:3], back[3:])
        place = lax.broadcasted_iota(jnp.int32, (ROWS, 256), 0) + step * ROWS
        for c in range(3):
            kept = jnp.where(place == 0, 0.0, back[c])
            up, down = split(front[c] + kept)
            eh[c, 0, rows, :] = up
            el[c, 0, rows, :] = down
            up, down = split(front[c] - kept)
            eh[c, 1, rows, :] = up
            el[c, 1, rows, :] = down

        @pl.when(step == 0)
        def _():
            for c in range(3):
                tail[c, 0:8, :] = back[c][0:8, :]

        return carry

    lax.fori_loop(0, 256 // ROWS, forces, 0)

    def analyse(c, carry):
        e_h = eh[c, 0]
        e_l = el[c, 0]
        o_h = eh[c, 1]
        o_l = el[c, 1]
        re = dot(bch_ref[...], e_h) + dot(bch_ref[...], e_l) + dot(bcl_ref[...], e_h)
        im = dot(bsh_ref[...], o_h) + dot(bsh_ref[...], o_l) + dot(bsl_ref[...], o_h)
        sign = jnp.concatenate([sign_ref[...]] * 2, axis=1)
        re = re + sign * tail[c, 0:1, :]
        out_ref[:, c, 0] = re.reshape(16, 16, 256)
        out_ref[:, c, 1] = im.reshape(16, 16, 256)
        return carry

    lax.fori_loop(0, 3, analyse, 0)


def in_planes(blocks, rows):
    synth_cos, synth_sin, back_cos, back_sin, wave, sign = tables(256)
    wst, wlo = right_tables()
    consts = [wave, sign, wst, wlo]
    for table in (synth_cos, synth_sin, back_cos, back_sin):
        consts.extend(two_parts(table))
    consts = [jnp.asarray(c) for c in consts]

    def whole(array):
        return pl.BlockSpec(array.shape, lambda i: (0,) * array.ndim)

    block = pl.BlockSpec((16, 3, 2, 16, 256), lambda i: (0, 0, 0, 0, i))
    return pl.pallas_call(
        plane_kernel,
        grid=(2,),
        in_specs=[block, pl.BlockSpec((8, 256), lambda i: (0, i))] + [whole(c) for c in consts],
        out_specs=block,
        out_shape=jax.ShapeDtypeStruct((16, 3, 2, 16, 512), F32),
        scratch_shapes=[
            pltpu.VMEM((6, 2, 256, 256), BF16),
            pltpu.VMEM((6, 2, 256, 256), BF16),
            pltpu.VMEM((6, 2, 256, 256), F32),
            pltpu.VMEM((3, 2, 256, 256), BF16),
            pltpu.VMEM((3, 2, 256, 256), BF16),
            pltpu.VMEM((3, 8, 256), F32),
        ],
        compiler_params=pltpu.CompilerParams(vmem_limit_bytes=LIMIT),
        name="in_planes",
    )(blocks, rows, *consts)


def slopes_of(pair, forward):
    up, down = split(pair)
    both = dot(forward, jnp.concatenate([up, down, up], axis=0))
    return both[:64], both[64:]


def twice(value):
    return jnp.concatenate([value, value], axis=1)


def post_kernel(r_ref, wave_ref, coef_ref, fwd_ref, non_ref, raw_ref, edge_ref, tmp):
    half = low_half((8, 128))
    for c in range(3):
        for pair in range(64):
            g, i = divmod(pair, 4)
            cols = slice(128 * i, 128 * i + 128)
            re = r_ref[g, c, 0, :, cols]
            im = r_ref[g, c, 1, :, cols]
            tmp[c, 16 * pair : 16 * pair + 8, :] = jnp.where(half, re, swap(im))
            tmp[c, 16 * pair + 8 : 16 * pair + 16, :] = jnp.where(half, swap(re), im)
    base = pl.program_id(0) * 8
    for kl in range(8):
        cells = []
        for c in range(3):
            block = tmp[c, pl.ds(kl, 128, stride=8), :].T
            non_ref[c, :, kl] = block.reshape(2, 64, 128)
            cells.append(block)
        x_r, x_s = slopes_of(jnp.concatenate([cells[0][:64], cells[0][64:]], axis=1), fwd_ref[...])
        y_r, y_s = slopes_of(jnp.concatenate([cells[1][:64], cells[1][64:]], axis=1), fwd_ref[...])
        wave = wave_ref[pl.ds(base + kl, 1), :]
        scaled = wave * coef_ref[0]
        for part in range(2):
            cols = slice(128 * part, 128 * part + 128)
            value = (
                coef_ref[1] * x_r[:, cols]
                + coef_ref[2] * x_s[:, cols]
                + coef_ref[3] * y_r[:, cols]
                + coef_ref[4] * y_s[:, cols]
            )
            if part == 0:
                value = value + scaled * cells[2][64:]
            else:
                value = value - scaled * cells[2][:64]
            raw_ref[part, kl] = value
            edge_ref[0, part, kl] = raw_ref[part, kl, pl.ds(0, 8, stride=8), :]
            edge_ref[1, part, kl] = raw_ref[part, kl, pl.ds(7, 8, stride=8), :]


def whole_spec(shape):
    return pl.BlockSpec(shape, lambda i: (0,) * len(shape))


FIELD = (2, 16, 64, 128)
EDGE = (2, 2, 16, 8, 128)


def from_blocks(blocks, wave, coef, forward):
    return pl.pallas_call(
        post_kernel,
        grid=(2,),
        in_specs=[
            pl.BlockSpec((16, 3, 2, 8, 512), lambda i: (0, 0, 0, i, 0)),
            whole_spec(wave.shape),
            whole_spec(coef.shape),
            whole_spec(forward.shape),
        ],
        out_specs=[
            pl.BlockSpec((3, 2, 8, 64, 128), lambda i: (0, 0, i, 0, 0)),
            pl.BlockSpec((2, 8, 64, 128), lambda i: (0, i, 0, 0)),
            pl.BlockSpec((2, 2, 8, 8, 128), lambda i: (0, 0, i, 0, 0)),
        ],
        out_shape=[
            jax.ShapeDtypeStruct((3, 2, 16, 64, 128), F32),
            jax.ShapeDtypeStruct(FIELD, F32),
            jax.ShapeDtypeStruct(EDGE, F32),
        ],
        scratch_shapes=[pltpu.VMEM((3, 1024, 128), F32)],
        compiler_params=pltpu.CompilerParams(vmem_limit_bytes=LIMIT),
        name="from_blocks",
    )(blocks, wave, coef, forward)


def lanes(value, index):
    return jnp.take_along_axis(value, index, axis=1, mode="promise_in_bounds")


def share(out_ref, field_ref, west_ref, east_ref, link_ref, part, kl):
    west_lane, west_from = link_ref[0], link_ref[1]
    east_lane, east_from = link_ref[2], link_ref[3]
    south_lane, south_here = link_ref[4], link_ref[5]
    north_lane, north_here = link_ref[6], link_ref[7]
    first = field_ref[part, kl, pl.ds(0, 8, stride=8), :]
    last = field_ref[part, kl, pl.ds(7, 8, stride=8), :]

    def pick(side, own, lane, origin):
        value = jnp.where(origin == 1, lanes(own, lane), 0.0)
        value = jnp.where(origin == 0, lanes(west_ref[side, part, kl], lane), value)
        return jnp.where(origin == 2, lanes(east_ref[side, part, kl], lane), value)

    out_ref[part, kl] = field_ref[part, kl]
    out_ref[part, kl, pl.ds(0, 8, stride=8), :] = first + pick(1, last, west_lane, west_from)
    out_ref[part, kl, pl.ds(7, 8, stride=8), :] = last + pick(0, first, east_lane, east_from)
    bottom = out_ref[part, kl, 0:8, :]
    top = out_ref[part, kl, 56:64, :]
    out_ref[part, kl, 0:8, :] = bottom + jnp.where(south_here == 1, lanes(top, south_lane), 0.0)
    out_ref[part, kl, 56:64, :] = top + jnp.where(north_here == 1, lanes(bottom, north_lane), 0.0)


def apply_stiffness(pair, shift, stiff_ref, fwd_ref, adj_ref, adl_ref):
    along_r, along_s = slopes_of(pair, fwd_ref[...])
    cross = twice(stiff_ref[1])
    back = jnp.concatenate(
        [
            twice(stiff_ref[0]) * along_r + cross * along_s,
            cross * along_r + twice(stiff_ref[2]) * along_s,
        ],
        axis=0,
    )
    up, down = split(back)
    folded = dot(adj_ref[...], jnp.concatenate([up, down], axis=0)) + dot(adl_ref[...], up)
    return folded + shift * twice(stiff_ref[3]) * pair


def image_kernel(
    raw_ref, west_ref, east_ref, link_ref, wave_ref, stiff_ref, fwd_ref, adj_ref, adl_ref,
    field_ref, image_ref, *rest, first,
):
    width = raw_ref.shape[1]
    base = pl.program_id(0) * width

    def body(kl, carry):
        for part in range(2):
            share(field_ref, raw_ref, west_ref, east_ref, link_ref, part, kl)
        pair = jnp.concatenate([field_ref[0, kl], field_ref[1, kl]], axis=1)
        wave = wave_ref[pl.ds(base + kl, 1), :]
        shift = twice(wave * wave + 1.0)
        image = apply_stiffness(pair, shift, stiff_ref, fwd_ref, adj_ref, adl_ref)
        image_ref[0, kl] = image[:, :128]
        image_ref[1, kl] = image[:, 128:]
        if first:
            edge_ref, sum_ref = rest
            for part in range(2):
                edge_ref[0, part, kl] = image_ref[part, kl, pl.ds(0, 8, stride=8), :]
                edge_ref[1, part, kl] = image_ref[part, kl, pl.ds(7, 8, stride=8), :]
            weighed = pair * pair * twice(stiff_ref[4])
            weighed = weighed[:, :128] + weighed[:, 128:]
            energy = pair * image
            energy = energy[:, :128] + energy[:, 128:]
            sum_ref[0, pl.ds(base + kl, 1), :] = jnp.sum(weighed, axis=0, keepdims=True)
            sum_ref[1, pl.ds(base + kl, 1), :] = jnp.sum(energy, axis=0, keepdims=True)
        return carry

    lax.fori_loop(0, width, body, 0)


def image_of(raw, west, east, links, wave, stiff, tables_left, first):
    pieces = 2
    width = 16 // pieces
    field_spec = pl.BlockSpec((2, width, 64, 128), lambda i: (0, i, 0, 0))
    edge_spec = pl.BlockSpec((2, 2, width, 8, 128), lambda i: (0, 0, i, 0, 0))
    out_specs = [field_spec, field_spec]
    out_shape = [jax.ShapeDtypeStruct(FIELD, F32)] * 2
    if first:
        out_specs += [edge_spec, whole_spec((2, 16, 128))]
        out_shape += [jax.ShapeDtypeStruct(EDGE, F32), jax.ShapeDtypeStruct((2, 16, 128), F32)]

    def kernel(*refs):
        image_kernel(*refs, first=first)

    return pl.pallas_call(
        kernel,
        grid=(pieces,),
        in_specs=[field_spec, edge_spec, edge_spec]
        + [whole_spec(a.shape) for a in (links, wave, stiff) + tuple(tables_left)],
        out_specs=out_specs,
        out_shape=out_shape,
        compiler_params=pltpu.CompilerParams(vmem_limit_bytes=LIMIT),
        name="image_first" if first else "image_second",
    )(raw, west, east, links, wave, stiff, *tables_left)


def totals(sum_ref):
    total = sum_ref[0]
    for d in range(1, sum_ref.shape[0]):
        total = total + sum_ref[d]
    return jnp.broadcast_to(jnp.sum(total, axis=-1, keepdims=True), total.shape)


def residual_kernel(field_ref, image_ref, shared_ref, second_ref, sum_ref, stiff_ref, out_ref, alpha):
    total = totals(sum_ref)
    alpha[...] = total[0] / total[1]

    def body(kl, carry):
        step = alpha[pl.ds(kl, 1), :]
        norm = jnp.zeros((64, 128), F32)
        energy = jnp.zeros((64, 128), F32)
        for part in range(2):
            residual = field_ref[part, kl] - step * shared_ref[part, kl]
            image = image_ref[part, kl] - step * second_ref[part, kl]
            norm = norm + residual * residual
            energy = energy + residual * image
        norm = norm * stiff_ref[4]
        out_ref[0, pl.ds(kl, 1), :] = jnp.sum(norm, axis=0, keepdims=True)
        out_ref[1, pl.ds(kl, 1), :] = jnp.sum(energy, axis=0, keepdims=True)
        return carry

    lax.fori_loop(0, 16, body, 0)


def residual_sums(field, image, shared, second, sums, stiff):
    return pl.pallas_call(
        residual_kernel,
        out_shape=jax.ShapeDtypeStruct((2, 16, 128), F32),
        scratch_shapes=[pltpu.VMEM((16, 128), F32)],
        compiler_params=pltpu.CompilerParams(vmem_limit_bytes=LIMIT),
        name="residual_sums",
    )(field, image, shared, second, sums, stiff)


def final_kernel(field_ref, shared_ref, sum_ref, next_ref, out_ref, scales):
    total = totals(sum_ref)
    norm0, energy0 = total[0], total[1]
    total = totals(next_ref)
    norm1, energy1 = total[0], total[1]
    alpha0 = norm0 / energy0
    beta = norm1 / norm0
    alpha1 = norm1 / (energy1 - beta * norm1 / alpha0)
    scales[0] = alpha0 + alpha1 * (1.0 + beta)
    scales[1] = -alpha1 * alpha0

    def body(kl, carry):
        one = scales[0, pl.ds(kl, 1), :]
        two = scales[1, pl.ds(kl, 1), :]
        for part in range(2):
            out_ref[part, kl] = one * field_ref[part, kl] + two * shared_ref[part, kl]
        return carry

    lax.fori_loop(0, 16, body, 0)


def final(field, shared, sums, later):
    return pl.pallas_call(
        final_kernel,
        out_shape=jax.ShapeDtypeStruct(FIELD, F32),
        scratch_shapes=[pltpu.VMEM((2, 16, 128), F32)],
        compiler_params=pltpu.CompilerParams(vmem_limit_bytes=LIMIT),
        name="pressure",
    )(field, shared, sums, later)


def link_tables(neighbours, width):
    device = lax.axis_index("elem")
    rows = []
    for side in range(2):
        ident = neighbours[side]
        place = ident - (device - 1) * width
        here = ident >= 0
        rows.append(jnp.where(here, place % width, 0))
        rows.append(jnp.where(here, place // width, 3))
    for side in range(2, 4):
        ident = neighbours[side]
        here = ident >= 0
        rows.append(jnp.where(here, ident - device * width, 0))
        rows.append(here.astype(jnp.int32))
    return jnp.broadcast_to(jnp.stack(rows)[:, None, :], (8, 8, width))


def inverse_multiplicity(neighbours):
    here = (neighbours >= 0).astype(F32)
    place = jnp.arange(8)
    column = (
        1.0 + here[0][None, :] * (place == 0)[:, None] + here[1][None, :] * (place == 7)[:, None]
    )
    row = 1.0 + here[2][None, :] * (place == 0)[:, None] + here[3][None, :] * (place == 7)[:, None]
    return (1.0 / (row[:, None, :] * column[None, :, :])).reshape(64, -1)


def swap_edges(edges):
    count = lax.axis_size("elem")
    west = lax.ppermute(edges, "elem", [(i, i + 1) for i in range(count - 1)])
    east = lax.ppermute(edges, "elem", [(i + 1, i) for i in range(count - 1)])
    return west, east


def gather_sums(sums):
    count = lax.axis_size("elem")
    spread = jnp.broadcast_to(sums[None], (count,) + sums.shape)
    return lax.all_to_all(spread, "elem", split_axis=0, concat_axis=0, tiled=True)


def per_device(velocity, metric, mass, sponge_rate, sponge_mask, neighbours):
    place = lax.axis_index("mode")
    damping = sponge_mask.astype(F32)[None, :] * sponge_rate
    rows = jnp.concatenate([metric, damping[None], jnp.zeros((3, 64, 128), F32)], axis=0)
    rows = lax.dynamic_slice_in_dim(rows, place * 8, 8, axis=2)
    rows = rows.transpose(0, 2, 1).reshape(8, 512)
    wave = (place * 16 + jnp.arange(16)).astype(F32) * (jnp.pi / 256)
    wave = jnp.broadcast_to(wave[:, None], (16, 128))
    rx, ry, sx, sy = metric[0], metric[1], metric[2], metric[3]
    coef = jnp.stack([mass, -mass * rx, -mass * sx, -mass * ry, -mass * sy])
    stiff = jnp.stack(
        [
            mass * (rx * rx + ry * ry),
            mass * (rx * sx + ry * sy),
            mass * (sx * sx + sy * sy),
            mass,
            inverse_multiplicity(neighbours),
        ]
    )
    links = link_tables(neighbours, 128)
    left = [jnp.asarray(t) for t in left_tables()]

    blocks = to_blocks(velocity)
    blocks = lax.all_to_all(blocks, "mode", split_axis=0, concat_axis=0, tiled=True)
    blocks = in_planes(blocks, rows)
    blocks = lax.all_to_all(blocks, "mode", split_axis=0, concat_axis=0, tiled=True)
    nonlinear, raw, edges = from_blocks(blocks, wave, coef, left[0])
    west, east = swap_edges(edges)
    field, image, edges, sums = image_of(raw, west, east, links, wave, stiff, left, True)
    sums = gather_sums(sums)
    west, east = swap_edges(edges)
    shared, second = image_of(image, west, east, links, wave, stiff, left, False)
    later = gather_sums(residual_sums(field, image, shared, second, sums, stiff))
    return nonlinear, final(field, shared, sums, later)


def solution(mesh):
    return jax.shard_map(
        per_device,
        mesh=mesh,
        in_specs=(
            P(None, None, "mode", None, "elem"),
            P(None, None, "elem"),
            P(None, "elem"),
            P(None, "elem"),
            P("elem"),
            P(None, "elem"),
        ),
        out_specs=(P(None, None, "mode", None, "elem"), P(None, "mode", None, "elem")),
        check_vma=False,
    )
```

time: 777 us -> 197 us (0.25); the launches traced: 763 us -> 195 us
  local copies, waits for them, and re-layouts: 408 us -> 7.86 us
  other arithmetic: 65.5 us -> 0.32 us
  matrix products: 57.7 us -> 0 us
  Pallas kernels: 0 us -> 51.3 us
  blocking collectives: 56.7 us -> 10.7 us
  waiting for transfers between devices: 137 us -> 95.5 us
    unnamed x131 -> x56, local copies, waits for them, and re-layouts: 187 us -> 6.82 us
    all_to_all x3 -> x0, local copies, waits for them, and re-layouts: 66.7 us -> none  [the longest x2 63 us: per_device(): lax.all_to_all(packed, 'mode', split_axis=3, concat_axis=2, tiled=True)]
    concatenate x5 -> x1, local copies, waits for them, and re-layouts: 66.6 us -> 0.07 us  [per_device(): jnp.concatenate([metric, damping[None], jnp.zeros((3, 64, 128), F32)], ax...]
    dot_general x16 -> x0, matrix products: 57.7 us -> none  [the longest x1 22.9 us: per_device(): jnp.einsum('jc,fcp->fjp', synth, flat, precision=lax.Precision.HIGHEST)]
    psum x3 -> x0, blocking collectives: 56.7 us -> none  [inner(): lax.psum(jnp.sum(first * second / multiplicity, axis=(0, 2, 3)), 'elem')]
    gather x24 -> x0, local copies, waits for them, and re-layouts: 53.9 us -> none  [pick_from(): return jnp.take(values, index, axis=3) * present]
    pallas_call x0 -> x7, Pallas kernels: none -> 51.3 us  [the longest x1 19.4 us: in_planes(): pl.pallas_call(plane_kernel, grid=(2,), in_specs=[block, pl.BlockSpec((8,...]
    all_to_all x2 -> x3, waiting for transfers between devices: 132 us -> 91.7 us  [the longest x2 91.7 us: per_device(): lax.all_to_all(blocks, 'mode', split_axis=0, concat_axis=0, tiled=True)]
  transfers between devices with their start and end apart: 8 -> 7, of which waited for: 5 -> 3; matrix products, arithmetic and copies ran while one was open for 2% -> 1% of each run, Pallas kernels for 0% -> 4%
where the time goes in v1:
time: 197 us; the launch traced here: 195 us
  waiting for transfers between devices  95.5 us (48%)
  Pallas kernels  51.3 us (26%)
  starting transfers between devices  28.6 us (15%)
  blocking collectives  10.7 us (5%)
  local copies, waits for them, and re-layouts  7.86 us (4%)
    all_to_all x2, waiting for transfers between devices, per_device(): lax.all_to_all(blocks, 'mode', split_axis=0, concat_axis=0, tiled=True)  91.7 us
    pallas_call x1, Pallas kernels, in_planes(): pl.pallas_call(plane_kernel, grid=(2,), in_specs=[block, pl.BlockSpec((8,...  19.4 us
    pallas_call x2, Pallas kernels, image_of(): pl.pallas_call(kernel, grid=(pieces,), in_specs=[field_spec, edge_spec, e...  18.7 us
    all_to_all x2, starting transfers between devices, per_device(): lax.all_to_all(blocks, 'mode', split_axis=0, concat_axis=0, tiled=True)  13 us
    all_to_all x1, blocking collectives, gather_sums(): lax.all_to_all(spread, 'elem', split_axis=0, concat_axis=0, tiled=True)  10.7 us
    ppermute x2, starting transfers between devices, swap_edges(): west = lax.ppermute(edges, 'elem', [(i, i + 1) for i in range(count - 1)])  7.97 us
    unnamed x56, local copies, waits for them, and re-layouts  6.82 us
    pallas_call x1, Pallas kernels, to_blocks(): pl.pallas_call(pre_kernel, grid=(3,), in_specs=[pl.BlockSpec((1, 2, 16, 6...  5.25 us
  transfers between devices with their start and end apart: 7, of which 3 were waited for; matrix products, arithmetic and copies ran while one was open for 1% of the time, Pallas kernels for 4%

profile of v1, /device:TPU:0, one launch (start us, length us, event | category | flops | bytes accessed | tf_op | source)
XLA Modules:
  0.0 195.3 jit_solution(9042367517140237546)
XLA Ops:
  0.6 5.3 %to_blocks.1 = f32[16,3,2,16,512]{4,3,2,1,0:T(8,128)} custom-call(f32[3,2,16,64,128]{4,3,2,1,0:T(8,128)} %v_ref.1), custom_call_target="tpu_custom_call" | custom-call | tf_op jit(solution)/shard_map/to_blocks/pallas_call | solution.py:108
  5.9 0.0 copy-start.8
  5.9 0.0 copy-start.9
  5.9 0.0 copy-start.10
  5.9 0.0 copy-start.11
  5.9 0.0 copy-start.12
  6.0 0.0 copy-start.13
  6.0 0.0 copy-start.14
  6.0 0.0 copy-start.15
  6.0 0.0 copy-start.16
  6.0 0.0 copy-start.17
  6.0 0.0 copy-start.20
  6.0 8.3 %all-to-all-start = ((f32[16,3,2,16,512]{4,3,2,1,0:T(8,128)}), f32[16,3,2,16,512]{4,3,2,1,0:T(8,128)}, u32[]{:S(2)}, u32[]{:S(2)}) async-start(f32[16,3,2,16,512]{4,3,2,1,0:T(8,128)} %to_blocks.1), calls=%async_computation | async-start | bytes 6291456 | tf_op jit(solution)/shard_map/all_to_all | solution.py:584
  14.4 0.0 copy-done.27
  14.4 0.1 pad.2.clone
  14.5 0.0 copy-done.25
  14.5 0.1 fusion.1
  14.6 0.1 copy.23
  14.7 0.1 reshape.166.rows_ref
  14.8 47.1 %all-to-all-done.z_ref = f32[16,3,2,16,512]{4,3,2,1,0:T(8,128)} async-done(((f32[16,3,2,16,512]{4,3,2,1,0:T(8,128)}), f32[16,3,2,16,512]{4,3,2,1,0:T(8,128)}, u32[]{:S(2)}, u32[]{:S(2)}) %all-to-all-start) | async-done | bytes 3145760 | tf_op jit(solution)/shard_map/all_to_all | solution.py:584
  61.9 0.0 copy-done.10
  61.9 0.0 copy-done.11
  61.9 0.0 copy-done.12
  62.0 0.0 copy-done.13
  62.0 0.0 copy-done.14
  62.0 0.0 copy-done.15
  62.0 0.0 copy-done.16
  62.0 0.0 copy-done.17
  62.0 0.0 copy-done.20
  62.0 19.4 %in_planes.1 = f32[16,3,2,16,512]{4,3,2,1,0:T(8,128)} custom-call(f32[16,3,2,16,512]{4,3,2,1,0:T(8,128)} %all-to-all-done.z_ref, f32[8,512]{1,0:T(8,128)S(1)} %reshape.166.rows_ref, f32[256,128]{1,0:T(8,128)S(1)} %copy-done.9, f32[256,128]{1,0:T(8,128)S(1)} %copy-done.10, bf16[256,256]{1,0:T(8,128)(2,1)S(1)} %copy-done.11, bf16[128,256]{1,0:T(8,128)(2,1)S(1)} %copy-done.20, ...), custom_call_target="tpu_custom_call" | custom-call | tf_op jit(solution)/shard_map/in_planes/pallas_call | solution.py:252
  81.4 4.6 %all-to-all-start.1 = ((f32[16,3,2,16,512]{4,3,2,1,0:T(8,128)}), f32[16,3,2,16,512]{4,3,2,1,0:T(8,128)}, u32[]{:S(2)}, u32[]{:S(2)}) async-start(f32[16,3,2,16,512]{4,3,2,1,0:T(8,128)} %in_planes.1), calls=%async_computation.1 | async-start | bytes 6291456 | tf_op jit(solution)/shard_map/all_to_all | solution.py:586
  86.1 0.0 copy-start.18
  86.1 0.0 copy-start.21
  86.2 0.1 multiply_add_fusion.1
  86.3 0.0 copy-done.24
  86.4 44.6 %all-to-all-done.1.r_ref = f32[16,3,2,16,512]{4,3,2,1,0:T(8,128)} async-done(((f32[16,3,2,16,512]{4,3,2,1,0:T(8,128)}), f32[16,3,2,16,512]{4,3,2,1,0:T(8,128)}, u32[]{:S(2)}, u32[]{:S(2)}) %all-to-all-start.1) | async-done | bytes 3145760 | tf_op jit(solution)/shard_map/all_to_all | solution.py:586
  130.9 0.1 broadcast_in_dim.23.wave_ref.refs_4_
  131.0 4.8 %from_blocks.1 = (f32[3,2,16,64,128]{4,3,2,1,0:T(8,128)}, f32[2,16,64,128]{3,2,1,0:T(8,128)S(1)}, f32[2,2,16,8,128]{4,3,2,1,0:T(8,128)S(1)}) custom-call(f32[16,3,2,16,512]{4,3,2,1,0:T(8,128)} %all-to-all-done.1.r_ref, f32[16,128]{1,0:T(8,128)S(1)} %broadcast_in_dim.23.wave_ref.refs_4_, f32[5,64,128]{2,1,0:T(8,128)S(1)} %bitcast_dynamic-update-slice_fusion.4.coef_ref, ...), custom_call_target="tpu_custom_call" | custom-call | tf_op jit(solution)/shard_map/from_blocks/pallas_call | solution.py:328
  135.8 1.0 copy-done.1
  136.8 1.3 collective-permute-start
  138.1 1.3 collective-permute-start.1
  139.4 0.0 collective-permute-done.refs_1_
  139.5 3.8 %collective-permute-done.1.refs_2_ = f32[2,2,16,8,128]{4,3,2,1,0:T(8,128)S(1)} collective-permute-done((f32[2,2,16,8,128]{4,3,2,1,0:T(8,128)S(1)}, f32[2,2,16,8,128]{4,3,2,1,0:T(8,128)S(1)}, u32[]{:S(2)}, u32[]{:S(2)}) %collective-permute-start.1) | collective-permute-done | bytes 262176 | tf_op jit(solution)/shard_map/ppermute | solution.py:551
  143.2 10.0 %image_first.1 = (f32[2,16,64,128]{3,2,1,0:T(8,128)S(1)}, f32[2,16,64,128]{3,2,1,0:T(8,128)S(1)}, f32[2,2,16,8,128]{4,3,2,1,0:T(8,128)S(1)}, f32[2,16,128]{2,1,0:T(8,128)S(1)}) custom-call(f32[2,16,64,128]{3,2,1,0:T(8,128)} %copy-done.1, f32[2,2,16,8,128]{4,3,2,1,0:T(8,128)S(1)} %collective-permute-done.refs_1_, ...), custom_call_target="tpu_custom_call" | custom-call | tf_op jit(solution)/shard_map/image_first/pallas_call | solution.py:440
  153.2 6.7 %collective-permute-start.2 = (f32[2,2,16,8,128]{4,3,2,1,0:T(8,128)S(1)}, f32[2,2,16,8,128]{4,3,2,1,0:T(8,128)S(1)}, u32[]{:S(2)}, u32[]{:S(2)}) collective-permute-start(f32[2,2,16,8,128]{4,3,2,1,0:T(8,128)S(1)} %get-tuple-element.16), channel_id=1, source_target_pairs={{0,16},{16,32},{32,48},{48,64},{64,80},{80,96},{96,112},{1,17},{17... | collective-permute-start | bytes 786440 | tf_op jit(solution)/shard_map/ppermute | solution.py:550
  159.9 1.3 collective-permute-start.3
  161.2 0.7 broadcast_in_dim.26
  161.8 5.1 %all-to-all-start.2 = ((f32[8,2,16,128]{3,2,1,0:T(8,128)}), f32[8,2,16,128]{3,2,1,0:T(8,128)S(1)}, u32[]{:S(2)}, u32[]{:S(2)}) async-start(f32[8,2,16,128]{3,2,1,0:T(8,128)} %broadcast_in_dim.26), calls=%async_computation.2 | async-start | bytes 262144 | tf_op jit(solution)/shard_map/all_to_all | solution.py:558
  166.9 0.0 collective-permute-done.2.refs_1_
  166.9 0.0 copy-start.3
  166.9 0.7 copy-done.3
  167.6 0.0 collective-permute-done.3.refs_2_
  167.6 0.7 copy-done.5
  168.3 0.9 copy-done.4
  169.3 0.9 copy-done.6
  170.2 0.8 copy-done.19
  171.0 0.7 copy-done.22
  171.7 8.7 %image_second.1 = (f32[2,16,64,128]{3,2,1,0:T(8,128)S(1)}, f32[2,16,64,128]{3,2,1,0:T(8,128)S(1)}) custom-call(f32[2,16,64,128]{3,2,1,0:T(8,128)S(1)} %get-tuple-element.15.refs_0_.image_ref, f32[2,2,16,8,128]{4,3,2,1,0:T(8,128)S(1)} %copy-done.4, f32[2,2,16,8,128]{4,3,2,1,0:T(8,128)S(1)} %copy-done.6, s32[8,8,128]{2,1,0:T(8,128)S(1)} %broadcast_in_dim.25.refs_3_, ...), custom_call_target="tpu_custom_call" | custom-call | tf_op jit(solution)/shard_map/image_second/pallas_call | solution.py:440
  180.4 0.0 copy-start
  180.5 1.0 copy-done
  181.4 0.0 all-to-all-done.2.sum_ref
  181.4 1.9 residual_sums.1
  183.3 10.7 %all_to_all.20.next_ref = f32[8,2,16,128]{3,2,1,0:T(8,128)S(1)} all-to-all(f32[8,2,16,128]{3,2,1,0:T(8,128)S(1)} %broadcast_in_dim.52), channel_id=1, replica_groups=mesh['elem'=8,'mode'=16] {'elem'}, dimensions={0} | all-to-all | bytes 262144 | tf_op jit(solution)/shard_map/all_to_all | solution.py:558
  194.0 1.3 pressure.1
  (41 shorter events, 0.2 us)
Async XLA Ops:
  5.9 8.5 %copy-start.27 = (s32[128]{0:T(128)S(1)}, s32[128]{0:T(128)}, u32[]{:S(2)}) copy-start(s32[128]{0:T(128)} %param.25) | copy-start | bytes 1540
  5.9 8.6 %copy-start.25 = (f32[64,128]{1,0:T(8,128)S(1)}, f32[64,128]{1,0:T(8,128)}, u32[]{:S(2)}) copy-start(f32[64,128]{1,0:T(8,128)} %param.24) | copy-start | bytes 98308
  5.9 8.6 %copy-start.23 = (f32[4,64,128]{2,1,0:T(8,128)S(1)}, f32[4,64,128]{2,1,0:T(8,128)}, u32[]{:S(2)}) copy-start(f32[4,64,128]{2,1,0:T(8,128)} %param.22) | copy-start | bytes 393220
  5.9 56.0 %copy-start.7 = (bf16[272,256]{1,0:T(8,128)(2,1)S(1)}, bf16[272,256]{1,0:T(8,128)(2,1)}, u32[]{:S(2)}) copy-start(bf16[272,256]{1,0:T(8,128)(2,1)} %constant.106.clone.ch_ref) | copy-start | bytes 417796
  5.9 56.0 %copy-start.8 = (bf16[272,256]{1,0:T(8,128)(2,1)S(1)}, bf16[272,256]{1,0:T(8,128)(2,1)}, u32[]{:S(2)}) copy-start(bf16[272,256]{1,0:T(8,128)(2,1)} %constant.107.clone.cl_ref) | copy-start | bytes 417796
  5.9 56.0 %copy-start.9 = (f32[256,128]{1,0:T(8,128)S(1)}, f32[256,128]{1,0:T(8,128)}, u32[]{:S(2)}) copy-start(f32[256,128]{1,0:T(8,128)} %constant.102.clone.wave_ref) | copy-start | bytes 393220
  5.9 56.0 %copy-start.10 = (f32[256,128]{1,0:T(8,128)S(1)}, f32[256,128]{1,0:T(8,128)}, u32[]{:S(2)}) copy-start(f32[256,128]{1,0:T(8,128)} %constant.103.clone.sign_ref) | copy-start | bytes 393220
  5.9 56.0 %copy-start.11 = (bf16[256,256]{1,0:T(8,128)(2,1)S(1)}, bf16[256,256]{1,0:T(8,128)(2,1)}, u32[]{:S(2)}) copy-start(bf16[256,256]{1,0:T(8,128)(2,1)} %constant.104.clone.wst_ref) | copy-start | bytes 393220
  5.9 56.0 %copy-start.12 = (bf16[256,256]{1,0:T(8,128)(2,1)S(1)}, bf16[256,256]{1,0:T(8,128)(2,1)}, u32[]{:S(2)}) copy-start(bf16[256,256]{1,0:T(8,128)(2,1)} %constant.108.clone.sh_ref) | copy-start | bytes 393220
  6.0 56.0 %copy-start.13 = (bf16[256,256]{1,0:T(8,128)(2,1)S(1)}, bf16[256,256]{1,0:T(8,128)(2,1)}, u32[]{:S(2)}) copy-start(bf16[256,256]{1,0:T(8,128)(2,1)} %constant.109.clone.sl_ref) | copy-start | bytes 393220
  6.0 56.0 %copy-start.14 = (bf16[256,256]{1,0:T(8,128)(2,1)S(1)}, bf16[256,256]{1,0:T(8,128)(2,1)}, u32[]{:S(2)}) copy-start(bf16[256,256]{1,0:T(8,128)(2,1)} %constant.110.clone.bch_ref) | copy-start | bytes 393220
  6.0 56.0 %copy-start.15 = (bf16[256,256]{1,0:T(8,128)(2,1)S(1)}, bf16[256,256]{1,0:T(8,128)(2,1)}, u32[]{:S(2)}) copy-start(bf16[256,256]{1,0:T(8,128)(2,1)} %constant.111.clone.bcl_ref) | copy-start | bytes 393220
  6.0 56.0 %copy-start.16 = (bf16[256,256]{1,0:T(8,128)(2,1)S(1)}, bf16[256,256]{1,0:T(8,128)(2,1)}, u32[]{:S(2)}) copy-start(bf16[256,256]{1,0:T(8,128)(2,1)} %constant.112.clone.bsh_ref) | copy-start | bytes 393220
  6.0 56.0 %copy-start.17 = (bf16[256,256]{1,0:T(8,128)(2,1)S(1)}, bf16[256,256]{1,0:T(8,128)(2,1)}, u32[]{:S(2)}) copy-start(bf16[256,256]{1,0:T(8,128)(2,1)} %constant.113.clone.bsl_ref) | copy-start | bytes 393220
  6.0 56.0 %copy-start.20 = (bf16[128,256]{1,0:T(8,128)(2,1)S(1)}, bf16[128,256]{1,0:T(8,128)(2,1)}, u32[]{:S(2)}) copy-start(bf16[128,256]{1,0:T(8,128)(2,1)} %constant.105.clone.wlo_ref) | copy-start | bytes 196612
  6.0 55.9 %all-to-all-start = ((f32[16,3,2,16,512]{4,3,2,1,0:T(8,128)}), f32[16,3,2,16,512]{4,3,2,1,0:T(8,128)}, u32[]{:S(2)}, u32[]{:S(2)}) async-start(f32[16,3,2,16,512]{4,3,2,1,0:T(8,128)} %to_blocks.1), calls=%async_computation | async-start | bytes 6291456 | tf_op jit(solution)/shard_map/all_to_all | solution.py:584
  81.4 4.7 %copy-start.26 = (s32[4,128]{1,0:T(4,128)S(1)}, s32[4,128]{1,0:T(4,128)}, u32[]{:S(2)}) copy-start(s32[4,128]{1,0:T(4,128)} %param.26) | copy-start | bytes 6148
  81.4 4.9 %copy-start.24 = (f32[64,128]{1,0:T(8,128)S(1)}, f32[64,128]{1,0:T(8,128)}, u32[]{:S(2)}) copy-start(f32[64,128]{1,0:T(8,128)} %param.23) | copy-start | bytes 98308
  81.4 49.6 %copy-start.2 = (bf16[128,192]{1,0:T(8,128)(2,1)S(1)}, bf16[128,192]{1,0:T(8,128)(2,1)}, u32[]{:S(2)}) copy-start(bf16[128,192]{1,0:T(8,128)(2,1)} %constant.99.clone.fwd_ref.refs_6_) | copy-start | bytes 147460
  81.4 49.5 %all-to-all-start.1 = ((f32[16,3,2,16,512]{4,3,2,1,0:T(8,128)}), f32[16,3,2,16,512]{4,3,2,1,0:T(8,128)}, u32[]{:S(2)}, u32[]{:S(2)}) async-start(f32[16,3,2,16,512]{4,3,2,1,0:T(8,128)} %in_planes.1), calls=%async_computation.1 | async-start | bytes 6291456 | tf_op jit(solution)/shard_map/all_to_all | solution.py:586
  86.1 57.2 %copy-start.18 = (bf16[64,256]{1,0:T(8,128)(2,1)S(1)}, bf16[64,256]{1,0:T(8,128)(2,1)}, u32[]{:S(2)}) copy-start(bf16[64,256]{1,0:T(8,128)(2,1)} %constant.100.clone.refs_7_) | copy-start | bytes 98308
  86.1 57.2 %copy-start.21 = (bf16[64,128]{1,0:T(8,128)(2,1)S(1)}, bf16[64,128]{1,0:T(8,128)(2,1)}, u32[]{:S(2)}) copy-start(bf16[64,128]{1,0:T(8,128)(2,1)} %constant.101.clone.refs_8_) | copy-start | bytes 49156
  135.8 1.0 copy-start.1
  136.8 2.7 %collective-permute-start = (f32[2,2,16,8,128]{4,3,2,1,0:T(8,128)S(1)}, f32[2,2,16,8,128]{4,3,2,1,0:T(8,128)S(1)}, u32[]{:S(2)}, u32[]{:S(2)}) collective-permute-start(f32[2,2,16,8,128]{4,3,2,1,0:T(8,128)S(1)} %get-tuple-element.13), channel_id=1, source_target_pairs={{0,16},{16,32},{32,48},{48,64},{64,80},{80,96},{96,112},{1,17},{17... | collective-permute-start | bytes 786440 | tf_op jit(solution)/shard_map/ppermute | solution.py:550
  138.1 5.1 %collective-permute-start.1 = (f32[2,2,16,8,128]{4,3,2,1,0:T(8,128)S(1)}, f32[2,2,16,8,128]{4,3,2,1,0:T(8,128)S(1)}, u32[]{:S(2)}, u32[]{:S(2)}) collective-permute-start(f32[2,2,16,8,128]{4,3,2,1,0:T(8,128)S(1)} %get-tuple-element.13), channel_id=1, source_target_pairs={{16,0},{32,16},{48,32},{64,48},{80,64},{96,80},{112,96},{17,1},{33... | collective-permute-start | bytes 786440 | tf_op jit(solution)/shard_map/ppermute | solution.py:551
  153.2 13.7 %collective-permute-start.2 = (f32[2,2,16,8,128]{4,3,2,1,0:T(8,128)S(1)}, f32[2,2,16,8,128]{4,3,2,1,0:T(8,128)S(1)}, u32[]{:S(2)}, u32[]{:S(2)}) collective-permute-start(f32[2,2,16,8,128]{4,3,2,1,0:T(8,128)S(1)} %get-tuple-element.16), channel_id=1, source_target_pairs={{0,16},{16,32},{32,48},{48,64},{64,80},{80,96},{96,112},{1,17},{17... | collective-permute-start | bytes 786440 | tf_op jit(solution)/shard_map/ppermute | solution.py:550
  159.9 7.7 %collective-permute-start.3 = (f32[2,2,16,8,128]{4,3,2,1,0:T(8,128)S(1)}, f32[2,2,16,8,128]{4,3,2,1,0:T(8,128)S(1)}, u32[]{:S(2)}, u32[]{:S(2)}) collective-permute-start(f32[2,2,16,8,128]{4,3,2,1,0:T(8,128)S(1)} %get-tuple-element.16), channel_id=1, source_target_pairs={{16,0},{32,16},{48,32},{64,48},{80,64},{96,80},{112,96},{17,1},{33... | collective-permute-start | bytes 786440 | tf_op jit(solution)/shard_map/ppermute | solution.py:551
  161.8 19.6 %all-to-all-start.2 = ((f32[8,2,16,128]{3,2,1,0:T(8,128)}), f32[8,2,16,128]{3,2,1,0:T(8,128)S(1)}, u32[]{:S(2)}, u32[]{:S(2)}) async-start(f32[8,2,16,128]{3,2,1,0:T(8,128)} %broadcast_in_dim.26), calls=%async_computation.2 | async-start | bytes 262144 | tf_op jit(solution)/shard_map/all_to_all | solution.py:558
  166.9 0.7 copy-start.3
  167.6 0.7 copy-start.5
  168.3 0.9 copy-start.4
  169.3 0.9 copy-start.6
  170.2 0.8 copy-start.19
  171.0 0.7 copy-start.22
  180.4 1.0 copy-start

commit v2 on v1

v2 whole, which is shorter than its diff:
```python
import jax
import jax.numpy as jnp
import ml_dtypes
import numpy as np
from jax import lax
from jax.experimental import pallas as pl
from jax.experimental.pallas import tpu as pltpu
from jax.sharding import PartitionSpec as P

F32 = jnp.float32
BF16 = jnp.bfloat16
MIB = 1024 * 1024
WIDE = 48 * MIB
NARROW = 16 * MIB


def cheb_matrix():
    count = 8
    places = np.arange(count)
    points = np.cos(np.pi * places / (count - 1))
    weights = np.where((places == 0) | (places == count - 1), 2.0, 1.0)
    signs = weights * (-1.0) ** places
    differ = points[:, None] - points[None, :] + np.eye(count)
    table = np.outer(signs, 1.0 / signs) / differ
    table = table - np.eye(count) * np.sum(table, axis=1)[:, None]
    return table.astype(np.float32).astype(np.float64)


def two_parts(table):
    high = table.astype(np.float32).astype(ml_dtypes.bfloat16)
    low = (table - high.astype(np.float64)).astype(np.float32).astype(ml_dtypes.bfloat16)
    return high, low


def tables(modes):
    planes = 2 * modes
    order = np.arange(modes)
    spots = np.arange(modes)
    phase = (spots[:, None] * order[None, :]) % planes
    angle = phase * (2.0 * np.pi / planes)
    weight = np.where(order == 0, 1.0, 2.0)
    cosine = np.cos(angle)
    sine = np.sin(angle)
    last = np.zeros((16, modes))
    last[0] = weight * (-1.0) ** order
    synth_cos = np.concatenate([weight * cosine, last], axis=0)
    synth_sin = weight * sine
    back_cos = cosine.T / planes
    back_sin = -sine.T / planes
    wave = np.broadcast_to((order * np.pi / modes)[:, None], (modes, 128)).astype(np.float32)
    sign = np.broadcast_to(((-1.0) ** order / planes)[:, None], (modes, 128)).astype(np.float32)
    return synth_cos, synth_sin, back_cos, back_sin, wave, sign


def right_tables():
    table = cheb_matrix()
    two = np.eye(2)
    eight = np.eye(8)
    along_r = np.kron(two, np.kron(eight, table.T))
    along_s = np.kron(two, np.kron(table.T, eight))
    high, low = two_parts(np.concatenate([along_r, along_s], axis=1))
    return np.concatenate([high, high, low], axis=0)


def left_tables():
    table = cheb_matrix()
    eight = np.eye(8)
    along_r = np.kron(eight, table)
    along_s = np.kron(table, eight)
    high, low = two_parts(np.concatenate([along_r, along_s], axis=0))
    forward = np.concatenate([high, high, low], axis=1)
    high, low = two_parts(np.concatenate([along_r.T, along_s.T], axis=1))
    return forward, np.concatenate([high, high], axis=1), low


def split(value):
    high = value.astype(BF16)
    low = (value - high.astype(F32)).astype(BF16)
    return high, low


def dot(first, second):
    return jnp.dot(first, second, preferred_element_type=F32)


def low_half(shape):
    return lax.broadcasted_iota(jnp.int32, shape, len(shape) - 1) < 64


def swap(value):
    return pltpu.roll(value, 64, 1)


def pre_kernel(v_ref, y_ref, tmp):
    for kl in range(16):
        block = v_ref[0, :, kl].reshape(128, 128)
        tmp[pl.ds(kl, 128, stride=16), :] = block.T
    half = low_half((16, 128))
    for pair in range(64):
        first = tmp[32 * pair : 32 * pair + 16, :]
        second = tmp[32 * pair + 16 : 32 * pair + 32, :]
        g, i = divmod(pair, 4)
        cols = slice(128 * i, 128 * i + 128)
        y_ref[g, 0, 0, :, cols] = jnp.where(half, first, swap(second))
        y_ref[g, 0, 1, :, cols] = jnp.where(half, swap(first), second)


def to_blocks(velocity):
    return pl.pallas_call(
        pre_kernel,
        grid=(3,),
        in_specs=[pl.BlockSpec((1, 2, 16, 64, 128), lambda c: (c, 0, 0, 0, 0))],
        out_specs=pl.BlockSpec((16, 1, 2, 16, 512), lambda c: (0, c, 0, 0, 0)),
        out_shape=jax.ShapeDtypeStruct((16, 3, 2, 16, 512), F32),
        scratch_shapes=[pltpu.VMEM((2048, 128), F32)],
        compiler_params=pltpu.CompilerParams(vmem_limit_bytes=WIDE),
        name="to_blocks",
    )(velocity)


ROWS = 32


def plane_kernel(
    z_ref, rows_ref, wave_ref, sign_ref, slope_ref, cos_ref, sin_ref, back_cos_ref, back_sin_ref, out_ref, high, low, planes, eh, el, tail,
):
    rx = rows_ref[0:1, :]
    ry = rows_ref[1:2, :]
    sx = rows_ref[2:3, :]
    sy = rows_ref[3:4, :]
    damping = rows_ref[4:5, :]
    count = ROWS // 16

    def curls(step, carry):
        rows = pl.ds(pl.multiple_of(step * ROWS, ROWS), ROWS)
        wave = jnp.concatenate([wave_ref[rows, :]] * 2, axis=1)
        fields = {}
        slopes = {}
        for c in range(3):
            for part in range(2):
                value = z_ref[pl.ds(step * count, count), c, part].reshape(ROWS, 256)
                up, down = split(value)
                high[c, part, rows, :] = up
                low[c, part, rows, :] = down
                fields[c, part] = value
                pieces = []
                for q in range(2):
                    cols = slice(128 * q, 128 * q + 128)
                    three = jnp.concatenate([up[:, cols], down[:, cols], up[:, cols]], axis=1)
                    pieces.append(dot(three, slope_ref[...]))
                slopes[c, part] = (
                    jnp.concatenate([pieces[0][:, :128], pieces[1][:, :128]], axis=1),
                    jnp.concatenate([pieces[0][:, 128:], pieces[1][:, 128:]], axis=1),
                )
        for part in range(2):
            u_r, u_s = slopes[0, part]
            v_r, v_s = slopes[1, part]
            w_r, w_s = slopes[2, part]
            if part == 0:
                dz_u = -wave * fields[0, 1]
                dz_v = -wave * fields[1, 1]
            else:
                dz_u = wave * fields[0, 0]
                dz_v = wave * fields[1, 0]
            swirl = (
                ry * w_r + sy * w_s - dz_v,
                dz_u - (rx * w_r + sx * w_s),
                rx * v_r + sx * v_s - (ry * u_r + sy * u_s),
            )
            for c in range(3):
                up, down = split(swirl[c])
                high[3 + c, part, rows, :] = up
                low[3 + c, part, rows, :] = down
        return carry

    lax.fori_loop(0, 256 // ROWS, curls, 0, unroll=True)

    def synth(c, carry):
        even = dot(cos_ref[...], jnp.concatenate([high[c, 0], low[c, 0], high[c, 0]], axis=0))
        odd = dot(sin_ref[...], jnp.concatenate([high[c, 1], low[c, 1], high[c, 1]], axis=0))
        planes[c, 0] = even[:256] - odd
        planes[c, 1] = even[:256] + odd
        planes[c, 1, 0:1, :] = even[256:257, :]
        return carry

    lax.fori_loop(0, 6, synth, 0, unroll=True)

    def force(u, w):
        return (
            u[1] * w[2] - u[2] * w[1] - damping * (u[0] - 1.0),
            u[2] * w[0] - u[0] * w[2] - damping * u[1],
            u[0] * w[1] - u[1] * w[0] - damping * u[2],
        )

    def forces(step, carry):
        rows = pl.ds(pl.multiple_of(step * ROWS, ROWS), ROWS)
        front = [planes[c, 0, rows, :] for c in range(6)]
        back = [planes[c, 1, rows, :] for c in range(6)]
        front = force(front[:3], front[3:])
        back = force(back[:3], back[3:])
        place = lax.broadcasted_iota(jnp.int32, (ROWS, 256), 0) + step * ROWS
        for c in range(3):
            kept = jnp.where(place == 0, 0.0, back[c])
            up, down = split(front[c] + kept)
            eh[c, 0, rows, :] = up
            el[c, 0, rows, :] = down
            up, down = split(front[c] - kept)
            eh[c, 1, rows, :] = up
            el[c, 1, rows, :] = down

        @pl.when(step == 0)
        def _():
            for c in range(3):
                tail[c, 0:8, :] = back[c][0:8, :]

        return carry

    lax.fori_loop(0, 256 // ROWS, forces, 0, unroll=True)

    def analyse(c, carry):
        re = dot(back_cos_ref[...], jnp.concatenate([eh[c, 0], el[c, 0], eh[c, 0]], axis=0))
        im = dot(back_sin_ref[...], jnp.concatenate([eh[c, 1], el[c, 1], eh[c, 1]], axis=0))
        sign = jnp.concatenate([sign_ref[...]] * 2, axis=1)
        re = re + sign * tail[c, 0:1, :]
        out_ref[:, c, 0] = re.reshape(16, 16, 256)
        out_ref[:, c, 1] = im.reshape(16, 16, 256)
        return carry

    lax.fori_loop(0, 3, analyse, 0, unroll=True)


def in_planes(blocks, rows):
    synth_cos, synth_sin, back_cos, back_sin, wave, sign = tables(256)
    consts = [wave, sign, right_tables()]
    for table in (synth_cos, synth_sin, back_cos, back_sin):
        high, low = two_parts(table)
        consts.append(np.concatenate([high, high, low], axis=1))
    consts = [jnp.asarray(c) for c in consts]

    def whole(array):
        return pl.BlockSpec(array.shape, lambda i: (0,) * array.ndim)

    block = pl.BlockSpec((16, 3, 2, 16, 256), lambda i: (0, 0, 0, 0, i))
    return pl.pallas_call(
        plane_kernel,
        grid=(2,),
        in_specs=[block, pl.BlockSpec((8, 256), lambda i: (0, i))] + [whole(c) for c in consts],
        out_specs=block,
        out_shape=jax.ShapeDtypeStruct((16, 3, 2, 16, 512), F32),
        scratch_shapes=[
            pltpu.VMEM((6, 2, 256, 256), BF16),
            pltpu.VMEM((6, 2, 256, 256), BF16),
            pltpu.VMEM((6, 2, 256, 256), F32),
            pltpu.VMEM((3, 2, 256, 256), BF16),
            pltpu.VMEM((3, 2, 256, 256), BF16),
            pltpu.VMEM((3, 8, 256), F32),
        ],
        compiler_params=pltpu.CompilerParams(vmem_limit_bytes=WIDE),
        name="in_planes",
    )(blocks, rows, *consts)


def slopes_of(pair, forward):
    up, down = split(pair)
    both = dot(forward, jnp.concatenate([up, down, up], axis=0))
    return both[:64], both[64:]


def twice(value):
    return jnp.concatenate([value, value], axis=1)


FIELD = (2, 16, 64, 128)
EDGE = (2, 2, 16, 8, 128)


def whole_spec(shape):
    return pl.BlockSpec(shape, lambda i: (0,) * len(shape))


def in_smem():
    return pl.BlockSpec(memory_space=pltpu.SMEM)


def wave_of(ids_ref, kl):
    return (ids_ref[1] * 16 + kl).astype(F32) * (np.pi / 256)


def post_kernel(ids_ref, r_ref, metric_ref, mass_ref, fwd_ref, non_ref, raw_ref, edge_ref, tmp, coef):
    half = low_half((8, 128))
    for c in range(3):
        for pair in range(64):
            g, i = divmod(pair, 4)
            cols = slice(128 * i, 128 * i + 128)
            re = r_ref[g, c, 0, :, cols]
            im = r_ref[g, c, 1, :, cols]
            tmp[c, 16 * pair : 16 * pair + 8, :] = jnp.where(half, re, swap(im))
            tmp[c, 16 * pair + 8 : 16 * pair + 16, :] = jnp.where(half, swap(re), im)
    mass = mass_ref[...]
    coef[0] = -mass * metric_ref[0]
    coef[1] = -mass * metric_ref[2]
    coef[2] = -mass * metric_ref[1]
    coef[3] = -mass * metric_ref[3]
    base = pl.program_id(0) * 8
    for kl in range(8):
        cells = []
        for c in range(3):
            block = tmp[c, pl.ds(kl, 128, stride=8), :].T
            non_ref[c, :, kl] = block.reshape(2, 64, 128)
            cells.append(block)
        x_r, x_s = slopes_of(jnp.concatenate([cells[0][:64], cells[0][64:]], axis=1), fwd_ref[...])
        y_r, y_s = slopes_of(jnp.concatenate([cells[1][:64], cells[1][64:]], axis=1), fwd_ref[...])
        scaled = wave_of(ids_ref, base + kl) * mass_ref[...]
        for part in range(2):
            cols = slice(128 * part, 128 * part + 128)
            value = (
                coef[0] * x_r[:, cols]
                + coef[1] * x_s[:, cols]
                + coef[2] * y_r[:, cols]
                + coef[3] * y_s[:, cols]
            )
            if part == 0:
                value = value + scaled * cells[2][64:]
            else:
                value = value - scaled * cells[2][:64]
            raw_ref[part, kl] = value
            edge_ref[0, part, kl] = raw_ref[part, kl, pl.ds(0, 8, stride=8), :]
            edge_ref[1, part, kl] = raw_ref[part, kl, pl.ds(7, 8, stride=8), :]


def from_blocks(ids, blocks, metric, mass, forward):
    return pl.pallas_call(
        post_kernel,
        grid=(2,),
        in_specs=[
            in_smem(),
            pl.BlockSpec((16, 3, 2, 8, 512), lambda i: (0, 0, 0, i, 0)),
            whole_spec(metric.shape),
            whole_spec(mass.shape),
            whole_spec(forward.shape),
        ],
        out_specs=[
            pl.BlockSpec((3, 2, 8, 64, 128), lambda i: (0, 0, i, 0, 0)),
            pl.BlockSpec((2, 8, 64, 128), lambda i: (0, i, 0, 0)),
            pl.BlockSpec((2, 2, 8, 8, 128), lambda i: (0, 0, i, 0, 0)),
        ],
        out_shape=[
            jax.ShapeDtypeStruct((3, 2, 16, 64, 128), F32),
            jax.ShapeDtypeStruct(FIELD, F32),
            jax.ShapeDtypeStruct(EDGE, F32),
        ],
        scratch_shapes=[pltpu.VMEM((3, 1024, 128), F32), pltpu.VMEM((4, 64, 128), F32)],
        compiler_params=pltpu.CompilerParams(vmem_limit_bytes=NARROW),
        name="from_blocks",
    )(ids, blocks, metric, mass, forward)


def lanes(value, index):
    return jnp.take_along_axis(value, index, axis=1, mode="promise_in_bounds")


def links_of(ids_ref, near_ref):
    device = ids_ref[0]
    links = []
    for side in range(4):
        ident = jnp.broadcast_to(near_ref[side : side + 1, :], (8, 128))
        here = ident >= 0
        if side < 2:
            place = ident - (device - 1) * 128
            links.append((jnp.where(here, place & 127, 0), jnp.where(here, place >> 7, 3)))
        else:
            links.append((jnp.where(here, ident - device * 128, 0), here))
    return links


def share(out_ref, field_ref, west_ref, east_ref, links, part, kl):
    (west_lane, west_from), (east_lane, east_from), (south_lane, south_here), (north_lane, north_here) = links
    first = field_ref[part, kl, pl.ds(0, 8, stride=8), :]
    last = field_ref[part, kl, pl.ds(7, 8, stride=8), :]

    def pick(side, own, lane, origin):
        value = jnp.where(origin == 1, lanes(own, lane), 0.0)
        value = jnp.where(origin == 0, lanes(west_ref[side, part, kl], lane), value)
        return jnp.where(origin == 2, lanes(east_ref[side, part, kl], lane), value)

    out_ref[part, kl] = field_ref[part, kl]
    out_ref[part, kl, pl.ds(0, 8, stride=8), :] = first + pick(1, last, west_lane, west_from)
    out_ref[part, kl, pl.ds(7, 8, stride=8), :] = last + pick(0, first, east_lane, east_from)
    bottom = out_ref[part, kl, 0:8, :]
    top = out_ref[part, kl, 56:64, :]
    out_ref[part, kl, 0:8, :] = bottom + jnp.where(south_here, lanes(top, south_lane), 0.0)
    out_ref[part, kl, 56:64, :] = top + jnp.where(north_here, lanes(bottom, north_lane), 0.0)


def set_stiff(stiff, metric_ref, mass_ref):
    mass = mass_ref[...]
    rx, ry, sx, sy = metric_ref[0], metric_ref[1], metric_ref[2], metric_ref[3]
    stiff[0] = mass * (rx * rx + ry * ry)
    stiff[1] = mass * (rx * sx + ry * sy)
    stiff[2] = mass * (sx * sx + sy * sy)


def set_inverse(inverse, near_ref):
    node = lax.broadcasted_iota(jnp.int32, (64, 128), 0)
    here = [near_ref[side : side + 1, :] >= 0 for side in range(4)]
    places = [(node & 7) == 0, (node & 7) == 7, node < 8, node >= 56]
    value = jnp.ones((64, 128), F32)
    for place, there in zip(places, here):
        value = jnp.where(place & there, 0.5 * value, value)
    inverse[...] = value


def stiffness(pair, shift, stiff, mass_ref, fwd_ref, adj_ref, adl_ref):
    along_r, along_s = slopes_of(pair, fwd_ref[...])
    cross = twice(stiff[1])
    back = jnp.concatenate(
        [
            twice(stiff[0]) * along_r + cross * along_s,
            cross * along_r + twice(stiff[2]) * along_s,
        ],
        axis=0,
    )
    up, down = split(back)
    folded = dot(adj_ref[...], jnp.concatenate([up, down], axis=0)) + dot(adl_ref[...], up)
    return folded + shift * twice(mass_ref[...]) * pair


def image_kernel(
    ids_ref, raw_ref, west_ref, east_ref, near_ref, metric_ref, mass_ref, fwd_ref, adj_ref, adl_ref,
    field_ref, image_ref, edge_ref, stiff,
):
    links = links_of(ids_ref, near_ref)
    set_stiff(stiff, metric_ref, mass_ref)
    for kl in range(16):
        for part in range(2):
            share(field_ref, raw_ref, west_ref, east_ref, links, part, kl)
    for kl in range(16):
        pair = jnp.concatenate([field_ref[0, kl], field_ref[1, kl]], axis=1)
        wave = wave_of(ids_ref, kl)
        image = stiffness(pair, wave * wave + 1.0, stiff, mass_ref, fwd_ref, adj_ref, adl_ref)
        for part in range(2):
            image_ref[part, kl] = image[:, 128 * part : 128 * part + 128]
            edge_ref[0, part, kl] = image_ref[part, kl, pl.ds(0, 8, stride=8), :]
            edge_ref[1, part, kl] = image_ref[part, kl, pl.ds(7, 8, stride=8), :]


def image_of(ids, raw, west, east, near, metric, mass, left):
    return pl.pallas_call(
        image_kernel,
        in_specs=[in_smem()] + [pl.BlockSpec(memory_space=pltpu.VMEM)] * 9,
        out_shape=[
            jax.ShapeDtypeStruct(FIELD, F32),
            jax.ShapeDtypeStruct(FIELD, F32),
            jax.ShapeDtypeStruct(EDGE, F32),
        ],
        scratch_shapes=[pltpu.VMEM((3, 64, 128), F32)],
        compiler_params=pltpu.CompilerParams(vmem_limit_bytes=NARROW),
        name="image",
    )(ids, raw, west, east, near, metric, mass, *left)


def folded_rows(value):
    return jnp.sum(value[0] + value[1], axis=0, keepdims=True)


def moments_kernel(
    ids_ref, image_ref, west_ref, east_ref, field_ref, near_ref, metric_ref, mass_ref, fwd_ref, adj_ref,
    adl_ref, shared_ref, sum_ref, stiff, inverse, second, rows, local,
):
    links = links_of(ids_ref, near_ref)
    set_stiff(stiff, metric_ref, mass_ref)
    set_inverse(inverse, near_ref)
    for kl in range(16):
        for part in range(2):
            share(shared_ref, image_ref, west_ref, east_ref, links, part, kl)
    for kl in range(16):
        pair = jnp.concatenate([shared_ref[0, kl], shared_ref[1, kl]], axis=1)
        wave = wave_of(ids_ref, kl)
        image = stiffness(pair, wave * wave + 1.0, stiff, mass_ref, fwd_ref, adj_ref, adl_ref)
        for part in range(2):
            second[part, kl] = image[:, 128 * part : 128 * part + 128]
        weighed = shared_ref[:, kl] * inverse[...]
        rows[0, kl : kl + 1, :] = folded_rows(weighed * field_ref[:, kl])
        rows[1, kl : kl + 1, :] = folded_rows(weighed * shared_ref[:, kl])
    cross = jnp.sum(rows[0], axis=1, keepdims=True)
    square = jnp.sum(rows[1], axis=1, keepdims=True)
    guess = jnp.where(square > 0.0, cross / jnp.where(square > 0.0, square, 1.0), 0.0)
    local[...] = jnp.broadcast_to(guess, (16, 128))
    for kl in range(16):
        step = local[kl : kl + 1, :]
        one = shared_ref[:, kl]
        two = second[:, kl]
        left = field_ref[:, kl] - step * one
        image = image_ref[:, kl] - step * two
        weighed = left * inverse[...]
        rows[0, kl : kl + 1, :] = folded_rows(left * weighed)
        rows[2, kl : kl + 1, :] = folded_rows(one * weighed)
        rows[3, kl : kl + 1, :] = folded_rows(left * image)
        rows[4, kl : kl + 1, :] = folded_rows(left * two + one * image)
        rows[5, kl : kl + 1, :] = folded_rows(one * two)
    place = lax.broadcasted_iota(jnp.int32, (16, 128), 1)
    packed = local[...]
    for q, row in enumerate((0, 2, 1, 3, 4, 5)):
        packed = jnp.where(place == q + 1, jnp.sum(rows[row], axis=1, keepdims=True), packed)
    for d in range(8):
        sum_ref[d] = packed


def moments_of(ids, image, west, east, field, near, metric, mass, left):
    return pl.pallas_call(
        moments_kernel,
        in_specs=[in_smem()] + [pl.BlockSpec(memory_space=pltpu.VMEM)] * 10,
        out_shape=[jax.ShapeDtypeStruct(FIELD, F32), jax.ShapeDtypeStruct((8, 16, 128), F32)],
        scratch_shapes=[
            pltpu.VMEM((3, 64, 128), F32),
            pltpu.VMEM((64, 128), F32),
            pltpu.VMEM(FIELD, F32),
            pltpu.VMEM((6, 16, 128), F32),
            pltpu.VMEM((16, 128), F32),
        ],
        compiler_params=pltpu.CompilerParams(vmem_limit_bytes=NARROW),
        name="moments",
    )(ids, image, west, east, field, near, metric, mass, *left)


def final_kernel(field_ref, shared_ref, sum_ref, out_ref, scales):
    packed = sum_ref[...]
    place = lax.broadcasted_iota(jnp.int32, packed.shape, 2)
    guess, left2, cross, square, energy, mixed, second = [
        jnp.broadcast_to(
            jnp.sum(jnp.where(place == q, packed, 0.0), axis=2, keepdims=True), packed.shape
        )
        for q in range(7)
    ]
    norm0 = jnp.sum(left2 + guess * (2.0 * cross + guess * square), axis=0)
    energy0 = jnp.sum(cross + guess * square, axis=0)
    alpha0 = norm0 / energy0
    off = guess - alpha0[None]
    norm1 = jnp.sum(left2 + off * (2.0 * cross + off * square), axis=0)
    energy1 = jnp.sum(energy + off * (mixed + off * second), axis=0)
    beta = norm1 / norm0
    alpha1 = norm1 / (energy1 - beta * norm1 / alpha0)
    scales[0] = alpha0 + alpha1 * (1.0 + beta)
    scales[1] = -alpha1 * alpha0
    for kl in range(16):
        one = scales[0, kl : kl + 1, :]
        two = scales[1, kl : kl + 1, :]
        out_ref[:, kl] = one * field_ref[:, kl] + two * shared_ref[:, kl]


def final(field, shared, sums):
    return pl.pallas_call(
        final_kernel,
        out_shape=jax.ShapeDtypeStruct(FIELD, F32),
        scratch_shapes=[pltpu.VMEM((2, 16, 128), F32)],
        compiler_params=pltpu.CompilerParams(vmem_limit_bytes=NARROW),
        name="pressure",
    )(field, shared, sums)


def swap_edges(edges):
    count = lax.axis_size("elem")
    west = lax.ppermute(edges, "elem", [(i, i + 1) for i in range(count - 1)])
    east = lax.ppermute(edges, "elem", [(i + 1, i) for i in range(count - 1)])
    return west, east


def over(array, axis):
    return lax.all_to_all(array, axis, split_axis=0, concat_axis=0, tiled=True)


def per_device(velocity, metric, mass, sponge_rate, sponge_mask, neighbours):
    place = lax.axis_index("mode")
    ids = jnp.stack([lax.axis_index("elem"), place]).astype(jnp.int32)
    damping = sponge_mask.astype(F32)[None, :] * sponge_rate
    rows = jnp.concatenate([metric, damping[None], jnp.zeros((3, 64, 128), F32)], axis=0)
    rows = lax.dynamic_slice_in_dim(rows, place * 8, 8, axis=2)
    rows = rows.transpose(0, 2, 1).reshape(8, 512)
    left = [jnp.asarray(t) for t in left_tables()]

    blocks = over(to_blocks(velocity), "mode")
    blocks = over(in_planes(blocks, rows), "mode")
    nonlinear, raw, edges = from_blocks(ids, blocks, metric, mass, left[0])
    west, east = swap_edges(edges)
    field, image, edges = image_of(ids, raw, west, east, neighbours, metric, mass, left)
    west, east = swap_edges(edges)
    shared, sums = moments_of(ids, image, west, east, field, neighbours, metric, mass, left)
    return nonlinear, final(field, shared, over(sums, "elem"))


def solution(mesh):
    return jax.shard_map(
        per_device,
        mesh=mesh,
        in_specs=(
            P(None, None, "mode", None, "elem"),
            P(None, None, "elem"),
            P(None, "elem"),
            P(None, "elem"),
            P("elem"),
            P(None, "elem"),
        ),
        out_specs=(P(None, None, "mode", None, "elem"), P(None, "mode", None, "elem")),
        check_vma=False,
    )
```

time: 197 us -> 167 us (0.85)
  Pallas kernels: 51.3 us -> 32.2 us
  local copies, waits for them, and re-layouts: 7.86 us -> 0.34 us
  blocking collectives: 10.7 us -> 15.2 us
  starting transfers between devices: 28.6 us -> 24.4 us
  waiting for transfers between devices: 95.5 us -> 93.1 us
    pallas_call x4 -> x3, Pallas kernels: 25.3 us -> 11.1 us  [the longest x1 4.13 us: moments_of(): pl.pallas_call(moments_kernel, in_specs=[in_smem()] + [pl.BlockSpec(memor...]
    unnamed x56 -> x30, local copies, waits for them, and re-layouts: 6.82 us -> 0.08 us
    all_to_all x3 -> x2, starting transfers between devices: 18 us -> 12.8 us  [over(): return lax.all_to_all(array, axis, split_axis=0, concat_axis=0, tiled=True)]
    pallas_call x1, Pallas kernels: 19.4 us -> 14.5 us  [in_planes(): pl.pallas_call(plane_kernel, grid=(2,), in_specs=[block, pl.BlockSpec((8,...]
    all_to_all x1, blocking collectives: 10.7 us -> 15.2 us  [over(): return lax.all_to_all(array, axis, split_axis=0, concat_axis=0, tiled=True)]
    ppermute x2, waiting for transfers between devices: 3.77 us -> 0.01 us  [swap_edges(): east = lax.ppermute(edges, 'elem', [(i + 1, i) for i in range(count - 1)])]
    ppermute x2, waiting for transfers between devices: 0.01 us -> 2.06 us  [swap_edges(): west = lax.ppermute(edges, 'elem', [(i, i + 1) for i in range(count - 1)])]
    all_to_all x3 -> x2, waiting for transfers between devices: 91.7 us -> 91 us  [over(): return lax.all_to_all(array, axis, split_axis=0, concat_axis=0, tiled=True)]
  transfers between devices with their start and end apart: 7 -> 6, of which waited for: 3 -> 4; matrix products, arithmetic and copies ran while one was open for 1% -> 0% of each run, Pallas kernels for 4% -> 0%
where the time goes in v2:
time: 167 us; the launch traced here: 166 us
  waiting for transfers between devices  93.1 us (56%)
  Pallas kernels  32.2 us (19%)
  starting transfers between devices  24.4 us (15%)
  blocking collectives  15.2 us (9%)
    all_to_all x2, waiting for transfers between devices, over(): return lax.all_to_all(array, axis, split_axis=0, concat_axis=0, tiled=True)  91 us
    all_to_all x1, blocking collectives, over(): return lax.all_to_all(array, axis, split_axis=0, concat_axis=0, tiled=True)  15.2 us
    pallas_call x1, Pallas kernels, in_planes(): pl.pallas_call(plane_kernel, grid=(2,), in_specs=[block, pl.BlockSpec((8,...  14.5 us
    all_to_all x2, starting transfers between devices, over(): return lax.all_to_all(array, axis, split_axis=0, concat_axis=0, tiled=True)  12.8 us
    ppermute x2, starting transfers between devices, swap_edges(): west = lax.ppermute(edges, 'elem', [(i, i + 1) for i in range(count - 1)])  9.03 us
    pallas_call x1, Pallas kernels, to_blocks(): pl.pallas_call(pre_kernel, grid=(3,), in_specs=[pl.BlockSpec((1, 2, 16, 6...  5.25 us
    pallas_call x1, Pallas kernels, moments_of(): pl.pallas_call(moments_kernel, in_specs=[in_smem()] + [pl.BlockSpec(memor...  4.13 us
    pallas_call x1, Pallas kernels, from_blocks(): pl.pallas_call(post_kernel, grid=(2,), in_specs=[in_smem(), pl.BlockSpec(...  4.05 us
  transfers between devices with their start and end apart: 6, of which 4 were waited for; matrix products, arithmetic and copies ran while one was open for 0% of the time, Pallas kernels for 0%

profile of v2, /device:TPU:0, one launch (start us, length us, event | category | flops | bytes accessed | tf_op | source)
XLA Modules:
  0.0 166.3 jit_solution(9847983215600582963)
XLA Ops:
  0.6 5.3 %to_blocks.1 = f32[16,3,2,16,512]{4,3,2,1,0:T(8,128)} custom-call(f32[3,2,16,64,128]{4,3,2,1,0:T(8,128)} %v_ref.1), custom_call_target="tpu_custom_call" | custom-call | tf_op jit(solution)/shard_map/to_blocks/pallas_call | solution.py:109
  5.9 0.0 copy-start.14
  5.9 0.0 copy-start.13
  5.9 0.0 copy-start
  5.9 0.0 copy-start.2
  5.9 0.0 copy-start.3
  5.9 0.0 copy-start.4
  5.9 0.0 copy-start.5
  5.9 0.0 copy-start.7
  5.9 0.0 copy-start.8
  6.0 0.0 copy-start.9
  6.0 8.3 %all-to-all-start = ((f32[16,3,2,16,512]{4,3,2,1,0:T(8,128)}), f32[16,3,2,16,512]{4,3,2,1,0:T(8,128)}, u32[]{:S(2)}, u32[]{:S(2)}) async-start(f32[16,3,2,16,512]{4,3,2,1,0:T(8,128)} %to_blocks.1), calls=%async_computation | async-start | bytes 6291456 | tf_op jit(solution)/shard_map/all_to_all | solution.py:569
  14.3 0.0 copy-done.14
  14.3 0.1 pad.2.clone
  14.4 0.0 copy-done.13
  14.4 0.0 copy-done
  14.4 0.1 fusion.1
  14.6 0.1 copy.18
  14.7 0.1 reshape.8.rows_ref
  14.7 47.1 %all-to-all-done.z_ref = f32[16,3,2,16,512]{4,3,2,1,0:T(8,128)} async-done(((f32[16,3,2,16,512]{4,3,2,1,0:T(8,128)}), f32[16,3,2,16,512]{4,3,2,1,0:T(8,128)}, u32[]{:S(2)}, u32[]{:S(2)}) %all-to-all-start) | async-done | bytes 3145760 | tf_op jit(solution)/shard_map/all_to_all | solution.py:569
  61.8 0.0 copy-done.2
  61.9 0.0 copy-done.3
  61.9 0.0 copy-done.4
  61.9 0.0 copy-done.5
  61.9 0.0 copy-done.7
  61.9 0.0 copy-done.8
  61.9 0.0 copy-done.9
  61.9 14.5 %in_planes.1 = f32[16,3,2,16,512]{4,3,2,1,0:T(8,128)} custom-call(f32[16,3,2,16,512]{4,3,2,1,0:T(8,128)} %all-to-all-done.z_ref, f32[8,512]{1,0:T(8,128)S(1)} %reshape.8.rows_ref, f32[256,128]{1,0:T(8,128)S(1)} %copy-done.9, f32[256,128]{1,0:T(8,128)S(1)} %copy-done.8, bf16[384,256]{1,0:T(8,128)(2,1)S(1)} %copy-done.7, bf16[272,768]{1,0:T(8,128)(2,1)S(1)} %copy-done.2, ...), custom_call_target="tpu_custom_call" | custom-call | tf_op jit(solution)/shard_map/in_planes/pallas_call | solution.py:244
  76.4 0.0 copy-start.1
  76.4 0.0 copy-start.6
  76.4 4.5 %all-to-all-start.1 = ((f32[16,3,2,16,512]{4,3,2,1,0:T(8,128)}), f32[16,3,2,16,512]{4,3,2,1,0:T(8,128)S(1)}, u32[]{:S(2)}, u32[]{:S(2)}) async-start(f32[16,3,2,16,512]{4,3,2,1,0:T(8,128)} %in_planes.1), calls=%async_computation.1 | async-start | bytes 6291456 | tf_op jit(solution)/shard_map/all_to_all | solution.py:569
  81.0 0.0 copy-start.10
  81.0 0.0 copy-start.11
  81.0 0.0 copy-start.12
  81.0 0.1 pad_add_fusion.ids_ref
  81.1 43.9 %all-to-all-done.1.r_ref = f32[16,3,2,16,512]{4,3,2,1,0:T(8,128)S(1)} async-done(((f32[16,3,2,16,512]{4,3,2,1,0:T(8,128)}), f32[16,3,2,16,512]{4,3,2,1,0:T(8,128)S(1)}, u32[]{:S(2)}, u32[]{:S(2)}) %all-to-all-start.1) | async-done | bytes 3145760 | tf_op jit(solution)/shard_map/all_to_all | solution.py:569
  125.0 0.0 copy-done.1
  125.0 0.0 copy-done.6
  125.0 4.0 %from_blocks.1 = (f32[3,2,16,64,128]{4,3,2,1,0:T(8,128)}, f32[2,16,64,128]{3,2,1,0:T(8,128)S(1)}, f32[2,2,16,8,128]{4,3,2,1,0:T(8,128)S(1)}) custom-call(s32[2]{0:T(128)S(1)} %pad_add_fusion.ids_ref, f32[16,3,2,16,512]{4,3,2,1,0:T(8,128)S(1)} %all-to-all-done.1.r_ref, f32[4,64,128]{2,1,0:T(8,128)S(1)} %copy-done, f32[64,128]{1,0:T(8,128)S(1)} %copy-done.6, ...), custom_call_target="tpu_custom_call" | custom-call | tf_op jit(solution)/shard_map/from_blocks/pallas_call | solution.py:332
  129.0 1.3 collective-permute-start.1
  130.3 3.0 %collective-permute-start = (f32[2,2,16,8,128]{4,3,2,1,0:T(8,128)S(1)}, f32[2,2,16,8,128]{4,3,2,1,0:T(8,128)S(1)}, u32[]{:S(2)}, u32[]{:S(2)}) collective-permute-start(f32[2,2,16,8,128]{4,3,2,1,0:T(8,128)S(1)} %get-tuple-element.12), channel_id=1, source_target_pairs={{0,16},{16,32},{32,48},{48,64},{64,80},{80,96},{96,112},{1,17},{17... | collective-permute-start | bytes 786440 | tf_op jit(solution)/shard_map/ppermute | solution.py:563
  133.4 0.0 collective-permute-done.1.east_ref
  133.4 1.1 collective-permute-done.west_ref
  134.5 0.0 copy-done.10
  134.5 0.0 copy-done.11
  134.5 0.0 copy-done.12
  134.5 2.9 %image.1 = (f32[2,16,64,128]{3,2,1,0:T(8,128)S(1)}, f32[2,16,64,128]{3,2,1,0:T(8,128)S(1)}, f32[2,2,16,8,128]{4,3,2,1,0:T(8,128)S(1)}) custom-call(s32[2]{0:T(128)S(1)} %pad_add_fusion.ids_ref, f32[2,16,64,128]{3,2,1,0:T(8,128)S(1)} %get-tuple-element.11.raw_ref, f32[2,2,16,8,128]{4,3,2,1,0:T(8,128)S(1)} %collective-permute-done.west_ref, ...), custom_call_target="tpu_custom_call" | custom-call | tf_op jit(solution)/shard_map/image/pallas_call | solution.py:448
  137.5 1.3 collective-permute-start.3
  138.8 6.0 %collective-permute-start.2 = (f32[2,2,16,8,128]{4,3,2,1,0:T(8,128)S(1)}, f32[2,2,16,8,128]{4,3,2,1,0:T(8,128)S(1)}, u32[]{:S(2)}, u32[]{:S(2)}) collective-permute-start(f32[2,2,16,8,128]{4,3,2,1,0:T(8,128)S(1)} %get-tuple-element.15), channel_id=1, source_target_pairs={{0,16},{16,32},{32,48},{48,64},{64,80},{80,96},{96,112},{1,17},{17... | collective-permute-start | bytes 786440 | tf_op jit(solution)/shard_map/ppermute | solution.py:563
  144.8 0.0 collective-permute-done.3.east_ref
  144.8 0.9 collective-permute-done.2.west_ref
  145.7 4.1 %moments.1 = (f32[2,16,64,128]{3,2,1,0:T(8,128)S(1)}, f32[8,16,128]{2,1,0:T(8,128)S(1)}) custom-call(s32[2]{0:T(128)S(1)} %pad_add_fusion.ids_ref, f32[2,16,64,128]{3,2,1,0:T(8,128)S(1)} %get-tuple-element.14.image_ref, f32[2,2,16,8,128]{4,3,2,1,0:T(8,128)S(1)} %collective-permute-done.2.west_ref, f32[2,2,16,8,128]{4,3,2,1,0:T(8,128)S(1)} %collective-permute-done.3.east_ref, ...), custom_call_target="tpu_custom_call" | custom-call | tf_op jit(solution)/shard_map/moments/pallas_call | solution.py:510
  149.8 15.2 %all_to_all.15.sum_ref = f32[8,16,128]{2,1,0:T(8,128)S(1)} all-to-all(f32[8,16,128]{2,1,0:T(8,128)S(1)} %get-tuple-element.17), channel_id=1, replica_groups=mesh['elem'=8,'mode'=16] {'elem'}, dimensions={0} | all-to-all | bytes 131072 | tf_op jit(solution)/shard_map/all_to_all | solution.py:569
  165.0 1.3 pressure.1
  (3 shorter events, 0.0 us)
Async XLA Ops:
  5.9 8.4 %copy-start.14 = (s32[128]{0:T(128)S(1)}, s32[128]{0:T(128)}, u32[]{:S(2)}) copy-start(s32[128]{0:T(128)} %param.20) | copy-start | bytes 1540
  5.9 8.5 %copy-start.13 = (f32[64,128]{1,0:T(8,128)S(1)}, f32[64,128]{1,0:T(8,128)}, u32[]{:S(2)}) copy-start(f32[64,128]{1,0:T(8,128)} %param.19) | copy-start | bytes 98308
  5.9 8.5 %copy-start = (f32[4,64,128]{2,1,0:T(8,128)S(1)}, f32[4,64,128]{2,1,0:T(8,128)}, u32[]{:S(2)}) copy-start(f32[4,64,128]{2,1,0:T(8,128)} %metric_ref.5) | copy-start | bytes 393220
  5.9 56.0 %copy-start.2 = (bf16[272,768]{1,0:T(8,128)(2,1)S(1)}, bf16[272,768]{1,0:T(8,128)(2,1)}, u32[]{:S(2)}) copy-start(bf16[272,768]{1,0:T(8,128)(2,1)} %constant.43.clone.cos_ref) | copy-start | bytes 1253380
  5.9 56.0 %copy-start.3 = (bf16[256,768]{1,0:T(8,128)(2,1)S(1)}, bf16[256,768]{1,0:T(8,128)(2,1)}, u32[]{:S(2)}) copy-start(bf16[256,768]{1,0:T(8,128)(2,1)} %constant.46.clone.back_sin_ref) | copy-start | bytes 1179652
  5.9 56.0 %copy-start.4 = (bf16[256,768]{1,0:T(8,128)(2,1)S(1)}, bf16[256,768]{1,0:T(8,128)(2,1)}, u32[]{:S(2)}) copy-start(bf16[256,768]{1,0:T(8,128)(2,1)} %constant.45.clone.back_cos_ref) | copy-start | bytes 1179652
  5.9 55.9 %copy-start.5 = (bf16[256,768]{1,0:T(8,128)(2,1)S(1)}, bf16[256,768]{1,0:T(8,128)(2,1)}, u32[]{:S(2)}) copy-start(bf16[256,768]{1,0:T(8,128)(2,1)} %constant.44.clone.sin_ref) | copy-start | bytes 1179652
  5.9 55.9 %copy-start.7 = (bf16[384,256]{1,0:T(8,128)(2,1)S(1)}, bf16[384,256]{1,0:T(8,128)(2,1)}, u32[]{:S(2)}) copy-start(bf16[384,256]{1,0:T(8,128)(2,1)} %constant.42.clone.slope_ref) | copy-start | bytes 589828
  5.9 55.9 %copy-start.8 = (f32[256,128]{1,0:T(8,128)S(1)}, f32[256,128]{1,0:T(8,128)}, u32[]{:S(2)}) copy-start(f32[256,128]{1,0:T(8,128)} %constant.41.clone.sign_ref) | copy-start | bytes 393220
  6.0 55.9 %copy-start.9 = (f32[256,128]{1,0:T(8,128)S(1)}, f32[256,128]{1,0:T(8,128)}, u32[]{:S(2)}) copy-start(f32[256,128]{1,0:T(8,128)} %constant.40.clone.wave_ref) | copy-start | bytes 393220
  6.0 55.9 %all-to-all-start = ((f32[16,3,2,16,512]{4,3,2,1,0:T(8,128)}), f32[16,3,2,16,512]{4,3,2,1,0:T(8,128)}, u32[]{:S(2)}, u32[]{:S(2)}) async-start(f32[16,3,2,16,512]{4,3,2,1,0:T(8,128)} %to_blocks.1), calls=%async_computation | async-start | bytes 6291456 | tf_op jit(solution)/shard_map/all_to_all | solution.py:569
  76.4 48.6 %copy-start.1 = (bf16[128,192]{1,0:T(8,128)(2,1)S(1)}, bf16[128,192]{1,0:T(8,128)(2,1)}, u32[]{:S(2)}) copy-start(bf16[128,192]{1,0:T(8,128)(2,1)} %constant.37.clone.fwd_ref) | copy-start | bytes 147460
  76.4 48.6 %copy-start.6 = (f32[64,128]{1,0:T(8,128)S(1)}, f32[64,128]{1,0:T(8,128)}, u32[]{:S(2)}) copy-start(f32[64,128]{1,0:T(8,128)} %mass_ref.5) | copy-start | bytes 98308
  76.4 48.5 %all-to-all-start.1 = ((f32[16,3,2,16,512]{4,3,2,1,0:T(8,128)}), f32[16,3,2,16,512]{4,3,2,1,0:T(8,128)S(1)}, u32[]{:S(2)}, u32[]{:S(2)}) async-start(f32[16,3,2,16,512]{4,3,2,1,0:T(8,128)} %in_planes.1), calls=%async_computation.1 | async-start | bytes 6291456 | tf_op jit(solution)/shard_map/all_to_all | solution.py:569
  81.0 53.6 %copy-start.10 = (bf16[64,256]{1,0:T(8,128)(2,1)S(1)}, bf16[64,256]{1,0:T(8,128)(2,1)}, u32[]{:S(2)}) copy-start(bf16[64,256]{1,0:T(8,128)(2,1)} %constant.38.clone.adj_ref) | copy-start | bytes 98308
  81.0 53.5 %copy-start.11 = (bf16[64,128]{1,0:T(8,128)(2,1)S(1)}, bf16[64,128]{1,0:T(8,128)(2,1)}, u32[]{:S(2)}) copy-start(bf16[64,128]{1,0:T(8,128)(2,1)} %constant.39.clone.adl_ref) | copy-start | bytes 49156
  81.0 53.5 %copy-start.12 = (s32[4,128]{1,0:T(4,128)S(1)}, s32[4,128]{1,0:T(4,128)}, u32[]{:S(2)}) copy-start(s32[4,128]{1,0:T(4,128)} %near_ref.3) | copy-start | bytes 6148
  129.0 4.3 %collective-permute-start.1 = (f32[2,2,16,8,128]{4,3,2,1,0:T(8,128)S(1)}, f32[2,2,16,8,128]{4,3,2,1,0:T(8,128)S(1)}, u32[]{:S(2)}, u32[]{:S(2)}) collective-permute-start(f32[2,2,16,8,128]{4,3,2,1,0:T(8,128)S(1)} %get-tuple-element.12), channel_id=1, source_target_pairs={{16,0},{32,16},{48,32},{64,48},{80,64},{96,80},{112,96},{17,1},{33... | collective-permute-start | bytes 786440 | tf_op jit(solution)/shard_map/ppermute | solution.py:564
  130.3 4.2 %collective-permute-start = (f32[2,2,16,8,128]{4,3,2,1,0:T(8,128)S(1)}, f32[2,2,16,8,128]{4,3,2,1,0:T(8,128)S(1)}, u32[]{:S(2)}, u32[]{:S(2)}) collective-permute-start(f32[2,2,16,8,128]{4,3,2,1,0:T(8,128)S(1)} %get-tuple-element.12), channel_id=1, source_target_pairs={{0,16},{16,32},{32,48},{48,64},{64,80},{80,96},{96,112},{1,17},{17... | collective-permute-start | bytes 786440 | tf_op jit(solution)/shard_map/ppermute | solution.py:563
  137.5 7.3 %collective-permute-start.3 = (f32[2,2,16,8,128]{4,3,2,1,0:T(8,128)S(1)}, f32[2,2,16,8,128]{4,3,2,1,0:T(8,128)S(1)}, u32[]{:S(2)}, u32[]{:S(2)}) collective-permute-start(f32[2,2,16,8,128]{4,3,2,1,0:T(8,128)S(1)} %get-tuple-element.15), channel_id=1, source_target_pairs={{16,0},{32,16},{48,32},{64,48},{80,64},{96,80},{112,96},{17,1},{33... | collective-permute-start | bytes 786440 | tf_op jit(solution)/shard_map/ppermute | solution.py:564
  138.8 6.9 %collective-permute-start.2 = (f32[2,2,16,8,128]{4,3,2,1,0:T(8,128)S(1)}, f32[2,2,16,8,128]{4,3,2,1,0:T(8,128)S(1)}, u32[]{:S(2)}, u32[]{:S(2)}) collective-permute-start(f32[2,2,16,8,128]{4,3,2,1,0:T(8,128)S(1)} %get-tuple-element.15), channel_id=1, source_target_pairs={{0,16},{16,32},{32,48},{48,64},{64,80},{80,96},{96,112},{1,17},{17... | collective-permute-start | bytes 786440 | tf_op jit(solution)/shard_map/ppermute | solution.py:563

commit v3 on v2

--- a/solution.py
+++ b/solution.py
@@ -121,50 +121,61 @@
 ROWS = 32
 
 
+def node_rows(rows, tmp, metric_ref, rate_ref, mask_ref):
+    place = pl.multiple_of(lax.axis_index("mode") * 8, 8)
+    damping = mask_ref[...].astype(F32) * rate_ref[...]
+    blank = jnp.zeros((64, 128), F32)
+    for q, value in enumerate([metric_ref[0], metric_ref[1], metric_ref[2], metric_ref[3], damping]):
+        tmp[q] = jnp.concatenate([value, blank], axis=0).T
+    for q in range(5):
+        mine = tmp[q, pl.ds(place, 8), :]
+        other = swap(mine)
+        for i in range(4):
+            row = mine[2 * i : 2 * i + 1, :] + other[2 * i + 1 : 2 * i + 2, :]
+            rows[i // 2, q : q + 1, 128 * (i % 2) : 128 * (i % 2) + 128] = row
+
+
 def plane_kernel(
-    z_ref, rows_ref, wave_ref, sign_ref, slope_ref, cos_ref, sin_ref, back_cos_ref, back_sin_ref, out_ref, high, low, planes, eh, el, tail,
+    z_ref, metric_ref, rate_ref, mask_ref, wave_ref, sign_ref, slope_ref, cos_ref, sin_ref,
+    back_cos_ref, back_sin_ref, out_ref, high, low, planes, eh, el, tail, grads, rows_all, turned,
 ):
-    rx = rows_ref[0:1, :]
-    ry = rows_ref[1:2, :]
-    sx = rows_ref[2:3, :]
-    sy = rows_ref[3:4, :]
-    damping = rows_ref[4:5, :]
+    @pl.when(pl.program_id(0) == 0)
+    def _():
+        node_rows(rows_all, turned, metric_ref, rate_ref, mask_ref)
+
+    node = rows_all[pl.program_id(0)]
+    rx = node[0:1, :]
+    ry = node[1:2, :]
+    sx = node[2:3, :]
+    sy = node[3:4, :]
+    damping = node[4:5, :]
     count = ROWS // 16
+
+    for c in range(3):
+        for part in range(2):
+            up, down = split(z_ref[:, c, part].reshape(256, 256))
+            high[c, part] = up
+            low[c, part] = down
+            for q in range(2):
+                cols = slice(128 * q, 128 * q + 128)
+                three = jnp.concatenate([up[:, cols], down[:, cols], up[:, cols]], axis=1)
+                both = dot(three, slope_ref[...])
+                grads[c, part, 0, :, cols] = both[:, :128]
+                grads[c, part, 1, :, cols] = both[:, 128:]
 
     def curls(step, carry):
         rows = pl.ds(pl.multiple_of(step * ROWS, ROWS), ROWS)
         wave = jnp.concatenate([wave_ref[rows, :]] * 2, axis=1)
-        fields = {}
-        slopes = {}
-        for c in range(3):
-            for part in range(2):
-                value = z_ref[pl.ds(step * count, count), c, part].reshape(ROWS, 256)
-                up, down = split(value)
-                high[c, part, rows, :] = up
-                low[c, part, rows, :] = down
-                fields[c, part] = value
-                pieces = []
-                for q in range(2):
-                    cols = slice(128 * q, 128 * q + 128)
-                    three = jnp.concatenate([up[:, cols], down[:, cols], up[:, cols]], axis=1)
-                    pieces.append(dot(three, slope_ref[...]))
-                slopes[c, part] = (
-                    jnp.concatenate([pieces[0][:, :128], pieces[1][:, :128]], axis=1),
-                    jnp.concatenate([pieces[0][:, 128:], pieces[1][:, 128:]], axis=1),
-                )
         for part in range(2):
-            u_r, u_s = slopes[0, part]
-            v_r, v_s = slopes[1, part]
-            w_r, w_s = slopes[2, part]
-            if part == 0:
-                dz_u = -wave * fields[0, 1]
-                dz_v = -wave * fields[1, 1]
-            else:
-                dz_u = wave * fields[0, 0]
-                dz_v = wave * fields[1, 0]
+            u_r, u_s = grads[0, part, 0, rows, :], grads[0, part, 1, rows, :]
+            v_r, v_s = grads[1, part, 0, rows, :], grads[1, part, 1, rows, :]
+            w_r, w_s = grads[2, part, 0, rows, :], grads[2, part, 1, rows, :]
+            u_t = z_ref[pl.ds(step * count, count), 0, 1 - part].reshape(ROWS, 256)
+            v_t = z_ref[pl.ds(step * count, count), 1, 1 - part].reshape(ROWS, 256)
+            turn = -wave if part == 0 else wave
             swirl = (
-                ry * w_r + sy * w_s - dz_v,
-                dz_u - (rx * w_r + sx * w_s),
+                ry * w_r + sy * w_s - turn * v_t,
+                turn * u_t - (rx * w_r + sx * w_s),
                 rx * v_r + sx * v_s - (ry * u_r + sy * u_s),
             )
             for c in range(3):
@@ -229,7 +240,7 @@
     lax.fori_loop(0, 3, analyse, 0, unroll=True)
 
 
-def in_planes(blocks, rows):
+def in_planes(blocks, metric, rate, mask):
     synth_cos, synth_sin, back_cos, back_sin, wave, sign = tables(256)
     consts = [wave, sign, right_tables()]
     for table in (synth_cos, synth_sin, back_cos, back_sin):
@@ -244,7 +255,7 @@
     return pl.pallas_call(
         plane_kernel,
         grid=(2,),
-        in_specs=[block, pl.BlockSpec((8, 256), lambda i: (0, i))] + [whole(c) for c in consts],
+        in_specs=[block] + [whole(c) for c in [metric, rate, mask] + consts],
         out_specs=block,
         out_shape=jax.ShapeDtypeStruct((16, 3, 2, 16, 512), F32),
         scratch_shapes=[
@@ -254,10 +265,13 @@
             pltpu.VMEM((3, 2, 256, 256), BF16),
             pltpu.VMEM((3, 2, 256, 256), BF16),
             pltpu.VMEM((3, 8, 256), F32),
+            pltpu.VMEM((3, 2, 2, 256, 256), F32),
+            pltpu.VMEM((2, 8, 256), F32),
+            pltpu.VMEM((5, 128, 128), F32),
         ],
         compiler_params=pltpu.CompilerParams(vmem_limit_bytes=WIDE),
         name="in_planes",
-    )(blocks, rows, *consts)
+    )(blocks, metric, rate, mask, *consts)
 
 
 def slopes_of(pair, forward):
@@ -278,15 +292,11 @@
     return pl.BlockSpec(shape, lambda i: (0,) * len(shape))
 
 
-def in_smem():
-    return pl.BlockSpec(memory_space=pltpu.SMEM)
-
-
-def wave_of(ids_ref, kl):
-    return (ids_ref[1] * 16 + kl).astype(F32) * (np.pi / 256)
-
-
-def post_kernel(ids_ref, r_ref, metric_ref, mass_ref, fwd_ref, non_ref, raw_ref, edge_ref, tmp, coef):
+def wave_of(kl):
+    return (lax.axis_index("mode") * 16 + kl).astype(F32) * (np.pi / 256)
+
+
+def post_kernel(r_ref, metric_ref, mass_ref, fwd_ref, non_ref, raw_ref, edge_ref, tmp, coef):
     half = low_half((8, 128))
     for c in range(3):
         for pair in range(64):
@@ -310,7 +320,7 @@
             cells.append(block)
         x_r, x_s = slopes_of(jnp.concatenate([cells[0][:64], cells[0][64:]], axis=1), fwd_ref[...])
         y_r, y_s = slopes_of(jnp.concatenate([cells[1][:64], cells[1][64:]], axis=1), fwd_ref[...])
-        scaled = wave_of(ids_ref, base + kl) * mass_ref[...]
+        scaled = wave_of(base + kl) * mass_ref[...]
         for part in range(2):
             cols = slice(128 * part, 128 * part + 128)
             value = (
@@ -328,12 +338,11 @@
             edge_ref[1, part, kl] = raw_ref[part, kl, pl.ds(7, 8, stride=8), :]
 
 
-def from_blocks(ids, blocks, metric, mass, forward):
+def from_blocks(blocks, metric, mass, forward):
     return pl.pallas_call(
         post_kernel,
         grid=(2,),
         in_specs=[
-            in_smem(),
             pl.BlockSpec((16, 3, 2, 8, 512), lambda i: (0, 0, 0, i, 0)),
             whole_spec(metric.shape),
             whole_spec(mass.shape),
@@ -352,36 +361,38 @@
         scratch_shapes=[pltpu.VMEM((3, 1024, 128), F32), pltpu.VMEM((4, 64, 128), F32)],
         compiler_params=pltpu.CompilerParams(vmem_limit_bytes=NARROW),
         name="from_blocks",
-    )(ids, blocks, metric, mass, forward)
+    )(blocks, metric, mass, forward)
 
 
 def lanes(value, index):
     return jnp.take_along_axis(value, index, axis=1, mode="promise_in_bounds")
 
 
-def links_of(ids_ref, near_ref):
-    device = ids_ref[0]
+def links_of(link_ref):
+    device = lax.axis_index("elem")
     links = []
     for side in range(4):
-        ident = jnp.broadcast_to(near_ref[side : side + 1, :], (8, 128))
+        ident = jnp.broadcast_to(link_ref[side : side + 1, :], (8, 128))
         here = ident >= 0
         if side < 2:
             place = ident - (device - 1) * 128
-            links.append((jnp.where(here, place & 127, 0), jnp.where(here, place >> 7, 3)))
+            origin = place >> 7
+            origin = jnp.where((device & 1) == 1, origin, 2 - origin)
+            links.append((jnp.where(here, place & 127, 0), jnp.where(here, origin, 3)))
         else:
             links.append((jnp.where(here, ident - device * 128, 0), here))
     return links
 
 
-def share(out_ref, field_ref, west_ref, east_ref, links, part, kl):
+def share(out_ref, field_ref, near_edge, far_edge, links, part, kl):
     (west_lane, west_from), (east_lane, east_from), (south_lane, south_here), (north_lane, north_here) = links
     first = field_ref[part, kl, pl.ds(0, 8, stride=8), :]
     last = field_ref[part, kl, pl.ds(7, 8, stride=8), :]
 
     def pick(side, own, lane, origin):
         value = jnp.where(origin == 1, lanes(own, lane), 0.0)
-        value = jnp.where(origin == 0, lanes(west_ref[side, part, kl], lane), value)
-        return jnp.where(origin == 2, lanes(east_ref[side, part, kl], lane), value)
+        value = jnp.where(origin == 0, lanes(near_edge[side, part, kl], lane), value)
+        return jnp.where(origin == 2, lanes(far_edge[side, part, kl], lane), value)
 
     out_ref[part, kl] = field_ref[part, kl]
     out_ref[part, kl, pl.ds(0, 8, stride=8), :] = first + pick(1, last, west_lane, west_from)
@@ -400,9 +411,9 @@
     stiff[2] = mass * (sx * sx + sy * sy)
 
 
-def set_inverse(inverse, near_ref):
+def set_inverse(inverse, link_ref):
     node = lax.broadcasted_iota(jnp.int32, (64, 128), 0)
-    here = [near_ref[side : side + 1, :] >= 0 for side in range(4)]
+    here = [link_ref[side : side + 1, :] >= 0 for side in range(4)]
     places = [(node & 7) == 0, (node & 7) == 7, node < 8, node >= 56]
     value = jnp.ones((64, 128), F32)
     for place, there in zip(places, here):
@@ -426,17 +437,17 @@
 
 
 def image_kernel(
-    ids_ref, raw_ref, west_ref, east_ref, near_ref, metric_ref, mass_ref, fwd_ref, adj_ref, adl_ref,
+    raw_ref, near_edge, far_edge, link_ref, metric_ref, mass_ref, fwd_ref, adj_ref, adl_ref,
     field_ref, image_ref, edge_ref, stiff,
 ):
-    links = links_of(ids_ref, near_ref)
+    links = links_of(link_ref)
     set_stiff(stiff, metric_ref, mass_ref)
     for kl in range(16):
         for part in range(2):
-            share(field_ref, raw_ref, west_ref, east_ref, links, part, kl)
+            share(field_ref, raw_ref, near_edge, far_edge, links, part, kl)
     for kl in range(16):
         pair = jnp.concatenate([field_ref[0, kl], field_ref[1, kl]], axis=1)
-        wave = wave_of(ids_ref, kl)
+        wave = wave_of(kl)
         image = stiffness(pair, wave * wave + 1.0, stiff, mass_ref, fwd_ref, adj_ref, adl_ref)
         for part in range(2):
             image_ref[part, kl] = image[:, 128 * part : 128 * part + 128]
@@ -444,10 +455,10 @@
             edge_ref[1, part, kl] = image_ref[part, kl, pl.ds(7, 8, stride=8), :]
 
 
-def image_of(ids, raw, west, east, near, metric, mass, left):
+def image_of(raw, near, far, links, metric, mass, left):
     return pl.pallas_call(
         image_kernel,
-        in_specs=[in_smem()] + [pl.BlockSpec(memory_space=pltpu.VMEM)] * 9,
+        in_specs=[pl.BlockSpec(memory_space=pltpu.VMEM)] * 9,
         out_shape=[
             jax.ShapeDtypeStruct(FIELD, F32),
             jax.ShapeDtypeStruct(FIELD, F32),
@@ -456,7 +467,7 @@
         scratch_shapes=[pltpu.VMEM((3, 64, 128), F32)],
         compiler_params=pltpu.CompilerParams(vmem_limit_bytes=NARROW),
         name="image",
-    )(ids, raw, west, east, near, metric, mass, *left)
+    )(raw, near, far, links, metric, mass, *left)
 
 
 def folded_rows(value):
@@ -464,18 +475,18 @@
 
 
 def moments_kernel(
-    ids_ref, image_ref, west_ref, east_ref, field_ref, near_ref, metric_ref, mass_ref, fwd_ref, adj_ref,
+    image_ref, near_edge, far_edge, field_ref, link_ref, metric_ref, mass_ref, fwd_ref, adj_ref,
     adl_ref, shared_ref, sum_ref, stiff, inverse, second, rows, local,
 ):
-    links = links_of(ids_ref, near_ref)
+    links = links_of(link_ref)
     set_stiff(stiff, metric_ref, mass_ref)
-    set_inverse(inverse, near_ref)
+    set_inverse(inverse, link_ref)
     for kl in range(16):
         for part in range(2):
-            share(shared_ref, image_ref, west_ref, east_ref, links, part, kl)
+            share(shared_ref, image_ref, near_edge, far_edge, links, part, kl)
     for kl in range(16):
         pair = jnp.concatenate([shared_ref[0, kl], shared_ref[1, kl]], axis=1)
-        wave = wave_of(ids_ref, kl)
+        wave = wave_of(kl)
         image = stiffness(pair, wave * wave + 1.0, stiff, mass_ref, fwd_ref, adj_ref, adl_ref)
         for part in range(2):
             second[part, kl] = image[:, 128 * part : 128 * part + 128]
@@ -506,10 +517,10 @@
         sum_ref[d] = packed
 
 
-def moments_of(ids, image, west, east, field, near, metric, mass, left):
+def moments_of(image, near, far, field, links, metric, mass, left):
     return pl.pallas_call(
         moments_kernel,
-        in_specs=[in_smem()] + [pl.BlockSpec(memory_space=pltpu.VMEM)] * 10,
+        in_specs=[pl.BlockSpec(memory_space=pltpu.VMEM)] * 10,
         out_shape=[jax.ShapeDtypeStruct(FIELD, F32), jax.ShapeDtypeStruct((8, 16, 128), F32)],
         scratch_shapes=[
             pltpu.VMEM((3, 64, 128), F32),
@@ -520,7 +531,7 @@
         ],
         compiler_params=pltpu.CompilerParams(vmem_limit_bytes=NARROW),
         name="moments",
-    )(ids, image, west, east, field, near, metric, mass, *left)
+    )(image, near, far, field, links, metric, mass, *left)
 
 
 def final_kernel(field_ref, shared_ref, sum_ref, out_ref, scales):
@@ -560,9 +571,10 @@
 
 def swap_edges(edges):
     count = lax.axis_size("elem")
-    west = lax.ppermute(edges, "elem", [(i, i + 1) for i in range(count - 1)])
-    east = lax.ppermute(edges, "elem", [(i + 1, i) for i in range(count - 1)])
-    return west, east
+    far = [pair for i in range(1, count - 1, 2) for pair in ((i, i + 1), (i + 1, i))]
+    far = lax.ppermute(edges, "elem", far)
+    near = lax.ppermute(edges, "elem", [(i, i ^ 1) for i in range(count)])
+    return near, far
 
 
 def over(array, axis):
@@ -570,21 +582,16 @@
 
 
 def per_device(velocity, metric, mass, sponge_rate, sponge_mask, neighbours):
-    place = lax.axis_index("mode")
-    ids = jnp.stack([lax.axis_index("elem"), place]).astype(jnp.int32)
-    damping = sponge_mask.astype(F32)[None, :] * sponge_rate
-    rows = jnp.concatenate([metric, damping[None], jnp.zeros((3, 64, 128), F32)], axis=0)
-    rows = lax.dynamic_slice_in_dim(rows, place * 8, 8, axis=2)
-    rows = rows.transpose(0, 2, 1).reshape(8, 512)
     left = [jnp.asarray(t) for t in left_tables()]
 
     blocks = over(to_blocks(velocity), "mode")
-    blocks = over(in_planes(blocks, rows), "mode")
-    nonlinear, raw, edges = from_blocks(ids, blocks, metric, mass, left[0])
-    west, east = swap_edges(edges)
-    field, image, edges = image_of(ids, raw, west, east, neighbours, metric, mass, left)
-    west, east = swap_edges(edges)
-    shared, sums = moments_of(ids, image, west, east, field, neighbours, metric, mass, left)
+    blocks = in_planes(blocks, metric, sponge_rate, sponge_mask.reshape(1, 128))
+    blocks = over(blocks, "mode")
+    nonlinear, raw, edges = from_blocks(blocks, metric, mass, left[0])
+    near, far = swap_edges(edges)
+    field, image, edges = image_of(raw, near, far, neighbours, metric, mass, left)
+    near, far = swap_edges(edges)
+    shared, sums = moments_of(image, near, far, field, neighbours, metric, mass, left)
     return nonlinear, final(field, shared, over(sums, "elem"))
 
 

time: 167 us -> 141 us (0.84)
  waiting for transfers between devices: 93.1 us -> 2.32 us
  blocking collectives: 15.2 us -> 103 us
  starting transfers between devices: 24.4 us -> 10.1 us
  Pallas kernels: 32.2 us -> 24.1 us
    all_to_all x2 -> x0, waiting for transfers between devices: 91 us -> none  [over(): return lax.all_to_all(array, axis, split_axis=0, concat_axis=0, tiled=True)]
    all_to_all x1 -> x3, blocking collectives: 15.2 us -> 103 us  [over(): return lax.all_to_all(array, axis, split_axis=0, concat_axis=0, tiled=True)]
    all_to_all x2 -> x0, starting transfers between devices: 12.8 us -> none  [over(): return lax.all_to_all(array, axis, split_axis=0, concat_axis=0, tiled=True)]
    pallas_call x4, Pallas kernels: 25.6 us -> 18.8 us  [the longest x1 9.21 us: in_planes(): pl.pallas_call(plane_kernel, grid=(2,), in_specs=[block] + [whole(c) for...]
  transfers between devices with their start and end apart: 6 -> 4, of which waited for: 4 -> 2; matrix products, arithmetic and copies ran while one was open for 0% -> 0% of each run, Pallas kernels for 0% -> 0%
where the time goes in v3:
time: 141 us; the launch traced here: 140 us
  blocking collectives  103 us (73%)
  Pallas kernels  24.1 us (17%)
  starting transfers between devices  10.1 us (7%)
  waiting for transfers between devices  2.32 us (2%)
    all_to_all x3, blocking collectives, over(): return lax.all_to_all(array, axis, split_axis=0, concat_axis=0, tiled=True)  103 us
    pallas_call x1, Pallas kernels, in_planes(): pl.pallas_call(plane_kernel, grid=(2,), in_specs=[block] + [whole(c) for...  9.21 us
    ppermute x2, starting transfers between devices, swap_edges(): near = lax.ppermute(edges, 'elem', [(i, i ^ 1) for i in range(count)])  8.78 us
    pallas_call x1, Pallas kernels, to_blocks(): pl.pallas_call(pre_kernel, grid=(3,), in_specs=[pl.BlockSpec((1, 2, 16, 6...  4.02 us
    pallas_call x1, Pallas kernels, from_blocks(): pl.pallas_call(post_kernel, grid=(2,), in_specs=[pl.BlockSpec((16, 3, 2,...  3.62 us
    pallas_call x1, Pallas kernels, moments_of(): pl.pallas_call(moments_kernel, in_specs=[pl.BlockSpec(memory_space=pltpu....  3.58 us
  transfers between devices with their start and end apart: 4, of which 2 were waited for; matrix products, arithmetic and copies ran while one was open for 0% of the time, Pallas kernels for 0%

profile of v3, /device:TPU:0, one launch (start us, length us, event | category | flops | bytes accessed | tf_op | source)
XLA Modules:
  0.0 140.1 jit_solution(10267891944265068372)
XLA Ops:
  0.6 4.0 %to_blocks.1 = f32[16,3,2,16,512]{4,3,2,1,0:T(8,128)S(1)} custom-call(f32[3,2,16,64,128]{4,3,2,1,0:T(8,128)} %v_ref.1), custom_call_target="tpu_custom_call" | custom-call | tf_op jit(solution)/shard_map/to_blocks/pallas_call | solution.py:109
  4.7 0.0 copy-start
  4.7 0.0 copy-start.2
  4.7 0.0 copy-start.3
  4.7 0.0 copy-start.4
  4.7 0.0 copy-start.5
  4.7 0.0 copy-start.7
  4.7 0.0 copy-start.8
  4.7 0.0 copy-start.9
  4.8 0.0 copy-start.12
  4.8 0.0 copy-start.14
  4.8 47.8 %all_to_all.15.z_ref = f32[16,3,2,16,512]{4,3,2,1,0:T(8,128)} all-to-all(f32[16,3,2,16,512]{4,3,2,1,0:T(8,128)S(1)} %to_blocks.1), channel_id=1, replica_groups=mesh['elem'=8,'mode'=16] {'mode'}, dimensions={0} | all-to-all | bytes 6291456 | tf_op jit(solution)/shard_map/all_to_all | solution.py:581
  52.6 0.0 copy-done
  52.6 0.0 copy-done.2
  52.6 0.0 copy-done.3
  52.6 0.0 copy-done.4
  52.6 0.0 copy-done.5
  52.6 0.0 copy-done.7
  52.6 0.0 copy-done.8
  52.6 0.0 copy-done.9
  52.6 0.0 copy-done.12
  52.6 0.0 copy-done.14
  52.7 9.2 %in_planes.1 = f32[16,3,2,16,512]{4,3,2,1,0:T(8,128)S(1)} custom-call(f32[16,3,2,16,512]{4,3,2,1,0:T(8,128)} %all_to_all.15.z_ref, f32[4,64,128]{2,1,0:T(8,128)S(1)} %copy-done, f32[64,128]{1,0:T(8,128)S(1)} %copy-done.12, s32[1,128]{1,0:T(1,128)S(1)} %bitcast.1, f32[256,128]{1,0:T(8,128)S(1)} %copy-done.9, f32[256,128]{1,0:T(8,128)S(1)} %copy-done.8, ...), custom_call_target="tpu_custom_call" | custom-call | tf_op jit(solution)/shard_map/in_planes/pallas_call | solution.py:255
  61.9 0.0 copy-start.1
  61.9 0.0 copy-start.6
  61.9 42.1 %all_to_all.16.r_ref = f32[16,3,2,16,512]{4,3,2,1,0:T(8,128)S(1)} all-to-all(f32[16,3,2,16,512]{4,3,2,1,0:T(8,128)S(1)} %in_planes.1), channel_id=1, replica_groups=mesh['elem'=8,'mode'=16] {'mode'}, dimensions={0} | all-to-all | bytes 6291456 | tf_op jit(solution)/shard_map/all_to_all | solution.py:581
  104.0 0.0 copy-done.1
  104.0 0.0 copy-done.6
  104.0 0.0 copy-start.10
  104.0 0.0 copy-start.11
  104.0 0.0 copy-start.13
  104.0 3.6 %from_blocks.1 = (f32[3,2,16,64,128]{4,3,2,1,0:T(8,128)}, f32[2,16,64,128]{3,2,1,0:T(8,128)S(1)}, f32[2,2,16,8,128]{4,3,2,1,0:T(8,128)S(1)}) custom-call(f32[16,3,2,16,512]{4,3,2,1,0:T(8,128)S(1)} %all_to_all.16.r_ref, f32[4,64,128]{2,1,0:T(8,128)S(1)} %copy-done, f32[64,128]{1,0:T(8,128)S(1)} %copy-done.6, bf16[128,192]{1,0:T(8,128)(2,1)S(1)} %copy-done.1), custom_call_target="tpu_custom_call" | custom-call | tf_op jit(solution)/shard_map/from_blocks/pallas_call | solution.py:342
  107.7 0.7 collective-permute-start.1
  108.3 2.9 %collective-permute-start = (f32[2,2,16,8,128]{4,3,2,1,0:T(8,128)S(1)}, f32[2,2,16,8,128]{4,3,2,1,0:T(8,128)S(1)}, u32[]{:S(2)}, u32[]{:S(2)}) collective-permute-start(f32[2,2,16,8,128]{4,3,2,1,0:T(8,128)S(1)} %get-tuple-element.12), channel_id=1, source_target_pairs={{0,16},{16,0},{32,48},{48,32},{64,80},{80,64},{96,112},{112,96},{1... | collective-permute-start | bytes 786440 | tf_op jit(solution)/shard_map/ppermute | solution.py:576
  111.3 0.0 collective-permute-done.1.far_edge
  111.3 1.2 collective-permute-done.near_edge
  112.4 0.0 copy-done.10
  112.4 0.0 copy-done.11
  112.4 0.0 copy-done.13
  112.4 2.4 %image.1 = (f32[2,16,64,128]{3,2,1,0:T(8,128)S(1)}, f32[2,16,64,128]{3,2,1,0:T(8,128)S(1)}, f32[2,2,16,8,128]{4,3,2,1,0:T(8,128)S(1)}) custom-call(f32[2,16,64,128]{3,2,1,0:T(8,128)S(1)} %get-tuple-element.11.raw_ref, f32[2,2,16,8,128]{4,3,2,1,0:T(8,128)S(1)} %collective-permute-done.near_edge, f32[2,2,16,8,128]{4,3,2,1,0:T(8,128)S(1)} %collective-permute-done.1.far_edge, ...), custom_call_target="tpu_custom_call" | custom-call | tf_op jit(solution)/shard_map/image/pallas_call | solution.py:459
  114.8 0.7 collective-permute-start.3
  115.5 5.9 %collective-permute-start.2 = (f32[2,2,16,8,128]{4,3,2,1,0:T(8,128)S(1)}, f32[2,2,16,8,128]{4,3,2,1,0:T(8,128)S(1)}, u32[]{:S(2)}, u32[]{:S(2)}) collective-permute-start(f32[2,2,16,8,128]{4,3,2,1,0:T(8,128)S(1)} %get-tuple-element.15), channel_id=1, source_target_pairs={{0,16},{16,0},{32,48},{48,32},{64,80},{80,64},{96,112},{112,96},{1... | collective-permute-start | bytes 786440 | tf_op jit(solution)/shard_map/ppermute | solution.py:576
  121.4 0.0 collective-permute-done.3.far_edge
  121.4 1.2 collective-permute-done.2.near_edge
  122.5 3.6 %moments.1 = (f32[2,16,64,128]{3,2,1,0:T(8,128)S(1)}, f32[8,16,128]{2,1,0:T(8,128)S(1)}) custom-call(f32[2,16,64,128]{3,2,1,0:T(8,128)S(1)} %get-tuple-element.14.image_ref, f32[2,2,16,8,128]{4,3,2,1,0:T(8,128)S(1)} %collective-permute-done.2.near_edge, f32[2,2,16,8,128]{4,3,2,1,0:T(8,128)S(1)} %collective-permute-done.3.far_edge, ...), custom_call_target="tpu_custom_call" | custom-call | tf_op jit(solution)/shard_map/moments/pallas_call | solution.py:521
  126.1 12.6 %all_to_all.17.sum_ref = f32[8,16,128]{2,1,0:T(8,128)S(1)} all-to-all(f32[8,16,128]{2,1,0:T(8,128)S(1)} %get-tuple-element.17), channel_id=1, replica_groups=mesh['elem'=8,'mode'=16] {'elem'}, dimensions={0} | all-to-all | bytes 131072 | tf_op jit(solution)/shard_map/all_to_all | solution.py:581
  138.8 1.3 pressure.1
Async XLA Ops:
  4.7 47.9 %copy-start = (f32[4,64,128]{2,1,0:T(8,128)S(1)}, f32[4,64,128]{2,1,0:T(8,128)}, u32[]{:S(2)}) copy-start(f32[4,64,128]{2,1,0:T(8,128)} %metric_ref.7) | copy-start | bytes 393220
  4.7 47.9 %copy-start.2 = (bf16[272,768]{1,0:T(8,128)(2,1)S(1)}, bf16[272,768]{1,0:T(8,128)(2,1)}, u32[]{:S(2)}) copy-start(bf16[272,768]{1,0:T(8,128)(2,1)} %constant.26.clone.cos_ref) | copy-start | bytes 1253380
  4.7 47.9 %copy-start.3 = (bf16[256,768]{1,0:T(8,128)(2,1)S(1)}, bf16[256,768]{1,0:T(8,128)(2,1)}, u32[]{:S(2)}) copy-start(bf16[256,768]{1,0:T(8,128)(2,1)} %constant.29.clone.back_sin_ref) | copy-start | bytes 1179652
  4.7 47.9 %copy-start.4 = (bf16[256,768]{1,0:T(8,128)(2,1)S(1)}, bf16[256,768]{1,0:T(8,128)(2,1)}, u32[]{:S(2)}) copy-start(bf16[256,768]{1,0:T(8,128)(2,1)} %constant.28.clone.back_cos_ref) | copy-start | bytes 1179652
  4.7 47.9 %copy-start.5 = (bf16[256,768]{1,0:T(8,128)(2,1)S(1)}, bf16[256,768]{1,0:T(8,128)(2,1)}, u32[]{:S(2)}) copy-start(bf16[256,768]{1,0:T(8,128)(2,1)} %constant.27.clone.sin_ref) | copy-start | bytes 1179652
  4.7 47.9 %copy-start.7 = (bf16[384,256]{1,0:T(8,128)(2,1)S(1)}, bf16[384,256]{1,0:T(8,128)(2,1)}, u32[]{:S(2)}) copy-start(bf16[384,256]{1,0:T(8,128)(2,1)} %constant.25.clone.slope_ref) | copy-start | bytes 589828
  4.7 47.9 %copy-start.8 = (f32[256,128]{1,0:T(8,128)S(1)}, f32[256,128]{1,0:T(8,128)}, u32[]{:S(2)}) copy-start(f32[256,128]{1,0:T(8,128)} %constant.24.clone.sign_ref) | copy-start | bytes 393220
  4.7 47.9 %copy-start.9 = (f32[256,128]{1,0:T(8,128)S(1)}, f32[256,128]{1,0:T(8,128)}, u32[]{:S(2)}) copy-start(f32[256,128]{1,0:T(8,128)} %constant.23.clone.wave_ref) | copy-start | bytes 393220
  4.8 47.9 %copy-start.12 = (f32[64,128]{1,0:T(8,128)S(1)}, f32[64,128]{1,0:T(8,128)}, u32[]{:S(2)}) copy-start(f32[64,128]{1,0:T(8,128)} %rate_ref.1) | copy-start | bytes 98308
  4.8 47.9 %copy-start.14 = (s32[128]{0:T(128)S(1)}, s32[128]{0:T(128)}, u32[]{:S(2)}) copy-start(s32[128]{0:T(128)} %param.20) | copy-start | bytes 1540
  61.9 42.1 %copy-start.1 = (bf16[128,192]{1,0:T(8,128)(2,1)S(1)}, bf16[128,192]{1,0:T(8,128)(2,1)}, u32[]{:S(2)}) copy-start(bf16[128,192]{1,0:T(8,128)(2,1)} %constant.20.clone.fwd_ref) | copy-start | bytes 147460
  61.9 42.1 %copy-start.6 = (f32[64,128]{1,0:T(8,128)S(1)}, f32[64,128]{1,0:T(8,128)}, u32[]{:S(2)}) copy-start(f32[64,128]{1,0:T(8,128)} %mass_ref.5) | copy-start | bytes 98308
  104.0 8.4 %copy-start.10 = (bf16[64,256]{1,0:T(8,128)(2,1)S(1)}, bf16[64,256]{1,0:T(8,128)(2,1)}, u32[]{:S(2)}) copy-start(bf16[64,256]{1,0:T(8,128)(2,1)} %constant.21.clone.adj_ref) | copy-start | bytes 98308
  104.0 8.4 %copy-start.11 = (bf16[64,128]{1,0:T(8,128)(2,1)S(1)}, bf16[64,128]{1,0:T(8,128)(2,1)}, u32[]{:S(2)}) copy-start(bf16[64,128]{1,0:T(8,128)(2,1)} %constant.22.clone.adl_ref) | copy-start | bytes 49156
  104.0 8.4 %copy-start.13 = (s32[4,128]{1,0:T(4,128)S(1)}, s32[4,128]{1,0:T(4,128)}, u32[]{:S(2)}) copy-start(s32[4,128]{1,0:T(4,128)} %link_ref.3) | copy-start | bytes 6148
  107.7 3.6 %collective-permute-start.1 = (f32[2,2,16,8,128]{4,3,2,1,0:T(8,128)S(1)}, f32[2,2,16,8,128]{4,3,2,1,0:T(8,128)S(1)}, u32[]{:S(2)}, u32[]{:S(2)}) collective-permute-start(f32[2,2,16,8,128]{4,3,2,1,0:T(8,128)S(1)} %get-tuple-element.12), channel_id=1, source_target_pairs={{16,32},{32,16},{48,64},{64,48},{80,96},{96,80},{17,33},{33,17},{4... | collective-permute-start | bytes 786440 | tf_op jit(solution)/shard_map/ppermute | solution.py:575
  108.3 4.1 %collective-permute-start = (f32[2,2,16,8,128]{4,3,2,1,0:T(8,128)S(1)}, f32[2,2,16,8,128]{4,3,2,1,0:T(8,128)S(1)}, u32[]{:S(2)}, u32[]{:S(2)}) collective-permute-start(f32[2,2,16,8,128]{4,3,2,1,0:T(8,128)S(1)} %get-tuple-element.12), channel_id=1, source_target_pairs={{0,16},{16,0},{32,48},{48,32},{64,80},{80,64},{96,112},{112,96},{1... | collective-permute-start | bytes 786440 | tf_op jit(solution)/shard_map/ppermute | solution.py:576
  114.8 6.5 %collective-permute-start.3 = (f32[2,2,16,8,128]{4,3,2,1,0:T(8,128)S(1)}, f32[2,2,16,8,128]{4,3,2,1,0:T(8,128)S(1)}, u32[]{:S(2)}, u32[]{:S(2)}) collective-permute-start(f32[2,2,16,8,128]{4,3,2,1,0:T(8,128)S(1)} %get-tuple-element.15), channel_id=1, source_target_pairs={{16,32},{32,16},{48,64},{64,48},{80,96},{96,80},{17,33},{33,17},{4... | collective-permute-start | bytes 786440 | tf_op jit(solution)/shard_map/ppermute | solution.py:575
  115.5 7.0 %collective-permute-start.2 = (f32[2,2,16,8,128]{4,3,2,1,0:T(8,128)S(1)}, f32[2,2,16,8,128]{4,3,2,1,0:T(8,128)S(1)}, u32[]{:S(2)}, u32[]{:S(2)}) collective-permute-start(f32[2,2,16,8,128]{4,3,2,1,0:T(8,128)S(1)} %get-tuple-element.15), channel_id=1, source_target_pairs={{0,16},{16,0},{32,48},{48,32},{64,80},{80,64},{96,112},{112,96},{1... | collective-permute-start | bytes 786440 | tf_op jit(solution)/shard_map/ppermute | solution.py:576

commit v4 on v3

--- a/solution.py
+++ b/solution.py
@@ -12,6 +12,7 @@
 MIB = 1024 * 1024
 WIDE = 48 * MIB
 NARROW = 16 * MIB
+SMALL = pl.CostEstimate(flops=1000, bytes_accessed=1000, transcendentals=0)
 
 
 def cheb_matrix():
@@ -121,13 +122,14 @@
 ROWS = 32
 
 
-def node_rows(rows, tmp, metric_ref, rate_ref, mask_ref):
+def node_rows(rows, tmp, metric_ref, rate_ref, mask_ref, mass_ref):
     place = pl.multiple_of(lax.axis_index("mode") * 8, 8)
     damping = mask_ref[...].astype(F32) * rate_ref[...]
     blank = jnp.zeros((64, 128), F32)
-    for q, value in enumerate([metric_ref[0], metric_ref[1], metric_ref[2], metric_ref[3], damping]):
+    values = [metric_ref[0], metric_ref[1], metric_ref[2], metric_ref[3], damping, mass_ref[...]]
+    for q, value in enumerate(values):
         tmp[q] = jnp.concatenate([value, blank], axis=0).T
-    for q in range(5):
+    for q in range(6):
         mine = tmp[q, pl.ds(place, 8), :]
         other = swap(mine)
         for i in range(4):
@@ -136,12 +138,12 @@
 
 
 def plane_kernel(
-    z_ref, metric_ref, rate_ref, mask_ref, wave_ref, sign_ref, slope_ref, cos_ref, sin_ref,
-    back_cos_ref, back_sin_ref, out_ref, high, low, planes, eh, el, tail, grads, rows_all, turned,
+    z_ref, metric_ref, rate_ref, mask_ref, mass_ref, wave_ref, sign_ref, slope_ref, cos_ref, sin_ref,
+    back_cos_ref, back_sin_ref, out_ref, raw_ref, high, low, planes, eh, el, tail, grads, rows_all, turned,
 ):
     @pl.when(pl.program_id(0) == 0)
     def _():
-        node_rows(rows_all, turned, metric_ref, rate_ref, mask_ref)
+        node_rows(rows_all, turned, metric_ref, rate_ref, mask_ref, mass_ref)
 
     node = rows_all[pl.program_id(0)]
     rx = node[0:1, :]
@@ -149,6 +151,7 @@
     sx = node[2:3, :]
     sy = node[3:4, :]
     damping = node[4:5, :]
+    mass = node[5:6, :]
     count = ROWS // 16
 
     for c in range(3):
@@ -239,8 +242,33 @@
 
     lax.fori_loop(0, 3, analyse, 0, unroll=True)
 
-
-def in_planes(blocks, metric, rate, mask):
+    for c in range(2):
+        for part in range(2):
+            up, down = split(out_ref[:, c, part].reshape(256, 256))
+            for q in range(2):
+                cols = slice(128 * q, 128 * q + 128)
+                three = jnp.concatenate([up[:, cols], down[:, cols], up[:, cols]], axis=1)
+                both = dot(three, slope_ref[...])
+                grads[c, part, 0, :, cols] = both[:, :128]
+                grads[c, part, 1, :, cols] = both[:, 128:]
+    x_r, x_s, y_r, y_s = -mass * rx, -mass * sx, -mass * ry, -mass * sy
+    for step in range(256 // ROWS):
+        rows = slice(step * ROWS, step * ROWS + ROWS)
+        wave = jnp.concatenate([wave_ref[rows, :]] * 2, axis=1)
+        for part in range(2):
+            other = out_ref[count * step : count * step + count, 2, 1 - part].reshape(ROWS, 256)
+            turn = wave if part == 0 else -wave
+            value = (
+                x_r * grads[0, part, 0, rows, :]
+                + x_s * grads[0, part, 1, rows, :]
+                + y_r * grads[1, part, 0, rows, :]
+                + y_s * grads[1, part, 1, rows, :]
+                + mass * (turn * other)
+            )
+            raw_ref[count * step : count * step + count, part] = value.reshape(count, 16, 256)
+
+
+def in_planes(blocks, metric, rate, mask, mass):
     synth_cos, synth_sin, back_cos, back_sin, wave, sign = tables(256)
     consts = [wave, sign, right_tables()]
     for table in (synth_cos, synth_sin, back_cos, back_sin):
@@ -255,9 +283,12 @@
     return pl.pallas_call(
         plane_kernel,
         grid=(2,),
-        in_specs=[block] + [whole(c) for c in [metric, rate, mask] + consts],
-        out_specs=block,
-        out_shape=jax.ShapeDtypeStruct((16, 3, 2, 16, 512), F32),
+        in_specs=[block] + [whole(c) for c in [metric, rate, mask, mass] + consts],
+        out_specs=[block, pl.BlockSpec((16, 2, 16, 256), lambda i: (0, 0, 0, i))],
+        out_shape=[
+            jax.ShapeDtypeStruct((16, 3, 2, 16, 512), F32),
+            jax.ShapeDtypeStruct((16, 2, 16, 512), F32),
+        ],
         scratch_shapes=[
             pltpu.VMEM((6, 2, 256, 256), BF16),
             pltpu.VMEM((6, 2, 256, 256), BF16),
@@ -267,11 +298,11 @@
             pltpu.VMEM((3, 8, 256), F32),
             pltpu.VMEM((3, 2, 2, 256, 256), F32),
             pltpu.VMEM((2, 8, 256), F32),
-            pltpu.VMEM((5, 128, 128), F32),
+            pltpu.VMEM((6, 128, 128), F32),
         ],
         compiler_params=pltpu.CompilerParams(vmem_limit_bytes=WIDE),
         name="in_planes",
-    )(blocks, metric, rate, mask, *consts)
+    )(blocks, metric, rate, mask, mass, *consts)
 
 
 def slopes_of(pair, forward):
@@ -296,72 +327,55 @@
     return (lax.axis_index("mode") * 16 + kl).astype(F32) * (np.pi / 256)
 
 
-def post_kernel(r_ref, metric_ref, mass_ref, fwd_ref, non_ref, raw_ref, edge_ref, tmp, coef):
-    half = low_half((8, 128))
-    for c in range(3):
-        for pair in range(64):
-            g, i = divmod(pair, 4)
-            cols = slice(128 * i, 128 * i + 128)
-            re = r_ref[g, c, 0, :, cols]
-            im = r_ref[g, c, 1, :, cols]
-            tmp[c, 16 * pair : 16 * pair + 8, :] = jnp.where(half, re, swap(im))
-            tmp[c, 16 * pair + 8 : 16 * pair + 16, :] = jnp.where(half, swap(re), im)
-    mass = mass_ref[...]
-    coef[0] = -mass * metric_ref[0]
-    coef[1] = -mass * metric_ref[2]
-    coef[2] = -mass * metric_ref[1]
-    coef[3] = -mass * metric_ref[3]
-    base = pl.program_id(0) * 8
-    for kl in range(8):
-        cells = []
-        for c in range(3):
-            block = tmp[c, pl.ds(kl, 128, stride=8), :].T
-            non_ref[c, :, kl] = block.reshape(2, 64, 128)
-            cells.append(block)
-        x_r, x_s = slopes_of(jnp.concatenate([cells[0][:64], cells[0][64:]], axis=1), fwd_ref[...])
-        y_r, y_s = slopes_of(jnp.concatenate([cells[1][:64], cells[1][64:]], axis=1), fwd_ref[...])
-        scaled = wave_of(base + kl) * mass_ref[...]
-        for part in range(2):
-            cols = slice(128 * part, 128 * part + 128)
-            value = (
-                coef[0] * x_r[:, cols]
-                + coef[1] * x_s[:, cols]
-                + coef[2] * y_r[:, cols]
-                + coef[3] * y_s[:, cols]
-            )
-            if part == 0:
-                value = value + scaled * cells[2][64:]
-            else:
-                value = value - scaled * cells[2][:64]
-            raw_ref[part, kl] = value
+def turn_back(r_ref, tmp, count):
+    half = low_half((count, 128))
+    for pair in range(64):
+        g, i = divmod(pair, 4)
+        cols = slice(128 * i, 128 * i + 128)
+        re = r_ref[g, 0, :, cols]
+        im = r_ref[g, 1, :, cols]
+        place = 2 * count * pair
+        tmp[place : place + count, :] = jnp.where(half, re, swap(im))
+        tmp[place + count : place + 2 * count, :] = jnp.where(half, swap(re), im)
+
+
+def right_kernel(r_ref, raw_ref, edge_ref, tmp):
+    turn_back(r_ref, tmp, 16)
+    for kl in range(16):
+        raw_ref[:, kl] = tmp[pl.ds(kl, 128, stride=16), :].T.reshape(2, 64, 128)
+        for part in range(2):
             edge_ref[0, part, kl] = raw_ref[part, kl, pl.ds(0, 8, stride=8), :]
             edge_ref[1, part, kl] = raw_ref[part, kl, pl.ds(7, 8, stride=8), :]
 
 
-def from_blocks(blocks, metric, mass, forward):
+def right_side(blocks):
+    return pl.pallas_call(
+        right_kernel,
+        out_shape=[jax.ShapeDtypeStruct(FIELD, F32), jax.ShapeDtypeStruct(EDGE, F32)],
+        scratch_shapes=[pltpu.VMEM((2048, 128), F32)],
+        compiler_params=pltpu.CompilerParams(vmem_limit_bytes=NARROW),
+        cost_estimate=SMALL,
+        name="right_side",
+    )(blocks)
+
+
+def post_kernel(r_ref, non_ref, tmp):
+    turn_back(r_ref.at[:, 0], tmp, 16)
+    for kl in range(16):
+        non_ref[0, :, kl] = tmp[pl.ds(kl, 128, stride=16), :].T.reshape(2, 64, 128)
+
+
+def from_blocks(blocks):
     return pl.pallas_call(
         post_kernel,
-        grid=(2,),
-        in_specs=[
-            pl.BlockSpec((16, 3, 2, 8, 512), lambda i: (0, 0, 0, i, 0)),
-            whole_spec(metric.shape),
-            whole_spec(mass.shape),
-            whole_spec(forward.shape),
-        ],
-        out_specs=[
-            pl.BlockSpec((3, 2, 8, 64, 128), lambda i: (0, 0, i, 0, 0)),
-            pl.BlockSpec((2, 8, 64, 128), lambda i: (0, i, 0, 0)),
-            pl.BlockSpec((2, 2, 8, 8, 128), lambda i: (0, 0, i, 0, 0)),
-        ],
-        out_shape=[
-            jax.ShapeDtypeStruct((3, 2, 16, 64, 128), F32),
-            jax.ShapeDtypeStruct(FIELD, F32),
-            jax.ShapeDtypeStruct(EDGE, F32),
-        ],
-        scratch_shapes=[pltpu.VMEM((3, 1024, 128), F32), pltpu.VMEM((4, 64, 128), F32)],
+        grid=(3,),
+        in_specs=[pl.BlockSpec((16, 1, 2, 16, 512), lambda c: (0, c, 0, 0, 0))],
+        out_specs=pl.BlockSpec((1, 2, 16, 64, 128), lambda c: (c, 0, 0, 0, 0)),
+        out_shape=jax.ShapeDtypeStruct((3, 2, 16, 64, 128), F32),
+        scratch_shapes=[pltpu.VMEM((2048, 128), F32)],
         compiler_params=pltpu.CompilerParams(vmem_limit_bytes=NARROW),
         name="from_blocks",
-    )(blocks, metric, mass, forward)
+    )(blocks)
 
 
 def lanes(value, index):
@@ -466,6 +480,7 @@
         ],
         scratch_shapes=[pltpu.VMEM((3, 64, 128), F32)],
         compiler_params=pltpu.CompilerParams(vmem_limit_bytes=NARROW),
+        cost_estimate=SMALL,
         name="image",
     )(raw, near, far, links, metric, mass, *left)
 
@@ -513,15 +528,14 @@
     packed = local[...]
     for q, row in enumerate((0, 2, 1, 3, 4, 5)):
         packed = jnp.where(place == q + 1, jnp.sum(rows[row], axis=1, keepdims=True), packed)
-    for d in range(8):
-        sum_ref[d] = packed
+    sum_ref[0] = packed
 
 
 def moments_of(image, near, far, field, links, metric, mass, left):
     return pl.pallas_call(
         moments_kernel,
         in_specs=[pl.BlockSpec(memory_space=pltpu.VMEM)] * 10,
-        out_shape=[jax.ShapeDtypeStruct(FIELD, F32), jax.ShapeDtypeStruct((8, 16, 128), F32)],
+        out_shape=[jax.ShapeDtypeStruct(FIELD, F32), jax.ShapeDtypeStruct((1, 16, 128), F32)],
         scratch_shapes=[
             pltpu.VMEM((3, 64, 128), F32),
             pltpu.VMEM((64, 128), F32),
@@ -530,6 +544,7 @@
             pltpu.VMEM((16, 128), F32),
         ],
         compiler_params=pltpu.CompilerParams(vmem_limit_bytes=NARROW),
+        cost_estimate=SMALL,
         name="moments",
     )(image, near, far, field, links, metric, mass, *left)
 
@@ -565,6 +580,7 @@
         out_shape=jax.ShapeDtypeStruct(FIELD, F32),
         scratch_shapes=[pltpu.VMEM((2, 16, 128), F32)],
         compiler_params=pltpu.CompilerParams(vmem_limit_bytes=NARROW),
+        cost_estimate=SMALL,
         name="pressure",
     )(field, shared, sums)
 
@@ -577,6 +593,14 @@
     return near, far
 
 
+def gather_sums(sums):
+    count = lax.axis_size("elem")
+    for step in (1, 2, 4):
+        other = lax.ppermute(sums, "elem", [(i, i ^ step) for i in range(count)])
+        sums = jnp.concatenate([sums, other], axis=0)
+    return sums
+
+
 def over(array, axis):
     return lax.all_to_all(array, axis, split_axis=0, concat_axis=0, tiled=True)
 
@@ -585,14 +609,16 @@
     left = [jnp.asarray(t) for t in left_tables()]
 
     blocks = over(to_blocks(velocity), "mode")
-    blocks = in_planes(blocks, metric, sponge_rate, sponge_mask.reshape(1, 128))
+    blocks, raw = in_planes(blocks, metric, sponge_rate, sponge_mask.reshape(1, 128), mass)
+    raw = over(raw, "mode")
+    blocks, raw = lax.optimization_barrier((blocks, raw))
     blocks = over(blocks, "mode")
-    nonlinear, raw, edges = from_blocks(blocks, metric, mass, left[0])
+    raw, edges = right_side(raw)
     near, far = swap_edges(edges)
     field, image, edges = image_of(raw, near, far, neighbours, metric, mass, left)
     near, far = swap_edges(edges)
     shared, sums = moments_of(image, near, far, field, neighbours, metric, mass, left)
-    return nonlinear, final(field, shared, over(sums, "elem"))
+    return from_blocks(blocks), final(field, shared, gather_sums(sums))
 
 
 def solution(mesh):

time: 141 us -> 132 us (0.936)
  blocking collectives: 103 us -> 67.3 us
  waiting for transfers between devices: 2.32 us -> 14.4 us
  starting transfers between devices: 10.1 us -> 21.8 us
  Pallas kernels: 24.1 us -> 26.1 us
    all_to_all x3 -> x2, blocking collectives: 103 us -> 67.3 us  [over(): return lax.all_to_all(array, axis, split_axis=0, concat_axis=0, tiled=True)]
    ppermute x0 -> x3, starting transfers between devices: none -> 7.79 us  [gather_sums(): other = lax.ppermute(sums, 'elem', [(i, i ^ step) for i in range(count)])]
    all_to_all x0 -> x1, waiting for transfers between devices: none -> 6.53 us  [over(): return lax.all_to_all(array, axis, split_axis=0, concat_axis=0, tiled=True)]
    ppermute x0 -> x3, waiting for transfers between devices: none -> 5.58 us  [gather_sums(): other = lax.ppermute(sums, 'elem', [(i, i ^ step) for i in range(count)])]
    all_to_all x0 -> x1, starting transfers between devices: none -> 3.89 us  [over(): return lax.all_to_all(array, axis, split_axis=0, concat_axis=0, tiled=True)]
    pallas_call x1, Pallas kernels: 9.21 us -> 10.7 us  [in_planes(): pl.pallas_call(plane_kernel, grid=(2,), in_specs=[block] + [whole(c) for...]
    pallas_call x1 -> x2, Pallas kernels: 3.62 us -> 4.15 us  [the longest x1 3.43 us: from_blocks(): pl.pallas_call(post_kernel, grid=(3,), in_specs=[pl.BlockSpec((16, 1, 2,...]
  transfers between devices with their start and end apart: 4 -> 8, of which waited for: 2 -> 6; matrix products, arithmetic and copies ran while one was open for 0% -> 0% of each run, Pallas kernels for 0% -> 6%
where the time goes in v4:
time: 132 us
  blocking collectives  67.3 us (51%)
  Pallas kernels  26.1 us (20%)
  starting transfers between devices  21.8 us (17%)
  waiting for transfers between devices  14.4 us (11%)
    all_to_all x2, blocking collectives, over(): return lax.all_to_all(array, axis, split_axis=0, concat_axis=0, tiled=True)  67.3 us
    pallas_call x1, Pallas kernels, in_planes(): pl.pallas_call(plane_kernel, grid=(2,), in_specs=[block] + [whole(c) for...  10.7 us
    ppermute x2, starting transfers between devices, swap_edges(): near = lax.ppermute(edges, 'elem', [(i, i ^ 1) for i in range(count)])  8.78 us
    ppermute x3, starting transfers between devices, gather_sums(): other = lax.ppermute(sums, 'elem', [(i, i ^ step) for i in range(count)])  7.79 us
    all_to_all x1, waiting for transfers between devices, over(): return lax.all_to_all(array, axis, split_axis=0, concat_axis=0, tiled=True)  6.53 us
    ppermute x3, waiting for transfers between devices, gather_sums(): other = lax.ppermute(sums, 'elem', [(i, i ^ step) for i in range(count)])  5.58 us
    pallas_call x1, Pallas kernels, to_blocks(): pl.pallas_call(pre_kernel, grid=(3,), in_specs=[pl.BlockSpec((1, 2, 16, 6...  4.02 us
    all_to_all x1, starting transfers between devices, over(): return lax.all_to_all(array, axis, split_axis=0, concat_axis=0, tiled=True)  3.89 us
  transfers between devices with their start and end apart: 8, of which 6 were waited for; matrix products, arithmetic and copies ran while one was open for 0% of the time, Pallas kernels for 6%

profile of v4, /device:TPU:0, one launch (start us, length us, event | category | flops | bytes accessed | tf_op | source)
XLA Modules:
  0.0 131.8 jit_solution(17444923226184613800)
XLA Ops:
  0.6 4.0 %to_blocks.1 = f32[16,3,2,16,512]{4,3,2,1,0:T(8,128)S(1)} custom-call(f32[3,2,16,64,128]{4,3,2,1,0:T(8,128)} %v_ref.1), custom_call_target="tpu_custom_call" | custom-call | tf_op jit(solution)/shard_map/to_blocks/pallas_call | solution.py:110
  4.7 0.0 copy-start.1
  4.7 0.0 copy-start.2
  4.7 0.0 copy-start.3
  4.7 0.0 copy-start.4
  4.7 0.0 copy-start.5
  4.7 0.0 copy-start.6
  4.7 0.0 copy-start.8
  4.7 0.0 copy-start.10
  4.8 0.0 copy-start.11
  4.8 0.0 copy-start.13
  4.8 0.0 copy-start.15
  4.8 47.8 %all_to_all.15.z_ref = f32[16,3,2,16,512]{4,3,2,1,0:T(8,128)} all-to-all(f32[16,3,2,16,512]{4,3,2,1,0:T(8,128)S(1)} %to_blocks.1), channel_id=1, replica_groups=mesh['elem'=8,'mode'=16] {'mode'}, dimensions={0} | all-to-all | bytes 6291456 | tf_op jit(solution)/shard_map/all_to_all | solution.py:605
  52.6 0.0 copy-done.1
  52.6 0.0 copy-done.2
  52.6 0.0 copy-done.3
  52.6 0.0 copy-done.4
  52.6 0.0 copy-done.5
  52.6 0.0 copy-done.6
  52.6 0.0 copy-done.8
  52.6 0.0 copy-done.10
  52.6 0.0 copy-done.11
  52.7 0.0 copy-done.13
  52.7 0.0 copy-done.15
  52.7 10.7 %in_planes.1 = (f32[16,3,2,16,512]{4,3,2,1,0:T(8,128)}, f32[16,2,16,512]{3,2,1,0:T(8,128)S(1)}) custom-call(f32[16,3,2,16,512]{4,3,2,1,0:T(8,128)} %all_to_all.15.z_ref, f32[4,64,128]{2,1,0:T(8,128)S(1)} %copy-done.1, f32[64,128]{1,0:T(8,128)S(1)} %copy-done.13, s32[1,128]{1,0:T(1,128)S(1)} %bitcast.1, f32[64,128]{1,0:T(8,128)S(1)} %copy-done.6, ...), custom_call_target="tpu_custom_call" | custom-call | tf_op jit(solution)/shard_map/in_planes/pallas_call | solution.py:283
  63.4 19.6 %all_to_all.16.r_ref = f32[16,2,16,512]{3,2,1,0:T(8,128)} all-to-all(f32[16,2,16,512]{3,2,1,0:T(8,128)S(1)} %get-tuple-element.14), channel_id=1, replica_groups=mesh['elem'=8,'mode'=16] {'mode'}, dimensions={0} | all-to-all | bytes 2097152 | tf_op jit(solution)/shard_map/all_to_all | solution.py:605
  83.0 0.0 copy-start.7
  83.0 0.0 copy-start.9
  83.0 0.0 copy-start.12
  83.0 0.0 copy-start.14
  83.0 3.9 %all-to-all-start.2 = ((f32[16,3,2,16,512]{4,3,2,1,0:T(8,128)}), f32[16,3,2,16,512]{4,3,2,1,0:T(8,128)S(1)}, u32[]{:S(2)}, u32[]{:S(2)}) async-start(f32[16,3,2,16,512]{4,3,2,1,0:T(8,128)} %get-tuple-element.15), calls=%async_computation.2 | async-start | bytes 6291456 | tf_op jit(solution)/shard_map/all_to_all | solution.py:605
  86.9 0.0 copy-start
  86.9 1.2 copy-done
  88.1 0.7 right_side.1
  88.8 0.7 collective-permute-start.1
  89.5 2.9 %collective-permute-start = (f32[2,2,16,8,128]{4,3,2,1,0:T(8,128)S(1)}, f32[2,2,16,8,128]{4,3,2,1,0:T(8,128)S(1)}, u32[]{:S(2)}, u32[]{:S(2)}) collective-permute-start(f32[2,2,16,8,128]{4,3,2,1,0:T(8,128)S(1)} %get-tuple-element.18), channel_id=1, source_target_pairs={{0,16},{16,0},{32,48},{48,32},{64,80},{80,64},{96,112},{112,96},{1... | collective-permute-start | bytes 786440 | tf_op jit(solution)/shard_map/ppermute | solution.py:592
  92.4 0.0 collective-permute-done.1.far_edge
  92.4 1.2 collective-permute-done.near_edge
  93.6 0.0 copy-done.7
  93.6 0.0 copy-done.9
  93.6 0.0 copy-done.12
  93.6 0.0 copy-done.14
  93.6 2.4 %image.1 = (f32[2,16,64,128]{3,2,1,0:T(8,128)S(1)}, f32[2,16,64,128]{3,2,1,0:T(8,128)S(1)}, f32[2,2,16,8,128]{4,3,2,1,0:T(8,128)S(1)}) custom-call(f32[2,16,64,128]{3,2,1,0:T(8,128)S(1)} %get-tuple-element.17.raw_ref, f32[2,2,16,8,128]{4,3,2,1,0:T(8,128)S(1)} %collective-permute-done.near_edge, f32[2,2,16,8,128]{4,3,2,1,0:T(8,128)S(1)} %collective-permute-done.1.far_edge, ...), custom_call_target="tpu_custom_call" | custom-call | flops 1000 | bytes 1000 | tf_op jit(solution)/shard_map/image/pallas_call | solution.py:473
  96.0 0.7 collective-permute-start.3
  96.7 5.9 %collective-permute-start.2 = (f32[2,2,16,8,128]{4,3,2,1,0:T(8,128)S(1)}, f32[2,2,16,8,128]{4,3,2,1,0:T(8,128)S(1)}, u32[]{:S(2)}, u32[]{:S(2)}) collective-permute-start(f32[2,2,16,8,128]{4,3,2,1,0:T(8,128)S(1)} %get-tuple-element.21), channel_id=1, source_target_pairs={{0,16},{16,0},{32,48},{48,32},{64,80},{80,64},{96,112},{112,96},{1... | collective-permute-start | bytes 786440 | tf_op jit(solution)/shard_map/ppermute | solution.py:592
  102.5 0.0 collective-permute-done.3.far_edge
  102.5 1.2 collective-permute-done.2.near_edge
  103.7 3.5 %moments.1 = (f32[2,16,64,128]{3,2,1,0:T(8,128)S(1)}, f32[1,16,128]{2,1,0:T(8,128)S(1)}) custom-call(f32[2,16,64,128]{3,2,1,0:T(8,128)S(1)} %get-tuple-element.20.image_ref, f32[2,2,16,8,128]{4,3,2,1,0:T(8,128)S(1)} %collective-permute-done.2.near_edge, f32[2,2,16,8,128]{4,3,2,1,0:T(8,128)S(1)} %collective-permute-done.3.far_edge, ...), custom_call_target="tpu_custom_call" | custom-call | flops 1000 | bytes 1000 | tf_op jit(solution)/shard_map/moments/pallas_call | solution.py:535
  107.2 3.4 %collective-permute-start.4 = (f32[1,16,128]{2,1,0:T(8,128)S(1)}, f32[1,16,128]{2,1,0:T(8,128)S(1)}, u32[]{:S(2)}, u32[]{:S(2)}) collective-permute-start(f32[1,16,128]{2,1,0:T(8,128)S(1)} %get-tuple-element.23), channel_id=1, source_target_pairs={{0,16},{16,0},{32,48},{48,32},{64,80},{80,64},{96,112},{112,96},{1... | collective-permute-start | bytes 24584 | tf_op jit(solution)/shard_map/ppermute | solution.py:599
  110.6 0.8 collective-permute-done.4
  111.4 1.5 %collective-permute-start.5 = (f32[2,16,128]{2,1,0:T(8,128)S(1)}, f32[2,16,128]{2,1,0:T(8,128)S(1)}, u32[]{:S(2)}, u32[]{:S(2)}) collective-permute-start(f32[2,16,128]{2,1,0:T(8,128)S(1)} %pad_maximum_fusion.2), channel_id=1, source_target_pairs={{0,32},{16,48},{32,0},{48,16},{64,96},{80,112},{96,64},{112,80},{1... | collective-permute-start | bytes 49160 | tf_op jit(solution)/shard_map/ppermute | solution.py:599
  112.9 2.2 %collective-permute-done.5 = f32[2,16,128]{2,1,0:T(8,128)S(1)} collective-permute-done((f32[2,16,128]{2,1,0:T(8,128)S(1)}, f32[2,16,128]{2,1,0:T(8,128)S(1)}, u32[]{:S(2)}, u32[]{:S(2)}) %collective-permute-start.5) | collective-permute-done | bytes 16416 | tf_op jit(solution)/shard_map/ppermute | solution.py:599
  115.1 2.9 %collective-permute-start.6 = (f32[4,16,128]{2,1,0:T(8,128)S(1)}, f32[4,16,128]{2,1,0:T(8,128)S(1)}, u32[]{:S(2)}, u32[]{:S(2)}) collective-permute-start(f32[4,16,128]{2,1,0:T(8,128)S(1)} %pad_maximum_fusion.1), channel_id=1, source_target_pairs={{0,64},{16,80},{32,96},{48,112},{64,0},{80,16},{96,32},{112,48},{1... | collective-permute-start | bytes 98312 | tf_op jit(solution)/shard_map/ppermute | solution.py:599
  118.0 2.5 %collective-permute-done.6 = f32[4,16,128]{2,1,0:T(8,128)S(1)} collective-permute-done((f32[4,16,128]{2,1,0:T(8,128)S(1)}, f32[4,16,128]{2,1,0:T(8,128)S(1)}, u32[]{:S(2)}, u32[]{:S(2)}) %collective-permute-start.6) | collective-permute-done | bytes 32800 | tf_op jit(solution)/shard_map/ppermute | solution.py:599
  120.6 1.3 pressure.1
  121.9 6.5 %all-to-all-done.2.r_ref = f32[16,3,2,16,512]{4,3,2,1,0:T(8,128)S(1)} async-done(((f32[16,3,2,16,512]{4,3,2,1,0:T(8,128)}), f32[16,3,2,16,512]{4,3,2,1,0:T(8,128)S(1)}, u32[]{:S(2)}, u32[]{:S(2)}) %all-to-all-start.2) | async-done | bytes 3145760 | tf_op jit(solution)/shard_map/all_to_all | solution.py:605
  128.4 3.4 %from_blocks.1 = f32[3,2,16,64,128]{4,3,2,1,0:T(8,128)} custom-call(f32[16,3,2,16,512]{4,3,2,1,0:T(8,128)S(1)} %all-to-all-done.2.r_ref), custom_call_target="tpu_custom_call" | custom-call | tf_op jit(solution)/shard_map/from_blocks/pallas_call | solution.py:369
  (3 shorter events, 0.0 us)
Async XLA Ops:
  4.7 47.9 %copy-start.1 = (f32[4,64,128]{2,1,0:T(8,128)S(1)}, f32[4,64,128]{2,1,0:T(8,128)}, u32[]{:S(2)}) copy-start(f32[4,64,128]{2,1,0:T(8,128)} %metric_ref.5) | copy-start | bytes 393220
  4.7 47.9 %copy-start.2 = (bf16[272,768]{1,0:T(8,128)(2,1)S(1)}, bf16[272,768]{1,0:T(8,128)(2,1)}, u32[]{:S(2)}) copy-start(bf16[272,768]{1,0:T(8,128)(2,1)} %constant.26.clone.cos_ref) | copy-start | bytes 1253380
  4.7 47.9 %copy-start.3 = (bf16[256,768]{1,0:T(8,128)(2,1)S(1)}, bf16[256,768]{1,0:T(8,128)(2,1)}, u32[]{:S(2)}) copy-start(bf16[256,768]{1,0:T(8,128)(2,1)} %constant.29.clone.back_sin_ref) | copy-start | bytes 1179652
  4.7 47.9 %copy-start.4 = (bf16[256,768]{1,0:T(8,128)(2,1)S(1)}, bf16[256,768]{1,0:T(8,128)(2,1)}, u32[]{:S(2)}) copy-start(bf16[256,768]{1,0:T(8,128)(2,1)} %constant.28.clone.back_cos_ref) | copy-start | bytes 1179652
  4.7 47.9 %copy-start.5 = (bf16[256,768]{1,0:T(8,128)(2,1)S(1)}, bf16[256,768]{1,0:T(8,128)(2,1)}, u32[]{:S(2)}) copy-start(bf16[256,768]{1,0:T(8,128)(2,1)} %constant.27.clone.sin_ref) | copy-start | bytes 1179652
  4.7 47.9 %copy-start.6 = (f32[64,128]{1,0:T(8,128)S(1)}, f32[64,128]{1,0:T(8,128)}, u32[]{:S(2)}) copy-start(f32[64,128]{1,0:T(8,128)} %mass_ref.5) | copy-start | bytes 98308
  4.7 47.9 %copy-start.8 = (bf16[384,256]{1,0:T(8,128)(2,1)S(1)}, bf16[384,256]{1,0:T(8,128)(2,1)}, u32[]{:S(2)}) copy-start(bf16[384,256]{1,0:T(8,128)(2,1)} %constant.25.clone.slope_ref) | copy-start | bytes 589828
  4.7 47.9 %copy-start.10 = (f32[256,128]{1,0:T(8,128)S(1)}, f32[256,128]{1,0:T(8,128)}, u32[]{:S(2)}) copy-start(f32[256,128]{1,0:T(8,128)} %constant.24.clone.sign_ref) | copy-start | bytes 393220
  4.8 47.9 %copy-start.11 = (f32[256,128]{1,0:T(8,128)S(1)}, f32[256,128]{1,0:T(8,128)}, u32[]{:S(2)}) copy-start(f32[256,128]{1,0:T(8,128)} %constant.23.clone.wave_ref) | copy-start | bytes 393220
  4.8 47.9 %copy-start.13 = (f32[64,128]{1,0:T(8,128)S(1)}, f32[64,128]{1,0:T(8,128)}, u32[]{:S(2)}) copy-start(f32[64,128]{1,0:T(8,128)} %rate_ref.1) | copy-start | bytes 98308
  4.8 47.9 %copy-start.15 = (s32[128]{0:T(128)S(1)}, s32[128]{0:T(128)}, u32[]{:S(2)}) copy-start(s32[128]{0:T(128)} %param.20) | copy-start | bytes 1540
  83.0 10.6 %copy-start.7 = (bf16[128,192]{1,0:T(8,128)(2,1)S(1)}, bf16[128,192]{1,0:T(8,128)(2,1)}, u32[]{:S(2)}) copy-start(bf16[128,192]{1,0:T(8,128)(2,1)} %constant.20.clone.fwd_ref) | copy-start | bytes 147460
  83.0 10.6 %copy-start.9 = (bf16[64,256]{1,0:T(8,128)(2,1)S(1)}, bf16[64,256]{1,0:T(8,128)(2,1)}, u32[]{:S(2)}) copy-start(bf16[64,256]{1,0:T(8,128)(2,1)} %constant.21.clone.adj_ref) | copy-start | bytes 98308
  83.0 10.6 %copy-start.12 = (bf16[64,128]{1,0:T(8,128)(2,1)S(1)}, bf16[64,128]{1,0:T(8,128)(2,1)}, u32[]{:S(2)}) copy-start(bf16[64,128]{1,0:T(8,128)(2,1)} %constant.22.clone.adl_ref) | copy-start | bytes 49156
  83.0 10.6 %copy-start.14 = (s32[4,128]{1,0:T(4,128)S(1)}, s32[4,128]{1,0:T(4,128)}, u32[]{:S(2)}) copy-start(s32[4,128]{1,0:T(4,128)} %link_ref.3) | copy-start | bytes 6148
  83.0 45.4 %all-to-all-start.2 = ((f32[16,3,2,16,512]{4,3,2,1,0:T(8,128)}), f32[16,3,2,16,512]{4,3,2,1,0:T(8,128)S(1)}, u32[]{:S(2)}, u32[]{:S(2)}) async-start(f32[16,3,2,16,512]{4,3,2,1,0:T(8,128)} %get-tuple-element.15), calls=%async_computation.2 | async-start | bytes 6291456 | tf_op jit(solution)/shard_map/all_to_all | solution.py:605
  86.9 1.2 copy-start
  88.8 3.6 %collective-permute-start.1 = (f32[2,2,16,8,128]{4,3,2,1,0:T(8,128)S(1)}, f32[2,2,16,8,128]{4,3,2,1,0:T(8,128)S(1)}, u32[]{:S(2)}, u32[]{:S(2)}) collective-permute-start(f32[2,2,16,8,128]{4,3,2,1,0:T(8,128)S(1)} %get-tuple-element.18), channel_id=1, source_target_pairs={{16,32},{32,16},{48,64},{64,48},{80,96},{96,80},{17,33},{33,17},{4... | collective-permute-start | bytes 786440 | tf_op jit(solution)/shard_map/ppermute | solution.py:591
  89.5 4.1 %collective-permute-start = (f32[2,2,16,8,128]{4,3,2,1,0:T(8,128)S(1)}, f32[2,2,16,8,128]{4,3,2,1,0:T(8,128)S(1)}, u32[]{:S(2)}, u32[]{:S(2)}) collective-permute-start(f32[2,2,16,8,128]{4,3,2,1,0:T(8,128)S(1)} %get-tuple-element.18), channel_id=1, source_target_pairs={{0,16},{16,0},{32,48},{48,32},{64,80},{80,64},{96,112},{112,96},{1... | collective-permute-start | bytes 786440 | tf_op jit(solution)/shard_map/ppermute | solution.py:592
  96.0 6.6 %collective-permute-start.3 = (f32[2,2,16,8,128]{4,3,2,1,0:T(8,128)S(1)}, f32[2,2,16,8,128]{4,3,2,1,0:T(8,128)S(1)}, u32[]{:S(2)}, u32[]{:S(2)}) collective-permute-start(f32[2,2,16,8,128]{4,3,2,1,0:T(8,128)S(1)} %get-tuple-element.21), channel_id=1, source_target_pairs={{16,32},{32,16},{48,64},{64,48},{80,96},{96,80},{17,33},{33,17},{4... | collective-permute-start | bytes 786440 | tf_op jit(solution)/shard_map/ppermute | solution.py:591
  96.7 7.0 %collective-permute-start.2 = (f32[2,2,16,8,128]{4,3,2,1,0:T(8,128)S(1)}, f32[2,2,16,8,128]{4,3,2,1,0:T(8,128)S(1)}, u32[]{:S(2)}, u32[]{:S(2)}) collective-permute-start(f32[2,2,16,8,128]{4,3,2,1,0:T(8,128)S(1)} %get-tuple-element.21), channel_id=1, source_target_pairs={{0,16},{16,0},{32,48},{48,32},{64,80},{80,64},{96,112},{112,96},{1... | collective-permute-start | bytes 786440 | tf_op jit(solution)/shard_map/ppermute | solution.py:592
  107.2 4.2 %collective-permute-start.4 = (f32[1,16,128]{2,1,0:T(8,128)S(1)}, f32[1,16,128]{2,1,0:T(8,128)S(1)}, u32[]{:S(2)}, u32[]{:S(2)}) collective-permute-start(f32[1,16,128]{2,1,0:T(8,128)S(1)} %get-tuple-element.23), channel_id=1, source_target_pairs={{0,16},{16,0},{32,48},{48,32},{64,80},{80,64},{96,112},{112,96},{1... | collective-permute-start | bytes 24584 | tf_op jit(solution)/shard_map/ppermute | solution.py:599
  111.4 3.7 %collective-permute-start.5 = (f32[2,16,128]{2,1,0:T(8,128)S(1)}, f32[2,16,128]{2,1,0:T(8,128)S(1)}, u32[]{:S(2)}, u32[]{:S(2)}) collective-permute-start(f32[2,16,128]{2,1,0:T(8,128)S(1)} %pad_maximum_fusion.2), channel_id=1, source_target_pairs={{0,32},{16,48},{32,0},{48,16},{64,96},{80,112},{96,64},{112,80},{1... | collective-permute-start | bytes 49160 | tf_op jit(solution)/shard_map/ppermute | solution.py:599
  115.1 5.4 %collective-permute-start.6 = (f32[4,16,128]{2,1,0:T(8,128)S(1)}, f32[4,16,128]{2,1,0:T(8,128)S(1)}, u32[]{:S(2)}, u32[]{:S(2)}) collective-permute-start(f32[4,16,128]{2,1,0:T(8,128)S(1)} %pad_maximum_fusion.1), channel_id=1, source_target_pairs={{0,64},{16,80},{32,96},{48,112},{64,0},{80,16},{96,32},{112,48},{1... | collective-permute-start | bytes 98312 | tf_op jit(solution)/shard_map/ppermute | solution.py:599

commit v5 on v4

--- a/solution.py
+++ b/solution.py
@@ -11,6 +11,7 @@
 BF16 = jnp.bfloat16
 MIB = 1024 * 1024
 WIDE = 48 * MIB
+BLOCKS = (16, 3, 128, 128)
 NARROW = 16 * MIB
 SMALL = pl.CostEstimate(flops=1000, bytes_accessed=1000, transcendentals=0)
 
@@ -33,24 +34,41 @@
     return high, low
 
 
+def mode_order(modes):
+    row = np.arange(modes)
+    return 16 * ((row % (modes // 2)) // 8) + 2 * (row % 8) + row // (modes // 2)
+
+
 def tables(modes):
     planes = 2 * modes
-    order = np.arange(modes)
-    spots = np.arange(modes)
-    phase = (spots[:, None] * order[None, :]) % planes
-    angle = phase * (2.0 * np.pi / planes)
-    weight = np.where(order == 0, 1.0, 2.0)
-    cosine = np.cos(angle)
-    sine = np.sin(angle)
-    last = np.zeros((16, modes))
-    last[0] = weight * (-1.0) ** order
-    synth_cos = np.concatenate([weight * cosine, last], axis=0)
-    synth_sin = weight * sine
-    back_cos = cosine.T / planes
-    back_sin = -sine.T / planes
+    half = modes // 2
+    order = mode_order(modes)
+    even, odd = order[:half], order[half:]
+    spots = np.arange(half)
+
+    def angles(places, ks):
+        return ((places[:, None] * ks[None, :]) % planes) * (2.0 * np.pi / planes)
+
+    quarter = np.array([half])
+    weight_even = np.where(even == 0, 1.0, 2.0)
+    extra = np.zeros((16, half))
+    extra[:1] = weight_even * np.cos(angles(quarter, even))
+    cos_even = np.concatenate([weight_even * np.cos(angles(spots, even)), extra], axis=0)
+    cos_odd = 2.0 * np.cos(angles(spots, odd))
+    sin_even = weight_even * np.sin(angles(spots, even))
+    sin_odd = 2.0 * np.sin(angles(spots, odd))
+    sin_odd[:1] = 2.0 * np.sin(angles(quarter, odd))
+    back_cos_even = np.cos(angles(spots, even)).T / planes
+    back_cos_odd = np.cos(angles(spots, odd)).T / planes
+    back_sin_even = -np.sin(angles(spots, even)).T / planes
+    back_sin_odd = -np.sin(angles(spots, odd)).T / planes
+    back_sin_odd[:, :1] = -np.sin(angles(quarter, odd)).T / planes
     wave = np.broadcast_to((order * np.pi / modes)[:, None], (modes, 128)).astype(np.float32)
-    sign = np.broadcast_to(((-1.0) ** order / planes)[:, None], (modes, 128)).astype(np.float32)
-    return synth_cos, synth_sin, back_cos, back_sin, wave, sign
+    sign = np.round(np.cos(angles(quarter, even)).T) / planes
+    sign = np.broadcast_to(sign, (half, 128)).astype(np.float32)
+    there = [cos_even, cos_odd, sin_even, sin_odd]
+    back = [back_cos_even, back_cos_odd, back_sin_even, back_sin_odd]
+    return there, back, wave, sign
 
 
 def right_tables():
@@ -92,29 +110,34 @@
     return pltpu.roll(value, 64, 1)
 
 
-def pre_kernel(v_ref, y_ref, tmp):
-    for kl in range(16):
-        block = v_ref[0, :, kl].reshape(128, 128)
-        tmp[pl.ds(kl, 128, stride=16), :] = block.T
-    half = low_half((16, 128))
-    for pair in range(64):
-        first = tmp[32 * pair : 32 * pair + 16, :]
-        second = tmp[32 * pair + 16 : 32 * pair + 32, :]
-        g, i = divmod(pair, 4)
-        cols = slice(128 * i, 128 * i + 128)
-        y_ref[g, 0, 0, :, cols] = jnp.where(half, first, swap(second))
-        y_ref[g, 0, 1, :, cols] = jnp.where(half, swap(first), second)
+def spot(kl):
+    return 8 * (kl % 2) + kl // 2
+
+
+def pre_kernel(v_all, y_ref, v_ref, sems):
+    def fetch(c, h):
+        part = pl.ds(8 * h, 8)
+        return pltpu.make_async_copy(v_all.at[c, :, part], v_ref.at[c, :, part], sems.at[c, h])
+
+    pieces = [(c, h) for c in range(3) for h in range(2)]
+    for piece in pieces:
+        fetch(*piece).start()
+    for c, h in pieces:
+        fetch(c, h).wait()
+        for kl in range(8 * h, 8 * h + 8):
+            turned = v_ref[c, :, kl].reshape(128, 128).T
+            for g in range(16):
+                y_ref[g, c, pl.ds(spot(kl), 8, stride=16), :] = turned[8 * g : 8 * g + 8, :]
 
 
 def to_blocks(velocity):
     return pl.pallas_call(
         pre_kernel,
-        grid=(3,),
-        in_specs=[pl.BlockSpec((1, 2, 16, 64, 128), lambda c: (c, 0, 0, 0, 0))],
-        out_specs=pl.BlockSpec((16, 1, 2, 16, 512), lambda c: (0, c, 0, 0, 0)),
-        out_shape=jax.ShapeDtypeStruct((16, 3, 2, 16, 512), F32),
-        scratch_shapes=[pltpu.VMEM((2048, 128), F32)],
-        compiler_params=pltpu.CompilerParams(vmem_limit_bytes=WIDE),
+        in_specs=[pl.BlockSpec(memory_space=pl.ANY)],
+        out_specs=pl.BlockSpec(memory_space=pltpu.VMEM),
+        out_shape=jax.ShapeDtypeStruct(BLOCKS, F32),
+        scratch_shapes=[pltpu.VMEM((3, 2, 16, 64, 128), F32), pltpu.SemaphoreType.DMA((3, 2))],
+        compiler_params=pltpu.CompilerParams(vmem_limit_bytes=48 * MIB),
         name="to_blocks",
     )(velocity)
 
@@ -137,44 +160,94 @@
             rows[i // 2, q : q + 1, 128 * (i % 2) : 128 * (i % 2) + 128] = row
 
 
+def stacked(high, low):
+    return jnp.concatenate([high, low, high], axis=0)
+
+
 def plane_kernel(
-    z_ref, metric_ref, rate_ref, mask_ref, mass_ref, wave_ref, sign_ref, slope_ref, cos_ref, sin_ref,
-    back_cos_ref, back_sin_ref, out_ref, raw_ref, high, low, planes, eh, el, tail, grads, rows_all, turned,
+    z_all, metric_ref, rate_ref, mask_ref, mass_ref, wave_ref, sign_ref, slope_ref, ce_ref, co_ref,
+    se_ref, so_ref, bce_ref, bco_ref, bse_ref, bso_ref, out_all, raw_ref, z_ref, out_ref, high, low, planes, eh, el,
+    tail, grads, flat, rows_all, turned, z_sem,
+    out_sem,
 ):
-    @pl.when(pl.program_id(0) == 0)
-    def _():
-        node_rows(rows_all, turned, metric_ref, rate_ref, mask_ref, mass_ref)
-
-    node = rows_all[pl.program_id(0)]
+    def fetch(i, c):
+        part = pl.ds(pl.multiple_of(64 * i, 64), 64)
+        return pltpu.make_async_copy(z_all.at[:, c, part, :], z_ref.at[:, c, part, :], z_sem.at[i, c])
+
+    def store(i):
+        part = pl.ds(pl.multiple_of(64 * i, 64), 64)
+        return pltpu.make_async_copy(out_ref.at[i], out_all.at[:, :, part, :], out_sem.at[i])
+
+    for i in range(2):
+        for c in range(3):
+            fetch(i, c).start()
+    node_rows(rows_all, turned, metric_ref, rate_ref, mask_ref, mass_ref)
+
+    def one_half(i, carry):
+        half_kernel(
+            i, fetch, store, z_ref, wave_ref, sign_ref, slope_ref, ce_ref, co_ref, se_ref, so_ref, bce_ref, bco_ref,
+            bse_ref, bso_ref, out_ref.at[i], raw_ref, high, low, planes, eh, el, tail, grads, flat, rows_all,
+        )
+        return carry
+
+    lax.fori_loop(0, 2, one_half, 0)
+    for i in range(2):
+        store(i).wait()
+
+
+def half_kernel(
+    i, fetch, store, z_ref, wave_ref, sign_ref, slope_ref, ce_ref, co_ref, se_ref, so_ref, bce_ref, bco_ref,
+    bse_ref, bso_ref, out_ref, raw_ref, high, low, planes, eh, el, tail, grads, flat, rows_all,
+):
+    base = pl.multiple_of(64 * i, 64)
+    node = rows_all[i]
     rx = node[0:1, :]
     ry = node[1:2, :]
     sx = node[2:3, :]
     sy = node[3:4, :]
     damping = node[4:5, :]
     mass = node[5:6, :]
-    count = ROWS // 16
+    half = low_half((256, 128))
+
+    def trade(first, second):
+        return jnp.where(half, first, swap(second)), jnp.where(half, swap(first), second)
+
+    def cells(c, place):
+        return jnp.concatenate(
+            [z_ref[:, c, pl.ds(base + place + 8 * p, 8), :].reshape(128, 128) for p in range(2)], axis=0
+        )
+
+    def slopes(c, part, q, up, down):
+        cols = slice(128 * q, 128 * q + 128)
+        both = dot(jnp.concatenate([up, down, up], axis=1), slope_ref[...])
+        grads[c, part, 0, :, cols] = both[:, :128]
+        grads[c, part, 1, :, cols] = both[:, 128:]
 
     for c in range(3):
-        for part in range(2):
-            up, down = split(z_ref[:, c, part].reshape(256, 256))
-            high[c, part] = up
-            low[c, part] = down
+        fetch(i, c).wait()
+        for q in range(2):
+            cols = slice(128 * q, 128 * q + 128)
+            for part, value in enumerate(trade(cells(c, 32 * q), cells(c, 32 * q + 16))):
+                if c < 2:
+                    flat[c, part, :, cols] = value
+                up, down = split(value)
+                high[c, part, :, cols] = up
+                low[c, part, :, cols] = down
+    for c in range(3):
+        for part in range(2):
             for q in range(2):
                 cols = slice(128 * q, 128 * q + 128)
-                three = jnp.concatenate([up[:, cols], down[:, cols], up[:, cols]], axis=1)
-                both = dot(three, slope_ref[...])
-                grads[c, part, 0, :, cols] = both[:, :128]
-                grads[c, part, 1, :, cols] = both[:, 128:]
-
-    def curls(step, carry):
-        rows = pl.ds(pl.multiple_of(step * ROWS, ROWS), ROWS)
-        wave = jnp.concatenate([wave_ref[rows, :]] * 2, axis=1)
+                slopes(c, part, q, high[c, part, :, cols], low[c, part, :, cols])
+
+    for step in range(256 // ROWS):
+        rows = slice(step * ROWS, step * ROWS + ROWS)
+        wave = twice(wave_ref[rows, :])
         for part in range(2):
             u_r, u_s = grads[0, part, 0, rows, :], grads[0, part, 1, rows, :]
             v_r, v_s = grads[1, part, 0, rows, :], grads[1, part, 1, rows, :]
             w_r, w_s = grads[2, part, 0, rows, :], grads[2, part, 1, rows, :]
-            u_t = z_ref[pl.ds(step * count, count), 0, 1 - part].reshape(ROWS, 256)
-            v_t = z_ref[pl.ds(step * count, count), 1, 1 - part].reshape(ROWS, 256)
+            u_t = flat[0, 1 - part, rows, :]
+            v_t = flat[1, 1 - part, rows, :]
             turn = -wave if part == 0 else wave
             swirl = (
                 ry * w_r + sy * w_s - turn * v_t,
@@ -185,19 +258,22 @@
                 up, down = split(swirl[c])
                 high[3 + c, part, rows, :] = up
                 low[3 + c, part, rows, :] = down
-        return carry
-
-    lax.fori_loop(0, 256 // ROWS, curls, 0, unroll=True)
-
-    def synth(c, carry):
-        even = dot(cos_ref[...], jnp.concatenate([high[c, 0], low[c, 0], high[c, 0]], axis=0))
-        odd = dot(sin_ref[...], jnp.concatenate([high[c, 1], low[c, 1], high[c, 1]], axis=0))
-        planes[c, 0] = even[:256] - odd
-        planes[c, 1] = even[:256] + odd
-        planes[c, 1, 0:1, :] = even[256:257, :]
-        return carry
-
-    lax.fori_loop(0, 6, synth, 0, unroll=True)
+
+    for c in range(6):
+        ce = dot(ce_ref[...], stacked(high[c, 0, :128], low[c, 0, :128]))
+        co = dot(co_ref[...], stacked(high[c, 0, 128:], low[c, 0, 128:]))
+        se = dot(se_ref[...], stacked(high[c, 1, :128], low[c, 1, :128]))
+        so = dot(so_ref[...], stacked(high[c, 1, 128:], low[c, 1, 128:]))
+        top, bottom = ce[:128] + co, ce[:128] - co
+        add, sub = se + so, se - so
+        planes[c, 0] = top - add
+        planes[c, 1] = top + add
+        planes[c, 2] = bottom + sub
+        planes[c, 3] = bottom - sub
+        planes[c, 0, 0:1, :] = ce[0:1] + co[0:1]
+        planes[c, 1, 0:1, :] = ce[128:129] - so[0:1]
+        planes[c, 2, 0:1, :] = ce[0:1] - co[0:1]
+        planes[c, 3, 0:1, :] = ce[128:129] + so[0:1]
 
     def force(u, w):
         return (
@@ -206,101 +282,103 @@
             u[0] * w[1] - u[1] * w[0] - damping * u[2],
         )
 
-    def forces(step, carry):
-        rows = pl.ds(pl.multiple_of(step * ROWS, ROWS), ROWS)
-        front = [planes[c, 0, rows, :] for c in range(6)]
-        back = [planes[c, 1, rows, :] for c in range(6)]
-        front = force(front[:3], front[3:])
-        back = force(back[:3], back[3:])
-        place = lax.broadcasted_iota(jnp.int32, (ROWS, 256), 0) + step * ROWS
+    first_row = lax.broadcasted_iota(jnp.int32, (ROWS, 256), 0) == 0
+    for step in range(128 // ROWS):
+        rows = slice(step * ROWS, step * ROWS + ROWS)
+        quads = []
+        for quad in range(4):
+            here = [planes[c, quad, rows, :] for c in range(6)]
+            quads.append(force(here[:3], here[3:]))
         for c in range(3):
-            kept = jnp.where(place == 0, 0.0, back[c])
-            up, down = split(front[c] + kept)
-            eh[c, 0, rows, :] = up
-            el[c, 0, rows, :] = down
-            up, down = split(front[c] - kept)
-            eh[c, 1, rows, :] = up
-            el[c, 1, rows, :] = down
-
-        @pl.when(step == 0)
-        def _():
-            for c in range(3):
-                tail[c, 0:8, :] = back[c][0:8, :]
-
-        return carry
-
-    lax.fori_loop(0, 256 // ROWS, forces, 0, unroll=True)
-
-    def analyse(c, carry):
-        re = dot(back_cos_ref[...], jnp.concatenate([eh[c, 0], el[c, 0], eh[c, 0]], axis=0))
-        im = dot(back_sin_ref[...], jnp.concatenate([eh[c, 1], el[c, 1], eh[c, 1]], axis=0))
-        sign = jnp.concatenate([sign_ref[...]] * 2, axis=1)
-        re = re + sign * tail[c, 0:1, :]
-        out_ref[:, c, 0] = re.reshape(16, 16, 256)
-        out_ref[:, c, 1] = im.reshape(16, 16, 256)
-        return carry
-
-    lax.fori_loop(0, 3, analyse, 0, unroll=True)
-
+            one, two, three, four = [quad[c] for quad in quads]
+            plus, minus = one + two, one - two
+            more, less = three + four, three - four
+            sums = [plus + more, plus - more, minus - less, minus + less]
+            if step == 0:
+                sums[0] = jnp.where(first_row, one + three, sums[0])
+                sums[1] = jnp.where(first_row, one - three, sums[1])
+                sums[3] = jnp.where(first_row, two - four, sums[3])
+                tail[c, 0:8, :] = (two + four)[0:8, :]
+            for quad in range(4):
+                up, down = split(sums[quad])
+                eh[c, quad, rows, :] = up
+                el[c, quad, rows, :] = down
+
+    backs = (bce_ref, bco_ref, bse_ref, bso_ref)
+    for c in range(3):
+        for quad in range(4):
+            value = dot(backs[quad][...], stacked(eh[c, quad], el[c, quad]))
+            if quad == 0:
+                value = value + twice(sign_ref[...]) * tail[c, 0:1, :]
+            flat[c, quad // 2, 128 * (quad % 2) : 128 * (quad % 2) + 128, :] = value
+    def put(ref, place, value):
+        for p in range(2):
+            ref[:, pl.ds(place + 8 * p, 8), :] = value[128 * p : 128 * p + 128].reshape(16, 8, 128)
+
+    for c in range(3):
+        for q in range(2):
+            cols = slice(128 * q, 128 * q + 128)
+            first, second = trade(flat[c, 0, :, cols], flat[c, 1, :, cols])
+            put(out_ref.at[:, c], 32 * q, first)
+            put(out_ref.at[:, c], 32 * q + 16, second)
+    store(i).start()
     for c in range(2):
         for part in range(2):
-            up, down = split(out_ref[:, c, part].reshape(256, 256))
             for q in range(2):
-                cols = slice(128 * q, 128 * q + 128)
-                three = jnp.concatenate([up[:, cols], down[:, cols], up[:, cols]], axis=1)
-                both = dot(three, slope_ref[...])
-                grads[c, part, 0, :, cols] = both[:, :128]
-                grads[c, part, 1, :, cols] = both[:, 128:]
+                slopes(c, part, q, *split(flat[c, part, :, 128 * q : 128 * q + 128]))
+
     x_r, x_s, y_r, y_s = -mass * rx, -mass * sx, -mass * ry, -mass * sy
-    for step in range(256 // ROWS):
-        rows = slice(step * ROWS, step * ROWS + ROWS)
-        wave = jnp.concatenate([wave_ref[rows, :]] * 2, axis=1)
-        for part in range(2):
-            other = out_ref[count * step : count * step + count, 2, 1 - part].reshape(ROWS, 256)
-            turn = wave if part == 0 else -wave
-            value = (
-                x_r * grads[0, part, 0, rows, :]
-                + x_s * grads[0, part, 1, rows, :]
-                + y_r * grads[1, part, 0, rows, :]
-                + y_s * grads[1, part, 1, rows, :]
-                + mass * (turn * other)
+    for q in range(2):
+        cols = slice(128 * q, 128 * q + 128)
+        values = []
+        for part in range(2):
+            turn = wave_ref[...] if part == 0 else -wave_ref[...]
+            values.append(
+                x_r[:, cols] * grads[0, part, 0, :, cols]
+                + x_s[:, cols] * grads[0, part, 1, :, cols]
+                + y_r[:, cols] * grads[1, part, 0, :, cols]
+                + y_s[:, cols] * grads[1, part, 1, :, cols]
+                + mass[:, cols] * (turn * flat[2, 1 - part, :, cols])
             )
-            raw_ref[count * step : count * step + count, part] = value.reshape(count, 16, 256)
+        first, second = trade(*values)
+        put(raw_ref, base + 32 * q, first)
+        put(raw_ref, base + 32 * q + 16, second)
 
 
 def in_planes(blocks, metric, rate, mask, mass):
-    synth_cos, synth_sin, back_cos, back_sin, wave, sign = tables(256)
+    there, back, wave, sign = tables(256)
     consts = [wave, sign, right_tables()]
-    for table in (synth_cos, synth_sin, back_cos, back_sin):
+    for table in there + back:
         high, low = two_parts(table)
         consts.append(np.concatenate([high, high, low], axis=1))
     consts = [jnp.asarray(c) for c in consts]
 
-    def whole(array):
-        return pl.BlockSpec(array.shape, lambda i: (0,) * array.ndim)
-
-    block = pl.BlockSpec((16, 3, 2, 16, 256), lambda i: (0, 0, 0, 0, i))
+    in_vmem = pl.BlockSpec(memory_space=pltpu.VMEM)
     return pl.pallas_call(
         plane_kernel,
-        grid=(2,),
-        in_specs=[block] + [whole(c) for c in [metric, rate, mask, mass] + consts],
-        out_specs=[block, pl.BlockSpec((16, 2, 16, 256), lambda i: (0, 0, 0, i))],
+        in_specs=[pl.BlockSpec(memory_space=pl.ANY)] + [in_vmem] * (4 + len(consts)),
+        out_specs=[pl.BlockSpec(memory_space=pl.ANY), in_vmem],
         out_shape=[
-            jax.ShapeDtypeStruct((16, 3, 2, 16, 512), F32),
-            jax.ShapeDtypeStruct((16, 2, 16, 512), F32),
+            jax.ShapeDtypeStruct(BLOCKS, F32),
+            jax.ShapeDtypeStruct((16, 128, 128), F32),
         ],
         scratch_shapes=[
+            pltpu.VMEM(BLOCKS, F32),
+            pltpu.VMEM((2, 16, 3, 64, 128), F32),
             pltpu.VMEM((6, 2, 256, 256), BF16),
             pltpu.VMEM((6, 2, 256, 256), BF16),
-            pltpu.VMEM((6, 2, 256, 256), F32),
-            pltpu.VMEM((3, 2, 256, 256), BF16),
-            pltpu.VMEM((3, 2, 256, 256), BF16),
+            pltpu.VMEM((6, 4, 128, 256), F32),
+            pltpu.VMEM((3, 4, 128, 256), BF16),
+            pltpu.VMEM((3, 4, 128, 256), BF16),
             pltpu.VMEM((3, 8, 256), F32),
             pltpu.VMEM((3, 2, 2, 256, 256), F32),
+            pltpu.VMEM((3, 2, 256, 256), F32),
             pltpu.VMEM((2, 8, 256), F32),
             pltpu.VMEM((6, 128, 128), F32),
+            pltpu.SemaphoreType.DMA((2, 3)),
+            pltpu.SemaphoreType.DMA((2,)),
         ],
-        compiler_params=pltpu.CompilerParams(vmem_limit_bytes=WIDE),
+        compiler_params=pltpu.CompilerParams(vmem_limit_bytes=50 * MIB),
         name="in_planes",
     )(blocks, metric, rate, mask, mass, *consts)
 
@@ -327,22 +405,10 @@
     return (lax.axis_index("mode") * 16 + kl).astype(F32) * (np.pi / 256)
 
 
-def turn_back(r_ref, tmp, count):
-    half = low_half((count, 128))
-    for pair in range(64):
-        g, i = divmod(pair, 4)
-        cols = slice(128 * i, 128 * i + 128)
-        re = r_ref[g, 0, :, cols]
-        im = r_ref[g, 1, :, cols]
-        place = 2 * count * pair
-        tmp[place : place + count, :] = jnp.where(half, re, swap(im))
-        tmp[place + count : place + 2 * count, :] = jnp.where(half, swap(re), im)
-
-
-def right_kernel(r_ref, raw_ref, edge_ref, tmp):
-    turn_back(r_ref, tmp, 16)
+def right_kernel(r_ref, raw_ref, edge_ref):
     for kl in range(16):
-        raw_ref[:, kl] = tmp[pl.ds(kl, 128, stride=16), :].T.reshape(2, 64, 128)
+        block = jnp.concatenate([r_ref[g, pl.ds(spot(kl), 8, stride=16), :] for g in range(16)], axis=0)
+        raw_ref[:, kl] = block.T.reshape(2, 64, 128)
         for part in range(2):
             edge_ref[0, part, kl] = raw_ref[part, kl, pl.ds(0, 8, stride=8), :]
             edge_ref[1, part, kl] = raw_ref[part, kl, pl.ds(7, 8, stride=8), :]
@@ -352,27 +418,34 @@
     return pl.pallas_call(
         right_kernel,
         out_shape=[jax.ShapeDtypeStruct(FIELD, F32), jax.ShapeDtypeStruct(EDGE, F32)],
-        scratch_shapes=[pltpu.VMEM((2048, 128), F32)],
         compiler_params=pltpu.CompilerParams(vmem_limit_bytes=NARROW),
         cost_estimate=SMALL,
         name="right_side",
     )(blocks)
 
 
-def post_kernel(r_ref, non_ref, tmp):
-    turn_back(r_ref.at[:, 0], tmp, 16)
-    for kl in range(16):
-        non_ref[0, :, kl] = tmp[pl.ds(kl, 128, stride=16), :].T.reshape(2, 64, 128)
+def post_kernel(r_ref, non_all, non_ref, sems):
+    def store(c, h):
+        part = pl.ds(8 * h, 8)
+        return pltpu.make_async_copy(non_ref.at[c, :, part], non_all.at[c, :, part], sems.at[c, h])
+
+    pieces = [(c, h) for c in range(3) for h in range(2)]
+    for c, h in pieces:
+        for kl in range(8 * h, 8 * h + 8):
+            block = jnp.concatenate([r_ref[g, c, pl.ds(spot(kl), 8, stride=16), :] for g in range(16)], axis=0)
+            non_ref[c, :, kl] = block.T.reshape(2, 64, 128)
+        store(c, h).start()
+    for piece in pieces:
+        store(*piece).wait()
 
 
 def from_blocks(blocks):
     return pl.pallas_call(
         post_kernel,
-        grid=(3,),
-        in_specs=[pl.BlockSpec((16, 1, 2, 16, 512), lambda c: (0, c, 0, 0, 0))],
-        out_specs=pl.BlockSpec((1, 2, 16, 64, 128), lambda c: (c, 0, 0, 0, 0)),
+        in_specs=[pl.BlockSpec(memory_space=pltpu.VMEM)],
+        out_specs=pl.BlockSpec(memory_space=pl.ANY),
         out_shape=jax.ShapeDtypeStruct((3, 2, 16, 64, 128), F32),
-        scratch_shapes=[pltpu.VMEM((2048, 128), F32)],
+        scratch_shapes=[pltpu.VMEM((3, 2, 16, 64, 128), F32), pltpu.SemaphoreType.DMA((3, 2))],
         compiler_params=pltpu.CompilerParams(vmem_limit_bytes=NARROW),
         name="from_blocks",
     )(blocks)

time: 132 us -> 129 us (0.977)
  Pallas kernels: 26.1 us -> 22 us
    pallas_call x3, Pallas kernels: 18.2 us -> 14.4 us  [the longest x1 9.95 us: in_planes(): pl.pallas_call(plane_kernel, in_specs=[pl.BlockSpec(memory_space=pl.ANY)]...]
where the time goes in v5:
time: 129 us; the launch traced here: 128 us
  blocking collectives  67.4 us (52%)
  Pallas kernels  22 us (17%)
  starting transfers between devices  21.8 us (17%)
  waiting for transfers between devices  14.7 us (11%)
  local copies, waits for them, and re-layouts  1.33 us (1%)
    all_to_all x2, blocking collectives, over(): return lax.all_to_all(array, axis, split_axis=0, concat_axis=0, tiled=True)  67.4 us
    pallas_call x1, Pallas kernels, in_planes(): pl.pallas_call(plane_kernel, in_specs=[pl.BlockSpec(memory_space=pl.ANY)]...  9.95 us
    ppermute x2, starting transfers between devices, swap_edges(): near = lax.ppermute(edges, 'elem', [(i, i ^ 1) for i in range(count)])  8.78 us
    ppermute x3, starting transfers between devices, gather_sums(): other = lax.ppermute(sums, 'elem', [(i, i ^ step) for i in range(count)])  7.8 us
    all_to_all x1, waiting for transfers between devices, over(): return lax.all_to_all(array, axis, split_axis=0, concat_axis=0, tiled=True)  6.83 us
    ppermute x3, waiting for transfers between devices, gather_sums(): other = lax.ppermute(sums, 'elem', [(i, i ^ step) for i in range(count)])  5.58 us
    all_to_all x1, starting transfers between devices, over(): return lax.all_to_all(array, axis, split_axis=0, concat_axis=0, tiled=True)  3.89 us
    pallas_call x1, Pallas kernels, moments_of(): pl.pallas_call(moments_kernel, in_specs=[pl.BlockSpec(memory_space=pltpu....  3.48 us
  transfers between devices with their start and end apart: 8, of which 6 were waited for; matrix products, arithmetic and copies ran while one was open for 0% of the time, Pallas kernels for 6%

profile of v5, /device:TPU:0, one launch (start us, length us, event | category | flops | bytes accessed | tf_op | source)
XLA Modules:
  0.0 128.2 jit_solution(6868986270992561170)
XLA Ops:
  0.6 2.5 %to_blocks.1 = f32[16,3,128,128]{3,2,1,0:T(8,128)S(1)} custom-call(f32[3,2,16,64,128]{4,3,2,1,0:T(8,128)} %v_all.1), custom_call_target="tpu_custom_call" | custom-call | tf_op jit(solution)/shard_map/to_blocks/pallas_call | solution.py:134
  3.2 0.0 copy-start.1
  3.2 0.0 copy-start.2
  3.2 0.0 copy-start.4
  3.2 0.0 copy-start.6
  3.2 0.0 copy-start.7
  3.2 0.0 copy-start.8
  3.2 0.0 copy-start.9
  3.3 0.0 copy-start.10
  3.3 0.0 copy-start.11
  3.3 0.0 copy-start.12
  3.3 0.0 copy-start.13
  3.3 0.0 copy-start.14
  3.3 0.0 copy-start.15
  3.3 0.0 copy-start.17
  3.3 0.0 copy-start.19
  3.4 47.8 %all_to_all.15.z_all = f32[16,3,128,128]{3,2,1,0:T(8,128)} all-to-all(f32[16,3,128,128]{3,2,1,0:T(8,128)S(1)} %to_blocks.1), channel_id=1, replica_groups=mesh['elem'=8,'mode'=16] {'mode'}, dimensions={0} | all-to-all | bytes 6291456 | tf_op jit(solution)/shard_map/all_to_all | solution.py:678
  51.1 0.0 copy-done.1
  51.2 0.0 copy-done.2
  51.2 0.0 copy-done.4
  51.2 0.0 copy-done.6
  51.2 0.0 copy-done.7
  51.2 0.0 copy-done.8
  51.2 0.0 copy-done.9
  51.2 0.0 copy-done.10
  51.2 0.0 copy-done.11
  51.2 0.0 copy-done.12
  51.2 0.0 copy-done.13
  51.2 0.0 copy-done.14
  51.2 0.0 copy-done.15
  51.3 0.0 copy-done.17
  51.3 0.0 copy-done.19
  51.3 9.9 %in_planes.1 = (f32[16,3,128,128]{3,2,1,0:T(8,128)}, f32[16,128,128]{2,1,0:T(8,128)S(1)}) custom-call(f32[16,3,128,128]{3,2,1,0:T(8,128)} %all_to_all.15.z_all, f32[4,64,128]{2,1,0:T(8,128)S(1)} %copy-done.1, f32[64,128]{1,0:T(8,128)S(1)} %copy-done.17, s32[1,128]{1,0:T(1,128)S(1)} %bitcast.1, f32[64,128]{1,0:T(8,128)S(1)} %copy-done.2, ...), custom_call_target="tpu_custom_call" | custom-call | tf_op jit(solution)/shard_map/in_planes/pallas_call | solution.py:357
  61.2 19.6 %all_to_all.16.r_ref = f32[16,128,128]{2,1,0:T(8,128)} all-to-all(f32[16,128,128]{2,1,0:T(8,128)S(1)} %get-tuple-element.14), channel_id=1, replica_groups=mesh['elem'=8,'mode'=16] {'mode'}, dimensions={0} | all-to-all | bytes 2097152 | tf_op jit(solution)/shard_map/all_to_all | solution.py:678
  80.8 0.0 copy-start.3
  80.8 0.0 copy-start.5
  80.8 0.0 copy-start.16
  80.8 3.9 %all-to-all-start.2 = ((f32[16,3,128,128]{3,2,1,0:T(8,128)}), f32[16,3,128,128]{3,2,1,0:T(8,128)S(1)}, u32[]{:S(2)}, u32[]{:S(2)}) async-start(f32[16,3,128,128]{3,2,1,0:T(8,128)} %get-tuple-element.15), calls=%async_computation.2 | async-start | bytes 6291456 | tf_op jit(solution)/shard_map/all_to_all | solution.py:678
  84.7 0.0 copy-start
  84.7 1.2 copy-done
  85.9 0.4 right_side.1
  86.4 0.7 collective-permute-start.1
  87.0 2.9 %collective-permute-start = (f32[2,2,16,8,128]{4,3,2,1,0:T(8,128)S(1)}, f32[2,2,16,8,128]{4,3,2,1,0:T(8,128)S(1)}, u32[]{:S(2)}, u32[]{:S(2)}) collective-permute-start(f32[2,2,16,8,128]{4,3,2,1,0:T(8,128)S(1)} %get-tuple-element.18), channel_id=1, source_target_pairs={{0,16},{16,0},{32,48},{48,32},{64,80},{80,64},{96,112},{112,96},{1... | collective-permute-start | bytes 786440 | tf_op jit(solution)/shard_map/ppermute | solution.py:665
  90.0 0.0 collective-permute-done.1.far_edge
  90.0 1.2 collective-permute-done.near_edge
  91.1 0.0 copy-done.3
  91.1 0.0 copy-done.5
  91.1 0.0 copy-done.16
  91.1 0.0 copy-done.18
  91.1 2.4 %image.1 = (f32[2,16,64,128]{3,2,1,0:T(8,128)S(1)}, f32[2,16,64,128]{3,2,1,0:T(8,128)S(1)}, f32[2,2,16,8,128]{4,3,2,1,0:T(8,128)S(1)}) custom-call(f32[2,16,64,128]{3,2,1,0:T(8,128)S(1)} %get-tuple-element.17.raw_ref, f32[2,2,16,8,128]{4,3,2,1,0:T(8,128)S(1)} %collective-permute-done.near_edge, f32[2,2,16,8,128]{4,3,2,1,0:T(8,128)S(1)} %collective-permute-done.1.far_edge, ...), custom_call_target="tpu_custom_call" | custom-call | flops 1000 | bytes 1000 | tf_op jit(solution)/shard_map/image/pallas_call | solution.py:546
  93.5 0.7 collective-permute-start.3
  94.2 5.9 %collective-permute-start.2 = (f32[2,2,16,8,128]{4,3,2,1,0:T(8,128)S(1)}, f32[2,2,16,8,128]{4,3,2,1,0:T(8,128)S(1)}, u32[]{:S(2)}, u32[]{:S(2)}) collective-permute-start(f32[2,2,16,8,128]{4,3,2,1,0:T(8,128)S(1)} %get-tuple-element.21), channel_id=1, source_target_pairs={{0,16},{16,0},{32,48},{48,32},{64,80},{80,64},{96,112},{112,96},{1... | collective-permute-start | bytes 786440 | tf_op jit(solution)/shard_map/ppermute | solution.py:665
  100.1 0.0 collective-permute-done.3.far_edge
  100.1 1.2 collective-permute-done.2.near_edge
  101.2 3.5 %moments.1 = (f32[2,16,64,128]{3,2,1,0:T(8,128)S(1)}, f32[1,16,128]{2,1,0:T(8,128)S(1)}) custom-call(f32[2,16,64,128]{3,2,1,0:T(8,128)S(1)} %get-tuple-element.20.image_ref, f32[2,2,16,8,128]{4,3,2,1,0:T(8,128)S(1)} %collective-permute-done.2.near_edge, f32[2,2,16,8,128]{4,3,2,1,0:T(8,128)S(1)} %collective-permute-done.3.far_edge, ...), custom_call_target="tpu_custom_call" | custom-call | flops 1000 | bytes 1000 | tf_op jit(solution)/shard_map/moments/pallas_call | solution.py:608
  104.7 3.4 %collective-permute-start.4 = (f32[1,16,128]{2,1,0:T(8,128)S(1)}, f32[1,16,128]{2,1,0:T(8,128)S(1)}, u32[]{:S(2)}, u32[]{:S(2)}) collective-permute-start(f32[1,16,128]{2,1,0:T(8,128)S(1)} %get-tuple-element.23), channel_id=1, source_target_pairs={{0,16},{16,0},{32,48},{48,32},{64,80},{80,64},{96,112},{112,96},{1... | collective-permute-start | bytes 24584 | tf_op jit(solution)/shard_map/ppermute | solution.py:672
  108.1 0.8 collective-permute-done.4
  109.0 1.5 %collective-permute-start.5 = (f32[2,16,128]{2,1,0:T(8,128)S(1)}, f32[2,16,128]{2,1,0:T(8,128)S(1)}, u32[]{:S(2)}, u32[]{:S(2)}) collective-permute-start(f32[2,16,128]{2,1,0:T(8,128)S(1)} %pad_maximum_fusion.2), channel_id=1, source_target_pairs={{0,32},{16,48},{32,0},{48,16},{64,96},{80,112},{96,64},{112,80},{1... | collective-permute-start | bytes 49160 | tf_op jit(solution)/shard_map/ppermute | solution.py:672
  110.4 2.2 %collective-permute-done.5 = f32[2,16,128]{2,1,0:T(8,128)S(1)} collective-permute-done((f32[2,16,128]{2,1,0:T(8,128)S(1)}, f32[2,16,128]{2,1,0:T(8,128)S(1)}, u32[]{:S(2)}, u32[]{:S(2)}) %collective-permute-start.5) | collective-permute-done | bytes 16416 | tf_op jit(solution)/shard_map/ppermute | solution.py:672
  112.7 2.9 %collective-permute-start.6 = (f32[4,16,128]{2,1,0:T(8,128)S(1)}, f32[4,16,128]{2,1,0:T(8,128)S(1)}, u32[]{:S(2)}, u32[]{:S(2)}) collective-permute-start(f32[4,16,128]{2,1,0:T(8,128)S(1)} %pad_maximum_fusion.1), channel_id=1, source_target_pairs={{0,64},{16,80},{32,96},{48,112},{64,0},{80,16},{96,32},{112,48},{1... | collective-permute-start | bytes 98312 | tf_op jit(solution)/shard_map/ppermute | solution.py:672
  115.6 2.5 %collective-permute-done.6 = f32[4,16,128]{2,1,0:T(8,128)S(1)} collective-permute-done((f32[4,16,128]{2,1,0:T(8,128)S(1)}, f32[4,16,128]{2,1,0:T(8,128)S(1)}, u32[]{:S(2)}, u32[]{:S(2)}) %collective-permute-start.6) | collective-permute-done | bytes 32800 | tf_op jit(solution)/shard_map/ppermute | solution.py:672
  118.1 1.3 %pressure.1 = f32[2,16,64,128]{3,2,1,0:T(8,128)} custom-call(f32[2,16,64,128]{3,2,1,0:T(8,128)S(1)} %get-tuple-element.19.field_ref, f32[2,16,64,128]{3,2,1,0:T(8,128)S(1)} %get-tuple-element.22.shared_ref, f32[8,16,128]{2,1,0:T(8,128)S(1)} %pad_maximum_fusion.sum_ref), custom_call_target="tpu_custom_call" | custom-call | flops 1000 | bytes 1000 | tf_op jit(solution)/shard_map/pressure/pallas_call | solution.py:651
  119.4 6.8 %all-to-all-done.2.r_ref = f32[16,3,128,128]{3,2,1,0:T(8,128)S(1)} async-done(((f32[16,3,128,128]{3,2,1,0:T(8,128)}), f32[16,3,128,128]{3,2,1,0:T(8,128)S(1)}, u32[]{:S(2)}, u32[]{:S(2)}) %all-to-all-start.2) | async-done | bytes 3145760 | tf_op jit(solution)/shard_map/all_to_all | solution.py:678
  126.3 1.9 %from_blocks.1 = f32[3,2,16,64,128]{4,3,2,1,0:T(8,128)} custom-call(f32[16,3,128,128]{3,2,1,0:T(8,128)S(1)} %all-to-all-done.2.r_ref), custom_call_target="tpu_custom_call" | custom-call | tf_op jit(solution)/shard_map/from_blocks/pallas_call | solution.py:443
  (4 shorter events, 0.0 us)
Async XLA Ops:
  3.2 48.0 %copy-start.1 = (f32[4,64,128]{2,1,0:T(8,128)S(1)}, f32[4,64,128]{2,1,0:T(8,128)}, u32[]{:S(2)}) copy-start(f32[4,64,128]{2,1,0:T(8,128)} %metric_ref.5) | copy-start | bytes 393220
  3.2 48.0 %copy-start.2 = (f32[64,128]{1,0:T(8,128)S(1)}, f32[64,128]{1,0:T(8,128)}, u32[]{:S(2)}) copy-start(f32[64,128]{1,0:T(8,128)} %mass_ref.5) | copy-start | bytes 98308
  3.2 48.0 %copy-start.4 = (bf16[384,256]{1,0:T(8,128)(2,1)S(1)}, bf16[384,256]{1,0:T(8,128)(2,1)}, u32[]{:S(2)}) copy-start(bf16[384,256]{1,0:T(8,128)(2,1)} %constant.33.clone.slope_ref) | copy-start | bytes 589828
  3.2 48.0 %copy-start.6 = (f32[256,128]{1,0:T(8,128)S(1)}, f32[256,128]{1,0:T(8,128)}, u32[]{:S(2)}) copy-start(f32[256,128]{1,0:T(8,128)} %constant.31.clone.wave_ref) | copy-start | bytes 393220
  3.2 48.0 %copy-start.7 = (bf16[144,384]{1,0:T(8,128)(2,1)S(1)}, bf16[144,384]{1,0:T(8,128)(2,1)}, u32[]{:S(2)}) copy-start(bf16[144,384]{1,0:T(8,128)(2,1)} %constant.34.clone.ce_ref) | copy-start | bytes 331780
  3.2 47.9 %copy-start.8 = (bf16[128,384]{1,0:T(8,128)(2,1)S(1)}, bf16[128,384]{1,0:T(8,128)(2,1)}, u32[]{:S(2)}) copy-start(bf16[128,384]{1,0:T(8,128)(2,1)} %constant.41.clone.bso_ref) | copy-start | bytes 294916
  3.2 47.9 %copy-start.9 = (bf16[128,384]{1,0:T(8,128)(2,1)S(1)}, bf16[128,384]{1,0:T(8,128)(2,1)}, u32[]{:S(2)}) copy-start(bf16[128,384]{1,0:T(8,128)(2,1)} %constant.40.clone.bse_ref) | copy-start | bytes 294916
  3.3 47.9 %copy-start.10 = (bf16[128,384]{1,0:T(8,128)(2,1)S(1)}, bf16[128,384]{1,0:T(8,128)(2,1)}, u32[]{:S(2)}) copy-start(bf16[128,384]{1,0:T(8,128)(2,1)} %constant.39.clone.bco_ref) | copy-start | bytes 294916
  3.3 47.9 %copy-start.11 = (bf16[128,384]{1,0:T(8,128)(2,1)S(1)}, bf16[128,384]{1,0:T(8,128)(2,1)}, u32[]{:S(2)}) copy-start(bf16[128,384]{1,0:T(8,128)(2,1)} %constant.38.clone.bce_ref) | copy-start | bytes 294916
  3.3 47.9 %copy-start.12 = (bf16[128,384]{1,0:T(8,128)(2,1)S(1)}, bf16[128,384]{1,0:T(8,128)(2,1)}, u32[]{:S(2)}) copy-start(bf16[128,384]{1,0:T(8,128)(2,1)} %constant.37.clone.so_ref) | copy-start | bytes 294916
  3.3 47.9 %copy-start.13 = (bf16[128,384]{1,0:T(8,128)(2,1)S(1)}, bf16[128,384]{1,0:T(8,128)(2,1)}, u32[]{:S(2)}) copy-start(bf16[128,384]{1,0:T(8,128)(2,1)} %constant.36.clone.se_ref) | copy-start | bytes 294916
  3.3 47.9 %copy-start.14 = (bf16[128,384]{1,0:T(8,128)(2,1)S(1)}, bf16[128,384]{1,0:T(8,128)(2,1)}, u32[]{:S(2)}) copy-start(bf16[128,384]{1,0:T(8,128)(2,1)} %constant.35.clone.co_ref) | copy-start | bytes 294916
  3.3 47.9 %copy-start.15 = (f32[128,128]{1,0:T(8,128)S(1)}, f32[128,128]{1,0:T(8,128)}, u32[]{:S(2)}) copy-start(f32[128,128]{1,0:T(8,128)} %constant.32.clone.sign_ref) | copy-start | bytes 196612
  3.3 47.9 %copy-start.17 = (f32[64,128]{1,0:T(8,128)S(1)}, f32[64,128]{1,0:T(8,128)}, u32[]{:S(2)}) copy-start(f32[64,128]{1,0:T(8,128)} %rate_ref.1) | copy-start | bytes 98308
  3.3 47.9 %copy-start.19 = (s32[128]{0:T(128)S(1)}, s32[128]{0:T(128)}, u32[]{:S(2)}) copy-start(s32[128]{0:T(128)} %param.24) | copy-start | bytes 1540
  80.8 10.3 %copy-start.3 = (bf16[128,192]{1,0:T(8,128)(2,1)S(1)}, bf16[128,192]{1,0:T(8,128)(2,1)}, u32[]{:S(2)}) copy-start(bf16[128,192]{1,0:T(8,128)(2,1)} %constant.28.clone.fwd_ref) | copy-start | bytes 147460
  80.8 10.3 %copy-start.5 = (bf16[64,256]{1,0:T(8,128)(2,1)S(1)}, bf16[64,256]{1,0:T(8,128)(2,1)}, u32[]{:S(2)}) copy-start(bf16[64,256]{1,0:T(8,128)(2,1)} %constant.29.clone.adj_ref) | copy-start | bytes 98308
  80.8 10.3 %copy-start.16 = (bf16[64,128]{1,0:T(8,128)(2,1)S(1)}, bf16[64,128]{1,0:T(8,128)(2,1)}, u32[]{:S(2)}) copy-start(bf16[64,128]{1,0:T(8,128)(2,1)} %constant.30.clone.adl_ref) | copy-start | bytes 49156
  80.8 10.3 %copy-start.18 = (s32[4,128]{1,0:T(4,128)S(1)}, s32[4,128]{1,0:T(4,128)}, u32[]{:S(2)}) copy-start(s32[4,128]{1,0:T(4,128)} %link_ref.3) | copy-start | bytes 6148
  80.8 45.4 %all-to-all-start.2 = ((f32[16,3,128,128]{3,2,1,0:T(8,128)}), f32[16,3,128,128]{3,2,1,0:T(8,128)S(1)}, u32[]{:S(2)}, u32[]{:S(2)}) async-start(f32[16,3,128,128]{3,2,1,0:T(8,128)} %get-tuple-element.15), calls=%async_computation.2 | async-start | bytes 6291456 | tf_op jit(solution)/shard_map/all_to_all | solution.py:678
  84.7 1.2 copy-start
  86.4 3.6 %collective-permute-start.1 = (f32[2,2,16,8,128]{4,3,2,1,0:T(8,128)S(1)}, f32[2,2,16,8,128]{4,3,2,1,0:T(8,128)S(1)}, u32[]{:S(2)}, u32[]{:S(2)}) collective-permute-start(f32[2,2,16,8,128]{4,3,2,1,0:T(8,128)S(1)} %get-tuple-element.18), channel_id=1, source_target_pairs={{16,32},{32,16},{48,64},{64,48},{80,96},{96,80},{17,33},{33,17},{4... | collective-permute-start | bytes 786440 | tf_op jit(solution)/shard_map/ppermute | solution.py:664
  87.0 4.1 %collective-permute-start = (f32[2,2,16,8,128]{4,3,2,1,0:T(8,128)S(1)}, f32[2,2,16,8,128]{4,3,2,1,0:T(8,128)S(1)}, u32[]{:S(2)}, u32[]{:S(2)}) collective-permute-start(f32[2,2,16,8,128]{4,3,2,1,0:T(8,128)S(1)} %get-tuple-element.18), channel_id=1, source_target_pairs={{0,16},{16,0},{32,48},{48,32},{64,80},{80,64},{96,112},{112,96},{1... | collective-permute-start | bytes 786440 | tf_op jit(solution)/shard_map/ppermute | solution.py:665
  93.5 6.6 %collective-permute-start.3 = (f32[2,2,16,8,128]{4,3,2,1,0:T(8,128)S(1)}, f32[2,2,16,8,128]{4,3,2,1,0:T(8,128)S(1)}, u32[]{:S(2)}, u32[]{:S(2)}) collective-permute-start(f32[2,2,16,8,128]{4,3,2,1,0:T(8,128)S(1)} %get-tuple-element.21), channel_id=1, source_target_pairs={{16,32},{32,16},{48,64},{64,48},{80,96},{96,80},{17,33},{33,17},{4... | collective-permute-start | bytes 786440 | tf_op jit(solution)/shard_map/ppermute | solution.py:664
  94.2 7.0 %collective-permute-start.2 = (f32[2,2,16,8,128]{4,3,2,1,0:T(8,128)S(1)}, f32[2,2,16,8,128]{4,3,2,1,0:T(8,128)S(1)}, u32[]{:S(2)}, u32[]{:S(2)}) collective-permute-start(f32[2,2,16,8,128]{4,3,2,1,0:T(8,128)S(1)} %get-tuple-element.21), channel_id=1, source_target_pairs={{0,16},{16,0},{32,48},{48,32},{64,80},{80,64},{96,112},{112,96},{1... | collective-permute-start | bytes 786440 | tf_op jit(solution)/shard_map/ppermute | solution.py:665
  104.7 4.2 %collective-permute-start.4 = (f32[1,16,128]{2,1,0:T(8,128)S(1)}, f32[1,16,128]{2,1,0:T(8,128)S(1)}, u32[]{:S(2)}, u32[]{:S(2)}) collective-permute-start(f32[1,16,128]{2,1,0:T(8,128)S(1)} %get-tuple-element.23), channel_id=1, source_target_pairs={{0,16},{16,0},{32,48},{48,32},{64,80},{80,64},{96,112},{112,96},{1... | collective-permute-start | bytes 24584 | tf_op jit(solution)/shard_map/ppermute | solution.py:672
  109.0 3.7 %collective-permute-start.5 = (f32[2,16,128]{2,1,0:T(8,128)S(1)}, f32[2,16,128]{2,1,0:T(8,128)S(1)}, u32[]{:S(2)}, u32[]{:S(2)}) collective-permute-start(f32[2,16,128]{2,1,0:T(8,128)S(1)} %pad_maximum_fusion.2), channel_id=1, source_target_pairs={{0,32},{16,48},{32,0},{48,16},{64,96},{80,112},{96,64},{112,80},{1... | collective-permute-start | bytes 49160 | tf_op jit(solution)/shard_map/ppermute | solution.py:672
  112.7 5.4 %collective-permute-start.6 = (f32[4,16,128]{2,1,0:T(8,128)S(1)}, f32[4,16,128]{2,1,0:T(8,128)S(1)}, u32[]{:S(2)}, u32[]{:S(2)}) collective-permute-start(f32[4,16,128]{2,1,0:T(8,128)S(1)} %pad_maximum_fusion.1), channel_id=1, source_target_pairs={{0,64},{16,80},{32,96},{48,112},{64,0},{80,16},{96,32},{112,48},{1... | collective-permute-start | bytes 98312 | tf_op jit(solution)/shard_map/ppermute | solution.py:672

commit v6 on v5

--- a/solution.py
+++ b/solution.py
@@ -143,6 +143,7 @@
 
 
 ROWS = 32
+LAG = 26
 
 
 def node_rows(rows, tmp, metric_ref, rate_ref, mask_ref, mass_ref):
@@ -171,11 +172,11 @@
     out_sem,
 ):
     def fetch(i, c):
-        part = pl.ds(pl.multiple_of(64 * i, 64), 64)
+        part = pl.ds(64 * i, 64)
         return pltpu.make_async_copy(z_all.at[:, c, part, :], z_ref.at[:, c, part, :], z_sem.at[i, c])
 
     def store(i):
-        part = pl.ds(pl.multiple_of(64 * i, 64), 64)
+        part = pl.ds(64 * i, 64)
         return pltpu.make_async_copy(out_ref.at[i], out_all.at[:, :, part, :], out_sem.at[i])
 
     for i in range(2):
@@ -183,14 +184,19 @@
             fetch(i, c).start()
     node_rows(rows_all, turned, metric_ref, rate_ref, mask_ref, mass_ref)
 
-    def one_half(i, carry):
-        half_kernel(
+    def one_half(i):
+        return half_kernel(
             i, fetch, store, z_ref, wave_ref, sign_ref, slope_ref, ce_ref, co_ref, se_ref, so_ref, bce_ref, bco_ref,
-            bse_ref, bso_ref, out_ref.at[i], raw_ref, high, low, planes, eh, el, tail, grads, flat, rows_all,
+            bse_ref, bso_ref, out_ref.at[i], raw_ref, high.at[i], low.at[i], planes.at[i], eh.at[i], el.at[i], tail.at[i],
+            grads.at[i], flat.at[i], rows_all,
         )
-        return carry
-
-    lax.fori_loop(0, 2, one_half, 0)
+
+    ahead, behind = one_half(0), one_half(1)
+    for _ in range(LAG):
+        next(ahead, None)
+    running = [ahead, behind]
+    while running:
+        running = [half for half in running if next(half, "end") != "end"]
     for i in range(2):
         store(i).wait()
 
@@ -199,7 +205,7 @@
     i, fetch, store, z_ref, wave_ref, sign_ref, slope_ref, ce_ref, co_ref, se_ref, so_ref, bce_ref, bco_ref,
     bse_ref, bso_ref, out_ref, raw_ref, high, low, planes, eh, el, tail, grads, flat, rows_all,
 ):
-    base = pl.multiple_of(64 * i, 64)
+    base = 64 * i
     node = rows_all[i]
     rx = node[0:1, :]
     ry = node[1:2, :]
@@ -233,11 +239,13 @@
                 up, down = split(value)
                 high[c, part, :, cols] = up
                 low[c, part, :, cols] = down
+            yield
     for c in range(3):
         for part in range(2):
             for q in range(2):
                 cols = slice(128 * q, 128 * q + 128)
                 slopes(c, part, q, high[c, part, :, cols], low[c, part, :, cols])
+                yield
 
     for step in range(256 // ROWS):
         rows = slice(step * ROWS, step * ROWS + ROWS)
@@ -258,6 +266,7 @@
                 up, down = split(swirl[c])
                 high[3 + c, part, rows, :] = up
                 low[3 + c, part, rows, :] = down
+        yield
 
     for c in range(6):
         ce = dot(ce_ref[...], stacked(high[c, 0, :128], low[c, 0, :128]))
@@ -274,6 +283,7 @@
         planes[c, 1, 0:1, :] = ce[128:129] - so[0:1]
         planes[c, 2, 0:1, :] = ce[0:1] - co[0:1]
         planes[c, 3, 0:1, :] = ce[128:129] + so[0:1]
+        yield
 
     def force(u, w):
         return (
@@ -303,6 +313,7 @@
                 up, down = split(sums[quad])
                 eh[c, quad, rows, :] = up
                 el[c, quad, rows, :] = down
+        yield
 
     backs = (bce_ref, bco_ref, bse_ref, bso_ref)
     for c in range(3):
@@ -311,6 +322,7 @@
             if quad == 0:
                 value = value + twice(sign_ref[...]) * tail[c, 0:1, :]
             flat[c, quad // 2, 128 * (quad % 2) : 128 * (quad % 2) + 128, :] = value
+            yield
     def put(ref, place, value):
         for p in range(2):
             ref[:, pl.ds(place + 8 * p, 8), :] = value[128 * p : 128 * p + 128].reshape(16, 8, 128)
@@ -321,11 +333,13 @@
             first, second = trade(flat[c, 0, :, cols], flat[c, 1, :, cols])
             put(out_ref.at[:, c], 32 * q, first)
             put(out_ref.at[:, c], 32 * q + 16, second)
+            yield
     store(i).start()
     for c in range(2):
         for part in range(2):
             for q in range(2):
                 slopes(c, part, q, *split(flat[c, part, :, 128 * q : 128 * q + 128]))
+                yield
 
     x_r, x_s, y_r, y_s = -mass * rx, -mass * sx, -mass * ry, -mass * sy
     for q in range(2):
@@ -343,6 +357,7 @@
         first, second = trade(*values)
         put(raw_ref, base + 32 * q, first)
         put(raw_ref, base + 32 * q + 16, second)
+        yield
 
 
 def in_planes(blocks, metric, rate, mask, mass):
@@ -365,14 +380,14 @@
         scratch_shapes=[
             pltpu.VMEM(BLOCKS, F32),
             pltpu.VMEM((2, 16, 3, 64, 128), F32),
-            pltpu.VMEM((6, 2, 256, 256), BF16),
-            pltpu.VMEM((6, 2, 256, 256), BF16),
-            pltpu.VMEM((6, 4, 128, 256), F32),
-            pltpu.VMEM((3, 4, 128, 256), BF16),
-            pltpu.VMEM((3, 4, 128, 256), BF16),
-            pltpu.VMEM((3, 8, 256), F32),
-            pltpu.VMEM((3, 2, 2, 256, 256), F32),
-            pltpu.VMEM((3, 2, 256, 256), F32),
+            pltpu.VMEM((2, 6, 2, 256, 256), BF16),
+            pltpu.VMEM((2, 6, 2, 256, 256), BF16),
+            pltpu.VMEM((2, 6, 4, 128, 256), F32),
+            pltpu.VMEM((2, 3, 4, 128, 256), BF16),
+            pltpu.VMEM((2, 3, 4, 128, 256), BF16),
+            pltpu.VMEM((2, 3, 8, 256), F32),
+            pltpu.VMEM((2, 3, 2, 2, 256, 256), F32),
+            pltpu.VMEM((2, 3, 2, 256, 256), F32),
             pltpu.VMEM((2, 8, 256), F32),
             pltpu.VMEM((6, 128, 128), F32),
             pltpu.SemaphoreType.DMA((2, 3)),

time: 129 us -> 128 us (level)
  no operation moved by 1% of the time
where the time goes in v6:
time: 128 us
  blocking collectives  67.4 us (53%)
  starting transfers between devices  21.8 us (17%)
  Pallas kernels  21.6 us (17%)
  waiting for transfers between devices  14.7 us (11%)
  local copies, waits for them, and re-layouts  1.33 us (1%)
    all_to_all x2, blocking collectives, over(): return lax.all_to_all(array, axis, split_axis=0, concat_axis=0, tiled=True)  67.4 us
    pallas_call x1, Pallas kernels, in_planes(): pl.pallas_call(plane_kernel, in_specs=[pl.BlockSpec(memory_space=pl.ANY)]...  9.56 us
    ppermute x2, starting transfers between devices, swap_edges(): near = lax.ppermute(edges, 'elem', [(i, i ^ 1) for i in range(count)])  8.78 us
    ppermute x3, starting transfers between devices, gather_sums(): other = lax.ppermute(sums, 'elem', [(i, i ^ step) for i in range(count)])  7.8 us
    all_to_all x1, waiting for transfers between devices, over(): return lax.all_to_all(array, axis, split_axis=0, concat_axis=0, tiled=True)  6.83 us
    ppermute x3, waiting for transfers between devices, gather_sums(): other = lax.ppermute(sums, 'elem', [(i, i ^ step) for i in range(count)])  5.58 us
    all_to_all x1, starting transfers between devices, over(): return lax.all_to_all(array, axis, split_axis=0, concat_axis=0, tiled=True)  3.89 us
    pallas_call x1, Pallas kernels, moments_of(): pl.pallas_call(moments_kernel, in_specs=[pl.BlockSpec(memory_space=pltpu....  3.48 us
  transfers between devices with their start and end apart: 8, of which 6 were waited for; matrix products, arithmetic and copies ran while one was open for 0% of the time, Pallas kernels for 6%

profile of v6, /device:TPU:0, one launch (start us, length us, event | category | flops | bytes accessed | tf_op | source)
XLA Modules:
  0.0 128.0 jit_solution(8975351149866655579)
XLA Ops:
  0.6 2.5 %to_blocks.1 = f32[16,3,128,128]{3,2,1,0:T(8,128)S(1)} custom-call(f32[3,2,16,64,128]{4,3,2,1,0:T(8,128)} %v_all.1), custom_call_target="tpu_custom_call" | custom-call | tf_op jit(solution)/shard_map/to_blocks/pallas_call | solution.py:134
  3.2 0.0 copy-start.1
  3.2 0.0 copy-start.2
  3.2 0.0 copy-start.4
  3.2 0.0 copy-start.6
  3.2 0.0 copy-start.7
  3.2 0.0 copy-start.8
  3.2 0.0 copy-start.9
  3.3 0.0 copy-start.10
  3.3 0.0 copy-start.11
  3.3 0.0 copy-start.12
  3.3 0.0 copy-start.13
  3.3 0.0 copy-start.14
  3.3 0.0 copy-start.15
  3.3 0.0 copy-start.17
  3.3 0.0 copy-start.19
  3.4 47.8 %all_to_all.15.z_all = f32[16,3,128,128]{3,2,1,0:T(8,128)} all-to-all(f32[16,3,128,128]{3,2,1,0:T(8,128)S(1)} %to_blocks.1), channel_id=1, replica_groups=mesh['elem'=8,'mode'=16] {'mode'}, dimensions={0} | all-to-all | bytes 6291456 | tf_op jit(solution)/shard_map/all_to_all | solution.py:693
  51.1 0.0 copy-done.1
  51.2 0.0 copy-done.2
  51.2 0.0 copy-done.4
  51.2 0.0 copy-done.6
  51.2 0.0 copy-done.7
  51.2 0.0 copy-done.8
  51.2 0.0 copy-done.9
  51.2 0.0 copy-done.10
  51.2 0.0 copy-done.11
  51.2 0.0 copy-done.12
  51.2 0.0 copy-done.13
  51.2 0.0 copy-done.14
  51.2 0.0 copy-done.15
  51.3 0.0 copy-done.17
  51.3 0.0 copy-done.19
  51.3 9.6 %in_planes.1 = (f32[16,3,128,128]{3,2,1,0:T(8,128)}, f32[16,128,128]{2,1,0:T(8,128)S(1)}) custom-call(f32[16,3,128,128]{3,2,1,0:T(8,128)} %all_to_all.15.z_all, f32[4,64,128]{2,1,0:T(8,128)S(1)} %copy-done.1, f32[64,128]{1,0:T(8,128)S(1)} %copy-done.17, s32[1,128]{1,0:T(1,128)S(1)} %bitcast.1, f32[64,128]{1,0:T(8,128)S(1)} %copy-done.2, ...), custom_call_target="tpu_custom_call" | custom-call | tf_op jit(solution)/shard_map/in_planes/pallas_call | solution.py:372
  60.9 19.6 %all_to_all.16.r_ref = f32[16,128,128]{2,1,0:T(8,128)} all-to-all(f32[16,128,128]{2,1,0:T(8,128)S(1)} %get-tuple-element.14), channel_id=1, replica_groups=mesh['elem'=8,'mode'=16] {'mode'}, dimensions={0} | all-to-all | bytes 2097152 | tf_op jit(solution)/shard_map/all_to_all | solution.py:693
  80.4 0.0 copy-start.3
  80.4 0.0 copy-start.5
  80.4 0.0 copy-start.16
  80.4 3.9 %all-to-all-start.2 = ((f32[16,3,128,128]{3,2,1,0:T(8,128)}), f32[16,3,128,128]{3,2,1,0:T(8,128)S(1)}, u32[]{:S(2)}, u32[]{:S(2)}) async-start(f32[16,3,128,128]{3,2,1,0:T(8,128)} %get-tuple-element.15), calls=%async_computation.2 | async-start | bytes 6291456 | tf_op jit(solution)/shard_map/all_to_all | solution.py:693
  84.3 0.0 copy-start
  84.3 1.2 copy-done
  85.6 0.4 right_side.1
  86.0 0.7 collective-permute-start.1
  86.7 3.1 %collective-permute-start = (f32[2,2,16,8,128]{4,3,2,1,0:T(8,128)S(1)}, f32[2,2,16,8,128]{4,3,2,1,0:T(8,128)S(1)}, u32[]{:S(2)}, u32[]{:S(2)}) collective-permute-start(f32[2,2,16,8,128]{4,3,2,1,0:T(8,128)S(1)} %get-tuple-element.18), channel_id=1, source_target_pairs={{0,16},{16,0},{32,48},{48,32},{64,80},{80,64},{96,112},{112,96},{1... | collective-permute-start | bytes 786440 | tf_op jit(solution)/shard_map/ppermute | solution.py:680
  89.8 0.0 collective-permute-done.1.far_edge
  89.8 1.2 collective-permute-done.near_edge
  90.9 0.0 copy-done.3
  90.9 0.0 copy-done.5
  90.9 0.0 copy-done.16
  90.9 0.0 copy-done.18
  90.9 2.4 %image.1 = (f32[2,16,64,128]{3,2,1,0:T(8,128)S(1)}, f32[2,16,64,128]{3,2,1,0:T(8,128)S(1)}, f32[2,2,16,8,128]{4,3,2,1,0:T(8,128)S(1)}) custom-call(f32[2,16,64,128]{3,2,1,0:T(8,128)S(1)} %get-tuple-element.17.raw_ref, f32[2,2,16,8,128]{4,3,2,1,0:T(8,128)S(1)} %collective-permute-done.near_edge, f32[2,2,16,8,128]{4,3,2,1,0:T(8,128)S(1)} %collective-permute-done.1.far_edge, ...), custom_call_target="tpu_custom_call" | custom-call | flops 1000 | bytes 1000 | tf_op jit(solution)/shard_map/image/pallas_call | solution.py:561
  93.3 0.7 collective-permute-start.3
  94.0 5.7 %collective-permute-start.2 = (f32[2,2,16,8,128]{4,3,2,1,0:T(8,128)S(1)}, f32[2,2,16,8,128]{4,3,2,1,0:T(8,128)S(1)}, u32[]{:S(2)}, u32[]{:S(2)}) collective-permute-start(f32[2,2,16,8,128]{4,3,2,1,0:T(8,128)S(1)} %get-tuple-element.21), channel_id=1, source_target_pairs={{0,16},{16,0},{32,48},{48,32},{64,80},{80,64},{96,112},{112,96},{1... | collective-permute-start | bytes 786440 | tf_op jit(solution)/shard_map/ppermute | solution.py:680
  99.7 0.0 collective-permute-done.3.far_edge
  99.7 1.2 collective-permute-done.2.near_edge
  100.9 3.5 %moments.1 = (f32[2,16,64,128]{3,2,1,0:T(8,128)S(1)}, f32[1,16,128]{2,1,0:T(8,128)S(1)}) custom-call(f32[2,16,64,128]{3,2,1,0:T(8,128)S(1)} %get-tuple-element.20.image_ref, f32[2,2,16,8,128]{4,3,2,1,0:T(8,128)S(1)} %collective-permute-done.2.near_edge, f32[2,2,16,8,128]{4,3,2,1,0:T(8,128)S(1)} %collective-permute-done.3.far_edge, ...), custom_call_target="tpu_custom_call" | custom-call | flops 1000 | bytes 1000 | tf_op jit(solution)/shard_map/moments/pallas_call | solution.py:623
  104.3 3.4 %collective-permute-start.4 = (f32[1,16,128]{2,1,0:T(8,128)S(1)}, f32[1,16,128]{2,1,0:T(8,128)S(1)}, u32[]{:S(2)}, u32[]{:S(2)}) collective-permute-start(f32[1,16,128]{2,1,0:T(8,128)S(1)} %get-tuple-element.23), channel_id=1, source_target_pairs={{0,16},{16,0},{32,48},{48,32},{64,80},{80,64},{96,112},{112,96},{1... | collective-permute-start | bytes 24584 | tf_op jit(solution)/shard_map/ppermute | solution.py:687
  107.7 0.8 collective-permute-done.4
  108.6 1.5 %collective-permute-start.5 = (f32[2,16,128]{2,1,0:T(8,128)S(1)}, f32[2,16,128]{2,1,0:T(8,128)S(1)}, u32[]{:S(2)}, u32[]{:S(2)}) collective-permute-start(f32[2,16,128]{2,1,0:T(8,128)S(1)} %pad_maximum_fusion.2), channel_id=1, source_target_pairs={{0,32},{16,48},{32,0},{48,16},{64,96},{80,112},{96,64},{112,80},{1... | collective-permute-start | bytes 49160 | tf_op jit(solution)/shard_map/ppermute | solution.py:687
  110.1 2.2 %collective-permute-done.5 = f32[2,16,128]{2,1,0:T(8,128)S(1)} collective-permute-done((f32[2,16,128]{2,1,0:T(8,128)S(1)}, f32[2,16,128]{2,1,0:T(8,128)S(1)}, u32[]{:S(2)}, u32[]{:S(2)}) %collective-permute-start.5) | collective-permute-done | bytes 16416 | tf_op jit(solution)/shard_map/ppermute | solution.py:687
  112.3 2.9 %collective-permute-start.6 = (f32[4,16,128]{2,1,0:T(8,128)S(1)}, f32[4,16,128]{2,1,0:T(8,128)S(1)}, u32[]{:S(2)}, u32[]{:S(2)}) collective-permute-start(f32[4,16,128]{2,1,0:T(8,128)S(1)} %pad_maximum_fusion.1), channel_id=1, source_target_pairs={{0,64},{16,80},{32,96},{48,112},{64,0},{80,16},{96,32},{112,48},{1... | collective-permute-start | bytes 98312 | tf_op jit(solution)/shard_map/ppermute | solution.py:687
  115.2 2.5 %collective-permute-done.6 = f32[4,16,128]{2,1,0:T(8,128)S(1)} collective-permute-done((f32[4,16,128]{2,1,0:T(8,128)S(1)}, f32[4,16,128]{2,1,0:T(8,128)S(1)}, u32[]{:S(2)}, u32[]{:S(2)}) %collective-permute-start.6) | collective-permute-done | bytes 32800 | tf_op jit(solution)/shard_map/ppermute | solution.py:687
  117.7 1.3 %pressure.1 = f32[2,16,64,128]{3,2,1,0:T(8,128)} custom-call(f32[2,16,64,128]{3,2,1,0:T(8,128)S(1)} %get-tuple-element.19.field_ref, f32[2,16,64,128]{3,2,1,0:T(8,128)S(1)} %get-tuple-element.22.shared_ref, f32[8,16,128]{2,1,0:T(8,128)S(1)} %pad_maximum_fusion.sum_ref), custom_call_target="tpu_custom_call" | custom-call | flops 1000 | bytes 1000 | tf_op jit(solution)/shard_map/pressure/pallas_call | solution.py:666
  119.0 6.8 %all-to-all-done.2.r_ref = f32[16,3,128,128]{3,2,1,0:T(8,128)S(1)} async-done(((f32[16,3,128,128]{3,2,1,0:T(8,128)}), f32[16,3,128,128]{3,2,1,0:T(8,128)S(1)}, u32[]{:S(2)}, u32[]{:S(2)}) %all-to-all-start.2) | async-done | bytes 3145760 | tf_op jit(solution)/shard_map/all_to_all | solution.py:693
  125.9 1.9 %from_blocks.1 = f32[3,2,16,64,128]{4,3,2,1,0:T(8,128)} custom-call(f32[16,3,128,128]{3,2,1,0:T(8,128)S(1)} %all-to-all-done.2.r_ref), custom_call_target="tpu_custom_call" | custom-call | tf_op jit(solution)/shard_map/from_blocks/pallas_call | solution.py:458
  (4 shorter events, 0.0 us)
Async XLA Ops:
  3.2 48.0 %copy-start.1 = (f32[4,64,128]{2,1,0:T(8,128)S(1)}, f32[4,64,128]{2,1,0:T(8,128)}, u32[]{:S(2)}) copy-start(f32[4,64,128]{2,1,0:T(8,128)} %metric_ref.5) | copy-start | bytes 393220
  3.2 48.0 %copy-start.2 = (f32[64,128]{1,0:T(8,128)S(1)}, f32[64,128]{1,0:T(8,128)}, u32[]{:S(2)}) copy-start(f32[64,128]{1,0:T(8,128)} %mass_ref.5) | copy-start | bytes 98308
  3.2 48.0 %copy-start.4 = (bf16[384,256]{1,0:T(8,128)(2,1)S(1)}, bf16[384,256]{1,0:T(8,128)(2,1)}, u32[]{:S(2)}) copy-start(bf16[384,256]{1,0:T(8,128)(2,1)} %constant.33.clone.slope_ref) | copy-start | bytes 589828
  3.2 48.0 %copy-start.6 = (f32[256,128]{1,0:T(8,128)S(1)}, f32[256,128]{1,0:T(8,128)}, u32[]{:S(2)}) copy-start(f32[256,128]{1,0:T(8,128)} %constant.31.clone.wave_ref) | copy-start | bytes 393220
  3.2 48.0 %copy-start.7 = (bf16[144,384]{1,0:T(8,128)(2,1)S(1)}, bf16[144,384]{1,0:T(8,128)(2,1)}, u32[]{:S(2)}) copy-start(bf16[144,384]{1,0:T(8,128)(2,1)} %constant.34.clone.ce_ref) | copy-start | bytes 331780
  3.2 47.9 %copy-start.8 = (bf16[128,384]{1,0:T(8,128)(2,1)S(1)}, bf16[128,384]{1,0:T(8,128)(2,1)}, u32[]{:S(2)}) copy-start(bf16[128,384]{1,0:T(8,128)(2,1)} %constant.41.clone.bso_ref) | copy-start | bytes 294916
  3.2 47.9 %copy-start.9 = (bf16[128,384]{1,0:T(8,128)(2,1)S(1)}, bf16[128,384]{1,0:T(8,128)(2,1)}, u32[]{:S(2)}) copy-start(bf16[128,384]{1,0:T(8,128)(2,1)} %constant.40.clone.bse_ref) | copy-start | bytes 294916
  3.3 47.9 %copy-start.10 = (bf16[128,384]{1,0:T(8,128)(2,1)S(1)}, bf16[128,384]{1,0:T(8,128)(2,1)}, u32[]{:S(2)}) copy-start(bf16[128,384]{1,0:T(8,128)(2,1)} %constant.39.clone.bco_ref) | copy-start | bytes 294916
  3.3 47.9 %copy-start.11 = (bf16[128,384]{1,0:T(8,128)(2,1)S(1)}, bf16[128,384]{1,0:T(8,128)(2,1)}, u32[]{:S(2)}) copy-start(bf16[128,384]{1,0:T(8,128)(2,1)} %constant.38.clone.bce_ref) | copy-start | bytes 294916
  3.3 47.9 %copy-start.12 = (bf16[128,384]{1,0:T(8,128)(2,1)S(1)}, bf16[128,384]{1,0:T(8,128)(2,1)}, u32[]{:S(2)}) copy-start(bf16[128,384]{1,0:T(8,128)(2,1)} %constant.37.clone.so_ref) | copy-start | bytes 294916
  3.3 47.9 %copy-start.13 = (bf16[128,384]{1,0:T(8,128)(2,1)S(1)}, bf16[128,384]{1,0:T(8,128)(2,1)}, u32[]{:S(2)}) copy-start(bf16[128,384]{1,0:T(8,128)(2,1)} %constant.36.clone.se_ref) | copy-start | bytes 294916
  3.3 47.9 %copy-start.14 = (bf16[128,384]{1,0:T(8,128)(2,1)S(1)}, bf16[128,384]{1,0:T(8,128)(2,1)}, u32[]{:S(2)}) copy-start(bf16[128,384]{1,0:T(8,128)(2,1)} %constant.35.clone.co_ref) | copy-start | bytes 294916
  3.3 47.9 %copy-start.15 = (f32[128,128]{1,0:T(8,128)S(1)}, f32[128,128]{1,0:T(8,128)}, u32[]{:S(2)}) copy-start(f32[128,128]{1,0:T(8,128)} %constant.32.clone.sign_ref) | copy-start | bytes 196612
  3.3 47.9 %copy-start.17 = (f32[64,128]{1,0:T(8,128)S(1)}, f32[64,128]{1,0:T(8,128)}, u32[]{:S(2)}) copy-start(f32[64,128]{1,0:T(8,128)} %rate_ref.1) | copy-start | bytes 98308
  3.3 47.9 %copy-start.19 = (s32[128]{0:T(128)S(1)}, s32[128]{0:T(128)}, u32[]{:S(2)}) copy-start(s32[128]{0:T(128)} %param.24) | copy-start | bytes 1540
  80.4 10.5 %copy-start.3 = (bf16[128,192]{1,0:T(8,128)(2,1)S(1)}, bf16[128,192]{1,0:T(8,128)(2,1)}, u32[]{:S(2)}) copy-start(bf16[128,192]{1,0:T(8,128)(2,1)} %constant.28.clone.fwd_ref) | copy-start | bytes 147460
  80.4 10.5 %copy-start.5 = (bf16[64,256]{1,0:T(8,128)(2,1)S(1)}, bf16[64,256]{1,0:T(8,128)(2,1)}, u32[]{:S(2)}) copy-start(bf16[64,256]{1,0:T(8,128)(2,1)} %constant.29.clone.adj_ref) | copy-start | bytes 98308
  80.4 10.5 %copy-start.16 = (bf16[64,128]{1,0:T(8,128)(2,1)S(1)}, bf16[64,128]{1,0:T(8,128)(2,1)}, u32[]{:S(2)}) copy-start(bf16[64,128]{1,0:T(8,128)(2,1)} %constant.30.clone.adl_ref) | copy-start | bytes 49156
  80.4 10.5 %copy-start.18 = (s32[4,128]{1,0:T(4,128)S(1)}, s32[4,128]{1,0:T(4,128)}, u32[]{:S(2)}) copy-start(s32[4,128]{1,0:T(4,128)} %link_ref.3) | copy-start | bytes 6148
  80.4 45.4 %all-to-all-start.2 = ((f32[16,3,128,128]{3,2,1,0:T(8,128)}), f32[16,3,128,128]{3,2,1,0:T(8,128)S(1)}, u32[]{:S(2)}, u32[]{:S(2)}) async-start(f32[16,3,128,128]{3,2,1,0:T(8,128)} %get-tuple-element.15), calls=%async_computation.2 | async-start | bytes 6291456 | tf_op jit(solution)/shard_map/all_to_all | solution.py:693
  84.3 1.2 copy-start
  86.0 3.8 %collective-permute-start.1 = (f32[2,2,16,8,128]{4,3,2,1,0:T(8,128)S(1)}, f32[2,2,16,8,128]{4,3,2,1,0:T(8,128)S(1)}, u32[]{:S(2)}, u32[]{:S(2)}) collective-permute-start(f32[2,2,16,8,128]{4,3,2,1,0:T(8,128)S(1)} %get-tuple-element.18), channel_id=1, source_target_pairs={{16,32},{32,16},{48,64},{64,48},{80,96},{96,80},{17,33},{33,17},{4... | collective-permute-start | bytes 786440 | tf_op jit(solution)/shard_map/ppermute | solution.py:679
  86.7 4.3 %collective-permute-start = (f32[2,2,16,8,128]{4,3,2,1,0:T(8,128)S(1)}, f32[2,2,16,8,128]{4,3,2,1,0:T(8,128)S(1)}, u32[]{:S(2)}, u32[]{:S(2)}) collective-permute-start(f32[2,2,16,8,128]{4,3,2,1,0:T(8,128)S(1)} %get-tuple-element.18), channel_id=1, source_target_pairs={{0,16},{16,0},{32,48},{48,32},{64,80},{80,64},{96,112},{112,96},{1... | collective-permute-start | bytes 786440 | tf_op jit(solution)/shard_map/ppermute | solution.py:680
  93.3 6.4 %collective-permute-start.3 = (f32[2,2,16,8,128]{4,3,2,1,0:T(8,128)S(1)}, f32[2,2,16,8,128]{4,3,2,1,0:T(8,128)S(1)}, u32[]{:S(2)}, u32[]{:S(2)}) collective-permute-start(f32[2,2,16,8,128]{4,3,2,1,0:T(8,128)S(1)} %get-tuple-element.21), channel_id=1, source_target_pairs={{16,32},{32,16},{48,64},{64,48},{80,96},{96,80},{17,33},{33,17},{4... | collective-permute-start | bytes 786440 | tf_op jit(solution)/shard_map/ppermute | solution.py:679
  94.0 6.8 %collective-permute-start.2 = (f32[2,2,16,8,128]{4,3,2,1,0:T(8,128)S(1)}, f32[2,2,16,8,128]{4,3,2,1,0:T(8,128)S(1)}, u32[]{:S(2)}, u32[]{:S(2)}) collective-permute-start(f32[2,2,16,8,128]{4,3,2,1,0:T(8,128)S(1)} %get-tuple-element.21), channel_id=1, source_target_pairs={{0,16},{16,0},{32,48},{48,32},{64,80},{80,64},{96,112},{112,96},{1... | collective-permute-start | bytes 786440 | tf_op jit(solution)/shard_map/ppermute | solution.py:680
  104.3 4.2 %collective-permute-start.4 = (f32[1,16,128]{2,1,0:T(8,128)S(1)}, f32[1,16,128]{2,1,0:T(8,128)S(1)}, u32[]{:S(2)}, u32[]{:S(2)}) collective-permute-start(f32[1,16,128]{2,1,0:T(8,128)S(1)} %get-tuple-element.23), channel_id=1, source_target_pairs={{0,16},{16,0},{32,48},{48,32},{64,80},{80,64},{96,112},{112,96},{1... | collective-permute-start | bytes 24584 | tf_op jit(solution)/shard_map/ppermute | solution.py:687
  108.6 3.7 %collective-permute-start.5 = (f32[2,16,128]{2,1,0:T(8,128)S(1)}, f32[2,16,128]{2,1,0:T(8,128)S(1)}, u32[]{:S(2)}, u32[]{:S(2)}) collective-permute-start(f32[2,16,128]{2,1,0:T(8,128)S(1)} %pad_maximum_fusion.2), channel_id=1, source_target_pairs={{0,32},{16,48},{32,0},{48,16},{64,96},{80,112},{96,64},{112,80},{1... | collective-permute-start | bytes 49160 | tf_op jit(solution)/shard_map/ppermute | solution.py:687
  112.3 5.4 %collective-permute-start.6 = (f32[4,16,128]{2,1,0:T(8,128)S(1)}, f32[4,16,128]{2,1,0:T(8,128)S(1)}, u32[]{:S(2)}, u32[]{:S(2)}) collective-permute-start(f32[4,16,128]{2,1,0:T(8,128)S(1)} %pad_maximum_fusion.1), channel_id=1, source_target_pairs={{0,64},{16,80},{32,96},{48,112},{64,0},{80,16},{96,32},{112,48},{1... | collective-permute-start | bytes 98312 | tf_op jit(solution)/shard_map/ppermute | solution.py:687
